TPU v7x, 512 devices: a whole 4x4x16 slice. The times are simulated.
512 devices in a mesh: pipe: 32 (over z, core), tp: 16 (over x, y).
Axes of the slice: x: 4, y: 4, z: 16, core: 2. Of those that a mesh axis runs over, the one named last changes fastest.
Arguments:
- saved: bfloat16 [32, 2, 128, 4096], P('pipe', None, None, 'tp'), may hold values from -26 to 26
- incoming: bfloat16 [32, 128, 4096], P('pipe', None, 'tp'), may hold values from -6 to 6
- gain: bfloat16 [32, 4096], P('pipe'), may hold values from 0.5 to 1.5
- w_query: bfloat16 [32, 4096, 4096], P('pipe', None, 'tp'), may hold values from -0.09375 to 0.09375
- w_key: bfloat16 [32, 4096, 512], P('pipe', None, 'tp'), may hold values from -0.09375 to 0.09375
- w_value: bfloat16 [32, 4096, 512], P('pipe', None, 'tp'), may hold values from -0.09375 to 0.09375
- w_out: bfloat16 [32, 4096, 4096], P('pipe', 'tp'), may hold values from -0.09375 to 0.09375
- seg_lengths: int32 [32, 2, 4], P('pipe'), may hold values from 1 to 64, 128 in all within a row
- score_grad: bfloat16 [2, 128, 4096], P(None, None, 'tp'), may hold values from -6 to 6
- rewards: float32 [512], replicated, may hold values from -3 to 3
- sample_group: int32 [512], replicated, may hold values from 0 to 31, as said below
- head_sample: int32 [2, 128], replicated, may hold values from 0 to 511
Outputs:
- emitted: bfloat16 [32, 2, 128, 4096], P('pipe', None, None, 'tp')
- carried: bfloat16 [32, 128, 4096], P('pipe', None, 'tp')
Inputs may be any that keep to these rules, and one draw needn't show every extreme that they name: `sample_group`: each of the 32 prompt ids names exactly 16 rollouts.
All inputs are finite; a program needn't handle non-finite values.
Results may differ from a plain program's by a relative error of at most 0.027.
Values may be sent and summed in bfloat16 or wider, within the bound.
No kernel may reach another device: no remote copies, remote signals or barrier semaphores. Data moves between devices by JAX's collectives and lax.ppermute only.
A program may use at most 64 MiB of HBM per device.

v0:
```python
import math

import jax
import jax.numpy as jnp
from jax import lax
from jax.sharding import PartitionSpec as P

D = 4096
KV = 4
HD = 128
ROWS = 128
TICKS = 2
GROUP_SIZE = 16
GROUPS = 32


EPS = 1e-05
THETA = 500000.0


def from_partner(block, axis, distance):
    count = lax.axis_size(axis)
    route = []
    for low in range(count):
        high = low | 1 << distance
        if high != low and high < count:
            route += [(low, high), (high, low)]
    return lax.ppermute(block, axis, route)


def shifted(value, axis, steps):
    count = lax.axis_size(axis)
    first, last = (max(0, -steps), min(count, count - steps))
    return lax.ppermute(value, axis, [(source, source + steps) for source in range(first, last)])


def rotate_pairs(values, positions, offset, direction):
    total_width = values.shape[1]
    column = (offset + jnp.arange(total_width, dtype=jnp.int32)) % HD
    pair_index = (column // 2).astype(jnp.float32)
    frequency = jnp.exp(pair_index * (-2.0 * math.log(THETA) / HD))
    angles = positions.astype(jnp.float32)[:, None] * frequency[None, :]
    parity = jnp.where(column % 2 == 0, -1.0, 1.0).astype(jnp.float32) * direction
    partner = values.reshape(values.shape[0], total_width // 2, 2)[:, :, ::-1].reshape(
        values.shape[0], total_width
    )
    return values * jnp.cos(angles) + partner * parity * jnp.sin(angles)


def row_layout(lengths):
    row_ids = jnp.arange(ROWS, dtype=jnp.int32)
    seg_ends = jnp.cumsum(lengths)
    segment = jnp.sum((row_ids[:, None] >= seg_ends[None, :]).astype(jnp.int32), axis=1)
    member = segment[:, None] == jnp.arange(lengths.shape[0], dtype=jnp.int32)[None, :]
    begins = jnp.sum(jnp.where(member, (seg_ends - lengths)[None, :], 0), axis=1)
    positions = row_ids - begins
    allowed = (segment[:, None] == segment[None, :]) & (row_ids[None, :] <= row_ids[:, None])
    return (positions, allowed)


def advantages(rewards, sample_group):
    member = (sample_group[:, None] == jnp.arange(GROUPS, dtype=jnp.int32)[None, :]).astype(
        jnp.float32
    )
    totals = jnp.sum(member * rewards[:, None], axis=0)
    own_total = jnp.sum(member * totals[None, :], axis=1)
    return rewards - (own_total - rewards) / (GROUP_SIZE - 1)


def head_gradient(advantage, head_sample, score_grad):
    chosen = (
        head_sample[:, :, None] == jnp.arange(advantage.shape[0], dtype=jnp.int32)[None, None, :]
    )
    row_adv = jnp.sum(jnp.where(chosen, advantage[None, None, :], 0.0), axis=2)
    return (-row_adv[:, :, None] * score_grad.astype(jnp.float32)).astype(jnp.bfloat16)


def per_device(
    saved,
    incoming,
    gain,
    w_query,
    w_key,
    w_value,
    w_out,
    seg_lengths,
    score_grad,
    rewards,
    sample_group,
    head_sample,
):
    tp_index = lax.axis_index("tp")
    tp_count = lax.axis_size("tp")
    last_section = lax.axis_index("pipe") == lax.axis_size("pipe") - 1
    query_weight = w_query[0]
    key_weight = w_key[0]
    value_weight = w_value[0]
    out_weight = w_out[0]
    gain_full = gain[0].astype(jnp.float32)[None, :]
    feature_share = saved.shape[3]
    query_share = query_weight.shape[1]
    kv_share = key_weight.shape[1]
    heads_here = query_share // HD
    query_start = tp_index * query_share
    kv_start = tp_index * kv_share
    feature_start = tp_index * feature_share
    group_bits = (tp_count // KV).bit_length() - 1
    score_scale = 1.0 / math.sqrt(HD)
    advantage = advantages(rewards, sample_group)
    outputs = []
    saved_full, score_full, grad_full = (
        lax.all_gather(saved[0], "tp", axis=2, tiled=True),
        lax.all_gather(score_grad, "tp", axis=2, tiled=True),
        lax.all_gather(incoming, "tp", axis=2, tiled=True),
    )
    grad_full = grad_full[0]
    head_rows = head_gradient(advantage, head_sample, score_full)
    for tick_index in range(TICKS):
        recompute_rows32 = saved_full[tick_index].astype(jnp.float32)
        recompute_inverse = lax.rsqrt(
            jnp.mean(recompute_rows32 * recompute_rows32, axis=1, keepdims=True) + EPS
        )
        normed = (recompute_rows32 * recompute_inverse * gain_full).astype(jnp.bfloat16)
        recompute_positions, recompute_allowed = row_layout(seg_lengths[0, tick_index])
        recompute_query_rows = rotate_pairs(
            jnp.dot(normed, query_weight, preferred_element_type=jnp.float32),
            recompute_positions,
            query_start,
            1.0,
        ).astype(jnp.bfloat16)
        recompute_key_part = rotate_pairs(
            jnp.dot(normed, key_weight, preferred_element_type=jnp.float32),
            recompute_positions,
            kv_start,
            1.0,
        ).astype(jnp.bfloat16)
        recompute_value_part = jnp.dot(
            normed, value_weight, preferred_element_type=jnp.float32
        ).astype(jnp.bfloat16)
        share_key_rows = recompute_key_part
        share_value_rows = recompute_value_part
        for share_bit_number in range(group_bits):
            key_other, value_other = from_partner(
                (share_key_rows, share_value_rows), "tp", share_bit_number
            )
            share_upper_half = tp_index // 2**share_bit_number % 2 == 1
            share_key_rows = jnp.where(
                share_upper_half,
                jnp.concatenate([key_other, share_key_rows], 1),
                jnp.concatenate([share_key_rows, key_other], 1),
            )
            share_value_rows = jnp.where(
                share_upper_half,
                jnp.concatenate([value_other, share_value_rows], 1),
                jnp.concatenate([share_value_rows, value_other], 1),
            )
        pieces = (
            recompute_rows32,
            recompute_inverse,
            recompute_positions,
            recompute_allowed,
            recompute_query_rows,
            share_key_rows,
            share_value_rows,
        )
        dout_rows = jnp.einsum(
            "rd,cd->rc", grad_full, out_weight, preferred_element_type=jnp.float32
        ).astype(jnp.bfloat16)
        rows32, inverse, positions, allowed, query_rows, key_rows, value_rows = pieces
        query_heads = query_rows.reshape(ROWS, heads_here, HD).transpose(1, 0, 2)
        dout_heads = dout_rows.reshape(ROWS, heads_here, HD).transpose(1, 0, 2)
        scores = (
            jnp.einsum("hrd,cd->hrc", query_heads, key_rows, preferred_element_type=jnp.float32)
            * score_scale
        )
        weights = jnp.where(allowed[None, :, :], jnp.exp(scores), 0.0)
        softmax = weights / jnp.sum(weights, axis=2, keepdims=True)
        softmax_low = softmax.astype(jnp.bfloat16)
        dprobs = jnp.einsum(
            "hrd,cd->hrc", dout_heads, value_rows, preferred_element_type=jnp.float32
        )
        dvalues = jnp.einsum(
            "hrc,hrd->cd", softmax_low, dout_heads, preferred_element_type=jnp.float32
        )
        row_delta = jnp.sum(softmax * dprobs, axis=2, keepdims=True)
        dscores = (softmax * (dprobs - row_delta) * score_scale).astype(jnp.bfloat16)
        dquery = jnp.einsum(
            "hrc,cd->rhd", dscores, key_rows, preferred_element_type=jnp.float32
        ).reshape(ROWS, query_share)
        feature_dkey_sum = jnp.einsum(
            "hrc,hrd->cd", dscores, query_heads, preferred_element_type=jnp.float32
        )
        dquery = rotate_pairs(dquery, positions, query_start, -1.0).astype(jnp.bfloat16)
        key_part = feature_dkey_sum
        value_part = dvalues
        for bit_number in reversed(range(group_bits)):
            half_width = key_part.shape[1] // 2
            upper_half = tp_index // 2**bit_number % 2 == 1
            key_send = jnp.where(upper_half, key_part[:, :half_width], key_part[:, half_width:])
            key_keep = jnp.where(upper_half, key_part[:, half_width:], key_part[:, :half_width])
            value_send = jnp.where(
                upper_half, value_part[:, :half_width], value_part[:, half_width:]
            )
            value_keep = jnp.where(
                upper_half, value_part[:, half_width:], value_part[:, :half_width]
            )
            key_got, value_got = (
                from_partner(key_send.astype(jnp.bfloat16), "tp", bit_number).astype(
                    key_send.dtype
                ),
                from_partner(value_send.astype(jnp.bfloat16), "tp", bit_number).astype(
                    value_send.dtype
                ),
            )
            key_part = key_keep + key_got
            value_part = value_keep + value_got
        dkey_part = key_part
        dvalue_part = value_part
        dkey_part = rotate_pairs(dkey_part, positions, kv_start, -1.0).astype(jnp.bfloat16)
        dvalue_part = dvalue_part.astype(jnp.bfloat16)
        partial_value = jnp.einsum(
            "rc,dc->rd", dquery, query_weight, preferred_element_type=jnp.float32
        )
        partial_value = partial_value + jnp.einsum(
            "rc,dc->rd", dkey_part, key_weight, preferred_element_type=jnp.float32
        )
        partial_value = partial_value + jnp.einsum(
            "rc,dc->rd", dvalue_part, value_weight, preferred_element_type=jnp.float32
        )
        dnormed = lax.psum(partial_value.astype(jnp.bfloat16), "tp").astype(jnp.float32)
        rows32 = pieces[0]
        inverse = pieces[1]
        moment = jnp.sum(rows32 * gain_full * dnormed, axis=1, keepdims=True) / D
        result = (
            grad_full.astype(jnp.float32)
            + inverse * gain_full * dnormed
            - rows32 * inverse**3 * moment
        ).astype(jnp.bfloat16)
        outputs.append(lax.dynamic_slice_in_dim(result, feature_start, feature_share, 1))
        received = shifted(result, "pipe", -1)
        grad_full = jnp.where(last_section, head_rows[tick_index], received)
    carried = lax.dynamic_slice_in_dim(grad_full, feature_start, feature_share, 1)
    emitted = jnp.stack(outputs, axis=0)[None]
    return (emitted, carried[None])


def solution(mesh):
    placed = (
        P("pipe", None, None, "tp"),
        P("pipe", None, "tp"),
        P("pipe", None),
        P("pipe", None, "tp"),
        P("pipe", None, "tp"),
        P("pipe", None, "tp"),
        P("pipe", "tp", None),
        P("pipe", None, None),
        P(None, None, "tp"),
        P(),
        P(),
        P(),
    )
    return jax.shard_map(
        per_device,
        mesh=mesh,
        in_specs=placed,
        out_specs=(P("pipe", None, None, "tp"), P("pipe", None, "tp")),
        check_vma=False,
    )
```

profile of v0, /device:TPU:1, one launch (start us, length us, event | category | flops | bytes accessed | tf_op | source)
XLA Modules:
  0.0 543.1 jit_solution(10631922588093465636)
XLA Ops:
  16.1 57.5 %all-gather.5.cloned.1.call-done = bf16[1,128,4096]{2,1,0:T(8,128)(2,1)} async-done(((bf16[1,128,256]{2,1,0:T(8,128)(2,1)}), bf16[1,128,4096]{2,1,0:T(8,128)(2,1)}) %all-gather.5.cloned.1.call-update) | async-done | bytes 1048592 | tf_op jit(solution)/shard_map/all_gather | solution.py:114
  73.7 2.8 fusion.50
  76.6 63.1 %all-gather.9.cloned.1.call-done = bf16[1,2,128,4096]{3,2,1,0:T(8,128)(2,1)} async-done(((bf16[1,2,128,256]{3,2,1,0:T(8,128)(2,1)}), bf16[1,2,128,4096]{3,2,1,0:T(8,128)(2,1)}) %all-gather.9.cloned.1.call-update) | async-done | bytes 2097168 | tf_op jit(solution)/shard_map/all_gather | solution.py:112
  139.6 1.7 fusion.18
  141.8 1.8 convolution_convert_fusion.1
  143.6 2.8 collective-permute-start.2
  147.1 2.5 collective-permute-start
  149.7 1.7 fusion.38
  152.6 3.7 collective-permute-start.3
  156.4 3.0 collective-permute-start.1
  159.7 2.7 collective-permute-done.1
  162.9 3.0 collective-permute-start.4
  167.1 2.1 fusion.36
  169.3 3.7 collective-permute-start.6
  173.1 2.8 collective-permute-start.5
  175.9 2.5 collective-permute-start.7
  178.5 2.2 convolution_add_fusion.3
  180.7 1.5 fusion.2
  182.5 22.6 %all-gather.7.cloned.1.call-done = bf16[2,128,4096]{2,1,0:T(8,128)(2,1)} async-done(((bf16[2,128,256]{2,1,0:T(8,128)(2,1)}), bf16[2,128,4096]{2,1,0:T(8,128)(2,1)}) %all-gather.7.cloned.1.call-update) | async-done | bytes 2097168 | tf_op jit(solution)/shard_map/all_gather | solution.py:113
  205.1 3.5 multiply_convert_fusion
  208.6 116.3 %all-reduce.3.cloned.1.call-done = bf16[128,4096]{1,0:T(8,128)(2,1)} async-done(((bf16[128,4096]{1,0:T(8,128)(2,1)}), bf16[128,4096]{1,0:T(8,128)(2,1)}) %all-reduce.3.cloned.1.call-update) | async-done | bytes 1048592 | tf_op jit(solution)/shard_map/psum | solution.py:230
  324.9 2.6 fusion.13
  327.6 3.2 fusion.12
  330.8 4.2 collective-permute-start.8
  337.0 2.6 collective-permute-start.9
  339.6 1.7 fusion.34
  342.1 1.8 rev.29
  343.9 1.7 copy.66
  345.6 2.4 convolution_convert_fusion
  350.2 2.7 collective-permute-start.11
  353.7 3.5 collective-permute-start.10
  358.6 3.4 collective-permute-start.12
  362.1 1.6 fusion.102
  363.7 2.7 fusion.53
  368.3 3.5 collective-permute-start.15
  371.9 1.7 fusion.123
  375.5 3.2 collective-permute-start.13
  381.0 1.5 fusion.97
  382.5 2.2 fusion.32
  385.4 2.6 collective-permute-start.14
  388.8 2.7 collective-permute-start.16
  391.6 2.3 convolution_add_fusion.1
  393.9 1.5 fusion.3
  395.4 117.7 %all-reduce.5.cloned.1.call-done = bf16[128,4096]{1,0:T(8,128)(2,1)} async-done(((bf16[128,4096]{1,0:T(8,128)(2,1)}), bf16[128,4096]{1,0:T(8,128)(2,1)}) %all-reduce.5.cloned.1.call-update) | async-done | bytes 1048592 | tf_op jit(solution)/shard_map/psum | solution.py:230
  513.1 2.1 fusion.17
  515.4 2.8 fusion.16
  518.2 4.1 collective-permute-start.17
  523.9 12.0 %collective-permute-done.17 = bf16[128,4096]{1,0:T(8,128)(2,1)S(1)} collective-permute-done((bf16[128,4096]{1,0:T(8,128)(2,1)S(1)}, bf16[128,4096]{1,0:T(8,128)(2,1)S(1)}, u32[]{:S(2)}, u32[]{:S(2)}) %collective-permute-start.17) | collective-permute-done | bytes 1048608 | tf_op jit(solution)/shard_map/ppermute | solution.py:34
  (181 shorter events, 30.6 us)
Async XLA Ops:
  7.2 142.5 %copy-start = (bf16[1,4096,256]{2,1,0:T(8,128)(2,1)S(1)}, bf16[1,4096,256]{2,1,0:T(8,128)(2,1)}, u32[]{:S(2)}) copy-start(bf16[1,4096,256]{2,1,0:T(8,128)(2,1)} %param.15) | copy-start | bytes 6291460
  7.2 66.5 %all-gather.5.cloned.1.call-start = ((), (), s32[]{:S(2)}) async-start(), calls=%async_computation | async-start | bytes 1114112 | tf_op jit(solution)/shard_map/all_gather | solution.py:114
  7.9 131.7 %all-gather.9.cloned.1.call-start = ((), (), s32[]{:S(2)}) async-start(), calls=%async_computation.4 | async-start | bytes 2228224 | tf_op jit(solution)/shard_map/all_gather | solution.py:112
  8.7 196.5 %all-gather.7.cloned.1.call-start = ((), (), s32[]{:S(2)}) async-start(), calls=%async_computation.2 | async-start | bytes 2228224 | tf_op jit(solution)/shard_map/all_gather | solution.py:113
  9.4 315.5 %all-reduce.3.cloned.1.call-start = ((), (), s32[]{:S(2)}) async-start(), calls=%async_computation.1 | async-start | bytes 2097152 | tf_op jit(solution)/shard_map/psum | solution.py:230
  9.5 142.4 %copy-start.20 = (f32[256]{0:T(256)}, f32[256]{0:T(256)S(1)}, u32[]{:S(2)}) copy-start(f32[256]{0:T(256)S(1)} %get-tuple-element.12) | copy-start | bytes 3076
  9.5 142.4 %copy-start.22 = (f32[256]{0:T(256)}, f32[256]{0:T(256)S(1)}, u32[]{:S(2)}) copy-start(f32[256]{0:T(256)S(1)} %get-tuple-element.13) | copy-start | bytes 3076
  9.5 157.0 %copy-start.18 = (f32[2,128]{1,0:T(2,128)}, f32[2,128]{1,0:T(2,128)S(1)}, u32[]{:S(2)}) copy-start(f32[2,128]{1,0:T(2,128)S(1)} %get-tuple-element.16) | copy-start | bytes 3076
  9.6 157.0 %copy-start.19 = (f32[2,128]{1,0:T(2,128)}, f32[2,128]{1,0:T(2,128)S(1)}, u32[]{:S(2)}) copy-start(f32[2,128]{1,0:T(2,128)S(1)} %get-tuple-element.17) | copy-start | bytes 3076
  9.6 137.4 %copy-start.28 = (f32[32]{0:T(128)}, f32[32]{0:T(128)S(1)}, u32[]{:S(2)}) copy-start(f32[32]{0:T(128)S(1)} %get-tuple-element.14) | copy-start | bytes 388
  9.6 168.9 %copy-start.26 = (f32[32]{0:T(128)}, f32[32]{0:T(128)S(1)}, u32[]{:S(2)}) copy-start(f32[32]{0:T(128)S(1)} %get-tuple-element.15) | copy-start | bytes 388
  9.6 168.8 %copy-start.30 = (f32[32]{0:T(128)}, f32[32]{0:T(128)S(1)}, u32[]{:S(2)}) copy-start(f32[32]{0:T(128)S(1)} %broadcast_multiply_fusion) | copy-start | bytes 388
  16.1 125.7 %copy-start.6 = (bf16[1,4096,32]{1,2,0:T(8,128)(2,1)S(1)}, bf16[1,4096,32]{1,2,0:T(8,128)(2,1)}, u32[]{:S(2)}) copy-start(bf16[1,4096,32]{1,2,0:T(8,128)(2,1)} %param.17) | copy-start | bytes 786436
  76.4 70.0 %copy-start.7 = (bf16[1,4096,32]{1,2,0:T(8,128)(2,1)S(1)}, bf16[1,4096,32]{1,2,0:T(8,128)(2,1)}, u32[]{:S(2)}) copy-start(bf16[1,4096,32]{1,2,0:T(8,128)(2,1)} %param.16) | copy-start | bytes 786436
  139.6 6.7 %copy-start.1 = (bf16[1,2,128,4096]{3,2,1,0:T(8,128)(2,1)S(1)}, bf16[1,2,128,4096]{3,2,1,0:T(8,128)(2,1)}, u32[]{:S(2)}) copy-start(bf16[1,2,128,4096]{3,2,1,0:T(8,128)(2,1)} %all-gather.9.cloned.1.call-done) | copy-start | bytes 6291460
  141.8 7.8 %copy-start.33 = (f32[128]{0:T(128)}, f32[128]{0:T(128)S(1)}, u32[]{:S(2)}) copy-start(f32[128]{0:T(128)S(1)} %get-tuple-element.11) | copy-start | bytes 1540
  143.6 9.0 %collective-permute-start.2 = (bf16[128,32]{0,1:T(8,128)(2,1)S(1)}, bf16[128,32]{0,1:T(8,128)(2,1)S(1)}, u32[]{:S(2)}, u32[]{:S(2)}) collective-permute-start(bf16[128,32]{0,1:T(8,128)(2,1)S(1)} %convolution_convert_fusion.1), channel_id=1, source_target_pairs={{0,1},{1,0},{2,3},{3,2},{4,5},{5,4},{6,7},{7,6},{8,9},{9,8},{10,11... | collective-permute-start | bytes 24584 | tf_op jit(solution)/shard_map/ppermute | solution.py:28
  147.1 9.2 %collective-permute-start = (bf16[128,32]{0,1:T(8,128)(2,1)S(1)}, bf16[128,32]{0,1:T(8,128)(2,1)S(1)}, u32[]{:S(2)}, u32[]{:S(2)}) collective-permute-start(bf16[128,32]{0,1:T(8,128)(2,1)S(1)} %fusion.149), channel_id=1, source_target_pairs={{0,1},{1,0},{2,3},{3,2},{4,5},{5,4},{6,7},{7,6},{8,9},{9,8},{10,11... | collective-permute-start | bytes 24584 | tf_op jit(solution)/shard_map/ppermute | solution.py:28
  152.6 6.8 %collective-permute-start.3 = (bf16[128,64]{0,1:T(8,128)(2,1)S(1)}, bf16[128,64]{0,1:T(8,128)(2,1)S(1)}, u32[]{:S(2)}, u32[]{:S(2)}) collective-permute-start(bf16[128,64]{0,1:T(8,128)(2,1)S(1)} %maximum_select_fusion.5), channel_id=1, source_target_pairs={{0,2},{2,0},{1,3},{3,1},{4,6},{6,4},{5,7},{7,5},{8,10},{10,8},{9,1... | collective-permute-start | bytes 49160 | tf_op jit(solution)/shard_map/ppermute | solution.py:28
  156.4 6.0 %collective-permute-start.1 = (bf16[128,64]{0,1:T(8,128)(2,1)S(1)}, bf16[128,64]{0,1:T(8,128)(2,1)S(1)}, u32[]{:S(2)}, u32[]{:S(2)}) collective-permute-start(bf16[128,64]{0,1:T(8,128)(2,1)S(1)} %maximum_select_fusion.4), channel_id=1, source_target_pairs={{0,2},{2,0},{1,3},{3,1},{4,6},{6,4},{5,7},{7,5},{8,10},{10,8},{9,1... | collective-permute-start | bytes 49160 | tf_op jit(solution)/shard_map/ppermute | solution.py:28
  162.9 10.2 %collective-permute-start.4 = (bf16[128,64]{0,1:T(8,128)(2,1)S(1)}, bf16[128,64]{0,1:T(8,128)(2,1)S(1)}, u32[]{:S(2)}, u32[]{:S(2)}) collective-permute-start(bf16[128,64]{0,1:T(8,128)(2,1)S(1)} %select_convert_fusion.3), channel_id=1, source_target_pairs={{0,2},{2,0},{1,3},{3,1},{4,6},{6,4},{5,7},{7,5},{8,10},{10,8},{9,1... | collective-permute-start | bytes 49160 | tf_op jit(solution)/shard_map/ppermute | solution.py:28
  169.3 6.5 %collective-permute-start.6 = (bf16[128,64]{0,1:T(8,128)(2,1)S(1)}, bf16[128,64]{0,1:T(8,128)(2,1)S(1)}, u32[]{:S(2)}, u32[]{:S(2)}) collective-permute-start(bf16[128,64]{0,1:T(8,128)(2,1)S(1)} %select_convert_fusion.2), channel_id=1, source_target_pairs={{0,2},{2,0},{1,3},{3,1},{4,6},{6,4},{5,7},{7,5},{8,10},{10,8},{9,1... | collective-permute-start | bytes 49160 | tf_op jit(solution)/shard_map/ppermute | solution.py:28
  173.1 5.3 collective-permute-start.5
  175.9 4.8 collective-permute-start.7
  182.2 330.9 %all-reduce.5.cloned.1.call-start = ((), (), s32[]{:S(2)}) async-start(), calls=%async_computation.3 | async-start | bytes 2097152 | tf_op jit(solution)/shard_map/psum | solution.py:230
  208.6 118.9 %copy-start.5 = (bf16[1,128,4096]{2,1,0:T(8,128)(2,1)S(1)}, bf16[1,128,4096]{2,1,0:T(8,128)(2,1)}, u32[]{:S(2)}) copy-start(bf16[1,128,4096]{2,1,0:T(8,128)(2,1)} %all-gather.5.cloned.1.call-done) | copy-start | bytes 3145732
  208.6 119.0 %copy-start.32 = (f32[128]{0:T(128)S(1)}, f32[128]{0:T(128)}, u32[]{:S(2)}) copy-start(f32[128]{0:T(128)} %get-tuple-element.10) | copy-start | bytes 1540
  208.6 119.0 %copy-start.34 = (f32[128]{0:T(128)S(1)}, f32[128]{0:T(128)}, u32[]{:S(2)}) copy-start(f32[128]{0:T(128)} %copy-done.33) | copy-start | bytes 1540
  327.6 8.0 %copy-start.8 = (bf16[1,4096,32]{1,2,0:T(8,128)(2,1)S(1)}, bf16[1,4096,32]{1,2,0:T(8,128)(2,1)}, u32[]{:S(2)}) copy-start(bf16[1,4096,32]{1,2,0:T(8,128)(2,1)} %param.16) | copy-start | bytes 786436
  330.8 5.5 %copy-start.27 = (f32[32]{0:T(128)S(1)}, f32[32]{0:T(128)}, u32[]{:S(2)}) copy-start(f32[32]{0:T(128)} %copy-done.26) | copy-start | bytes 388
  330.8 5.5 %copy-start.29 = (f32[32]{0:T(128)S(1)}, f32[32]{0:T(128)}, u32[]{:S(2)}) copy-start(f32[32]{0:T(128)} %copy-done.28) | copy-start | bytes 388
  330.8 32.9 %collective-permute-start.8 = (bf16[128,4096]{1,0:T(8,128)(2,1)}, bf16[128,4096]{1,0:T(8,128)(2,1)S(1)}, u32[]{:S(2)}, u32[]{:S(2)}) collective-permute-start(bf16[128,4096]{1,0:T(8,128)(2,1)} %fusion.12), channel_id=1, source_target_pairs={{16,0},{32,16},{48,32},{64,48},{80,64},{96,80},{112,96},{128,112},... | collective-permute-start | bytes 3145736 | tf_op jit(solution)/shard_map/ppermute | solution.py:34
  337.0 15.8 %collective-permute-start.9 = (bf16[128,32]{0,1:T(8,128)(2,1)}, bf16[128,32]{0,1:T(8,128)(2,1)}, u32[]{:S(2)}, u32[]{:S(2)}) collective-permute-start(bf16[128,32]{0,1:T(8,128)(2,1)} %fusion.145), channel_id=1, source_target_pairs={{0,1},{1,0},{2,3},{3,2},{4,5},{5,4},{6,7},{7,6},{8,9},{9,8},{10,11... | collective-permute-start | bytes 24584 | tf_op jit(solution)/shard_map/ppermute | solution.py:28
  350.2 13.5 %copy-start.16 = (bf16[128,256]{0,1:T(8,128)(2,1)}, bf16[128,256]{0,1:T(8,128)(2,1)S(1)}, u32[]{:S(2)}) copy-start(bf16[128,256]{0,1:T(8,128)(2,1)S(1)} %copy.94) | copy-start | bytes 196612
  350.2 7.1 %collective-permute-start.11 = (bf16[128,32]{0,1:T(8,128)(2,1)}, bf16[128,32]{0,1:T(8,128)(2,1)S(1)}, u32[]{:S(2)}, u32[]{:S(2)}) collective-permute-start(bf16[128,32]{0,1:T(8,128)(2,1)} %convolution_convert_fusion), channel_id=1, source_target_pairs={{0,1},{1,0},{2,3},{3,2},{4,5},{5,4},{6,7},{7,6},{8,9},{9,8},{10,11... | collective-permute-start | bytes 24584 | tf_op jit(solution)/shard_map/ppermute | solution.py:28
  353.7 10.0 %copy-start.17 = (bf16[128,64]{0,1:T(8,128)(2,1)}, bf16[128,64]{0,1:T(8,128)(2,1)S(1)}, u32[]{:S(2)}) copy-start(bf16[128,64]{0,1:T(8,128)(2,1)S(1)} %maximum_select_fusion.6) | copy-start | bytes 49156
  353.7 8.4 %collective-permute-start.10 = (bf16[128,64]{0,1:T(8,128)(2,1)S(1)}, bf16[128,64]{0,1:T(8,128)(2,1)S(1)}, u32[]{:S(2)}, u32[]{:S(2)}) collective-permute-start(bf16[128,64]{0,1:T(8,128)(2,1)S(1)} %maximum_select_fusion.6), channel_id=1, source_target_pairs={{0,2},{2,0},{1,3},{3,1},{4,6},{6,4},{5,7},{7,5},{8,10},{10,8},{9,1... | collective-permute-start | bytes 49160 | tf_op jit(solution)/shard_map/ppermute | solution.py:28
  358.6 13.2 %collective-permute-start.12 = (bf16[128,64]{0,1:T(8,128)(2,1)}, bf16[128,64]{0,1:T(8,128)(2,1)}, u32[]{:S(2)}, u32[]{:S(2)}) collective-permute-start(bf16[128,64]{0,1:T(8,128)(2,1)} %maximum_select_fusion.7), channel_id=1, source_target_pairs={{0,2},{2,0},{1,3},{3,1},{4,6},{6,4},{5,7},{7,5},{8,10},{10,8},{9,1... | collective-permute-start | bytes 49160 | tf_op jit(solution)/shard_map/ppermute | solution.py:28
  367.6 7.8 %copy-start.10 = (f32[128,128]{0,1:T(8,128)}, f32[128,128]{0,1:T(8,128)S(1)}, u32[]{:S(2)}) copy-start(f32[128,128]{0,1:T(8,128)S(1)} %convolution_bitcast_fusion) | copy-start | bytes 196612
  368.3 19.7 %collective-permute-start.15 = (bf16[128,64]{0,1:T(8,128)(2,1)}, bf16[128,64]{0,1:T(8,128)(2,1)}, u32[]{:S(2)}, u32[]{:S(2)}) collective-permute-start(bf16[128,64]{0,1:T(8,128)(2,1)} %select_convert_fusion), channel_id=1, source_target_pairs={{0,2},{2,0},{1,3},{3,1},{4,6},{6,4},{5,7},{7,5},{8,10},{10,8},{9,1... | collective-permute-start | bytes 49160 | tf_op jit(solution)/shard_map/ppermute | solution.py:28
  375.5 9.2 %collective-permute-start.13 = (bf16[128,64]{0,1:T(8,128)(2,1)}, bf16[128,64]{0,1:T(8,128)(2,1)}, u32[]{:S(2)}, u32[]{:S(2)}) collective-permute-start(bf16[128,64]{0,1:T(8,128)(2,1)} %select_convert_fusion.1), channel_id=1, source_target_pairs={{0,2},{2,0},{1,3},{3,1},{4,6},{6,4},{5,7},{7,5},{8,10},{10,8},{9,1... | collective-permute-start | bytes 49160 | tf_op jit(solution)/shard_map/ppermute | solution.py:28
  382.5 5.6 %copy-start.11 = (f32[128,128]{0,1:T(8,128)S(1)}, f32[128,128]{0,1:T(8,128)}, u32[]{:S(2)}) copy-start(f32[128,128]{0,1:T(8,128)} %copy-done.10) | copy-start | bytes 196612
  385.4 6.1 %collective-permute-start.14 = (bf16[128,32]{0,1:T(8,128)(2,1)S(1)}, bf16[128,32]{0,1:T(8,128)(2,1)S(1)}, u32[]{:S(2)}, u32[]{:S(2)}) collective-permute-start(bf16[128,32]{0,1:T(8,128)(2,1)S(1)} %select_convert_fusion.5), channel_id=1, source_target_pairs={{0,1},{1,0},{2,3},{3,2},{4,5},{5,4},{6,7},{7,6},{8,9},{9,8},{10,11... | collective-permute-start | bytes 24584 | tf_op jit(solution)/shard_map/ppermute | solution.py:28
  388.8 5.1 collective-permute-start.16
  395.4 119.9 %copy-start.35 = (f32[128]{0:T(128)S(1)}, f32[128]{0:T(128)}, u32[]{:S(2)}) copy-start(f32[128]{0:T(128)} %get-tuple-element.8) | copy-start | bytes 1540
  395.4 119.9 %copy-start.37 = (f32[128]{0:T(128)S(1)}, f32[128]{0:T(128)}, u32[]{:S(2)}) copy-start(f32[128]{0:T(128)} %copy-done.36) | copy-start | bytes 1540
  515.3 6.9 %copy-start.4 = (bf16[2,128,4096]{2,1,0:T(8,128)(2,1)S(1)}, bf16[2,128,4096]{2,1,0:T(8,128)(2,1)}, u32[]{:S(2)}) copy-start(bf16[2,128,4096]{2,1,0:T(8,128)(2,1)} %multiply_convert_fusion) | copy-start | bytes 6291460
  518.2 17.7 %collective-permute-start.17 = (bf16[128,4096]{1,0:T(8,128)(2,1)S(1)}, bf16[128,4096]{1,0:T(8,128)(2,1)S(1)}, u32[]{:S(2)}, u32[]{:S(2)}) collective-permute-start(bf16[128,4096]{1,0:T(8,128)(2,1)S(1)} %fusion.16), channel_id=1, source_target_pairs={{16,0},{32,16},{48,32},{64,48},{80,64},{96,80},{112,96},{128,112},... | collective-permute-start | bytes 3145736 | tf_op jit(solution)/shard_map/ppermute | solution.py:34
  (14 other events, 31.8 us)
Sparse Core Ops, SparseCore 0:
  11.0 62.6 all-gather.4
  76.7 62.9 all-gather.8
  142.6 62.4 all-gather.6
  208.2 116.6 all-reduce.2
  395.5 117.5 all-reduce.4
where the time goes:
time: 545 us; the launch traced here: 543 us
  waiting for transfers between devices  394 us (72%)
  starting transfers between devices  56.9 us (10%)
  other arithmetic  34.1 us (6%)
  matrix products  33.8 us (6%)
  between operations  14.8 us (3%)
  local copies, waits for them, and re-layouts  9.46 us (2%)
    psum x2, waiting for transfers between devices, per_device(): lax.psum(partial_value.astype(jnp.bfloat16), 'tp').astype(jnp.float32)  234 us
    all_gather x1, waiting for transfers between devices, per_device(): lax.all_gather(saved[0], 'tp', axis=2, tiled=True)  63.1 us
    all_gather x1, waiting for transfers between devices, per_device(): lax.all_gather(incoming, 'tp', axis=2, tiled=True)  57.5 us
    ppermute x16, starting transfers between devices, from_partner(): return lax.ppermute(block, axis, route)  48.4 us
    all_gather x1, waiting for transfers between devices, per_device(): lax.all_gather(score_grad, 'tp', axis=2, tiled=True)  22.6 us
    ppermute x2, waiting for transfers between devices, shifted(): lax.ppermute(value, axis, [(source, source + steps) for source in range(f...  12 us
  transfers between devices with their start and end apart: 23, of which 7 were waited for; matrix products, arithmetic and copies ran while one was open for 12% of the time, Pallas kernels for 0%

commit v1 on v0

v1 whole, which is shorter than its diff:
```python
import math

import jax
import jax.numpy as jnp
from jax import lax
from jax.experimental import pallas as pl
from jax.experimental.pallas import tpu as pltpu
from jax.sharding import PartitionSpec as P

D = 4096
KV = 4
HD = 128
ROWS = 128
TICKS = 2
GROUP_SIZE = 16
GROUPS = 32

EPS = 1e-05
THETA = 500000.0
SCALE = 1.0 / math.sqrt(HD)
F32 = jnp.float32
BF16 = jnp.bfloat16
VMEM_LIMIT = 48 * 1024 * 1024


def nn(a, b):
    return lax.dot_general(a, b, (((1,), (0,)), ((), ())), preferred_element_type=F32)


def nt(a, b):
    return lax.dot_general(a, b, (((1,), (1,)), ((), ())), preferred_element_type=F32)


def tn(a, b):
    return lax.dot_general(a, b, (((0,), (0,)), ((), ())), preferred_element_type=F32)


def pair_swap(v, axis):
    n = v.shape[axis]
    even = lax.broadcasted_iota(jnp.int32, v.shape, axis) % 2 == 0
    return jnp.where(even, pltpu.roll(v, n - 1, axis), pltpu.roll(v, 1, axis))


def kernel_call(body, outs, *args):
    vmem = pl.BlockSpec(memory_space=pltpu.VMEM)
    return pl.pallas_call(
        body,
        out_shape=outs,
        in_specs=[vmem] * len(args),
        out_specs=[vmem] * len(outs),
        compiler_params=pltpu.CompilerParams(vmem_limit_bytes=VMEM_LIMIT),
    )(*args)


def forward_body(
    x_ref, gain_ref, wq_ref, wkv_ref, cos_ref, sin_ref, cost_ref, sint_ref, q_ref, kv_ref, inv_ref
):
    blocks, rows, width = x_ref.shape
    squares = jnp.zeros((rows, width), F32)
    for j in range(blocks):
        xj = x_ref[j].astype(F32)
        squares = squares + xj * xj
    inverse = lax.rsqrt(jnp.sum(squares, axis=1, keepdims=True) * (1.0 / D) + EPS)
    inv_ref[...] = inverse
    query = jnp.zeros(q_ref.shape, F32)
    kvt = jnp.zeros(kv_ref.shape[1:], F32)
    for j in range(blocks):
        part = slice(j * width, (j + 1) * width)
        normed = (x_ref[j].astype(F32) * inverse * gain_ref[:, part].astype(F32)).astype(BF16)
        query = query + nn(normed, wq_ref[part, :])
        kvt = kvt + nt(wkv_ref[:, part], normed)
    for h in range(query.shape[1] // HD):
        cols = slice(h * HD, (h + 1) * HD)
        head = query[:, cols]
        q_ref[:, cols] = (head * cos_ref[...] + pair_swap(head, 1) * sin_ref[...]).astype(BF16)
    half = kvt.shape[0] // 2
    keys = kvt[:half]
    keys = keys * cost_ref[...] + pair_swap(keys, 0) * sint_ref[...]
    both = jnp.concatenate([keys, kvt[half:]], axis=0).astype(BF16)
    for i in range(kv_ref.shape[0]):
        kv_ref[i] = both


def attention_body(
    dy_ref, wo_ref, q_ref, kv_ref, mask_ref, cos_ref, sin_ref, dq_ref, dkv_ref, t_ref
):
    blocks, rows, width = dy_ref.shape
    dout = jnp.zeros(dq_ref.shape, F32)
    for j in range(blocks):
        dout = dout + nt(dy_ref[j], wo_ref[:, j * width : (j + 1) * width])
    dout = dout.astype(BF16)
    shares, both, _ = kv_ref.shape
    half = both // 2
    keys = jnp.concatenate([kv_ref[i, :half] for i in range(shares)], axis=0)
    values = jnp.concatenate([kv_ref[i, half:] for i in range(shares)], axis=0)
    allowed = mask_ref[...] > 0.0
    dkeys = jnp.zeros((HD, rows), F32)
    dvalues = jnp.zeros((HD, rows), F32)
    own = jnp.zeros((rows, HD), F32)
    for h in range(dq_ref.shape[1] // HD):
        cols = slice(h * HD, (h + 1) * HD)
        query = q_ref[:, cols]
        dhead = dout[:, cols]
        weights = jnp.where(allowed, jnp.exp(nn(query, keys) * SCALE), 0.0)
        softmax = weights / jnp.sum(weights, axis=1, keepdims=True)
        dprobs = nn(dhead, values)
        delta = jnp.sum(softmax * dprobs, axis=1, keepdims=True)
        dscores = (softmax * (dprobs - delta) * SCALE).astype(BF16)
        dquery = nt(dscores, keys)
        dkeys = dkeys + tn(query, dscores)
        dvalues = dvalues + tn(dhead, softmax.astype(BF16))
        own = own + dquery * query.astype(F32)
        dq_ref[:, cols] = (dquery * cos_ref[...] - pair_swap(dquery, 1) * sin_ref[...]).astype(BF16)
    shared = dkeys * keys.astype(F32) + dvalues * values.astype(F32)
    t_ref[...] = jnp.sum(own + shared.T, axis=1, keepdims=True)
    for i in range(shares):
        part = slice(i * half, (i + 1) * half)
        dkv_ref[i, :half] = dkeys[part].astype(BF16)
        dkv_ref[i, half:] = dvalues[part].astype(BF16)


def partial_body(
    dq_ref, dkv_ref, wq_ref, wkv_ref, x_ref, gain_ref, inv_ref, t_ref, cost_ref, sint_ref, out_ref
):
    blocks, _, width = x_ref.shape
    dkv = dkv_ref[0].astype(F32)
    for i in range(1, dkv_ref.shape[0]):
        dkv = dkv + dkv_ref[i].astype(F32)
    half = dkv.shape[0] // 2
    dkeys = dkv[:half]
    dkeys = dkeys * cost_ref[...] - pair_swap(dkeys, 0) * sint_ref[...]
    dkv = jnp.concatenate([dkeys, dkv[half:]], axis=0).astype(BF16)
    dq = dq_ref[...]
    inverse = inv_ref[...]
    along = inverse * inverse * t_ref[...] * (1.0 / D)
    for j in range(blocks):
        part = slice(j * width, (j + 1) * width)
        total = nt(dq, wq_ref[part, :]) + tn(dkv, wkv_ref[:, part])
        scaled = total * (inverse * gain_ref[:, part].astype(F32))
        out_ref[j] = (scaled - x_ref[j].astype(F32) * along).astype(BF16)


def shifted(value, axis, steps):
    count = lax.axis_size(axis)
    first, last = (max(0, -steps), min(count, count - steps))
    return lax.ppermute(value, axis, [(source, source + steps) for source in range(first, last)])


def rotation_tables(positions):
    column = jnp.arange(HD, dtype=jnp.int32)
    pair_index = (column // 2).astype(F32)
    frequency = jnp.exp(pair_index * (-2.0 * math.log(THETA) / HD))
    angles = positions.astype(F32)[:, None] * frequency[None, :]
    parity = jnp.where(column % 2 == 0, -1.0, 1.0).astype(F32)
    return jnp.cos(angles), jnp.sin(angles) * parity


def row_layout(lengths):
    row_ids = jnp.arange(ROWS, dtype=jnp.int32)
    seg_ends = jnp.cumsum(lengths)
    segment = jnp.sum((row_ids[:, None] >= seg_ends[None, :]).astype(jnp.int32), axis=1)
    member = segment[:, None] == jnp.arange(lengths.shape[0], dtype=jnp.int32)[None, :]
    begins = jnp.sum(jnp.where(member, (seg_ends - lengths)[None, :], 0), axis=1)
    positions = row_ids - begins
    allowed = (segment[:, None] == segment[None, :]) & (row_ids[None, :] <= row_ids[:, None])
    return (positions, allowed)


def advantages(rewards, sample_group):
    member = (sample_group[:, None] == jnp.arange(GROUPS, dtype=jnp.int32)[None, :]).astype(F32)
    totals = jnp.sum(member * rewards[:, None], axis=0)
    own_total = jnp.sum(member * totals[None, :], axis=1)
    return rewards - (own_total - rewards) / (GROUP_SIZE - 1)


def head_gradient(advantage, head_sample, score_grad):
    chosen = (
        head_sample[:, :, None] == jnp.arange(advantage.shape[0], dtype=jnp.int32)[None, None, :]
    )
    row_adv = jnp.sum(jnp.where(chosen, advantage[None, None, :], 0.0), axis=2)
    return (-row_adv[:, :, None] * score_grad.astype(F32)).astype(BF16)


def per_device(
    saved,
    incoming,
    gain,
    w_query,
    w_key,
    w_value,
    w_out,
    seg_lengths,
    score_grad,
    rewards,
    sample_group,
    head_sample,
):
    tp_index = lax.axis_index("tp")
    tp_count = lax.axis_size("tp")
    last_section = lax.axis_index("pipe") == lax.axis_size("pipe") - 1
    share = tp_count // KV
    groups = [list(range(g * share, (g + 1) * share)) for g in range(KV)]
    kv_share = w_key.shape[2]
    kv_start = (tp_index % share) * kv_share
    wq = w_query[0]
    wkv = jnp.concatenate([w_key[0].T, w_value[0].T], axis=0)
    wo = w_out[0]

    def to_all(block):
        return lax.all_to_all(
            jnp.broadcast_to(block[None], (tp_count,) + block.shape), "tp", 0, 0
        )

    def in_group(blocks):
        return lax.all_to_all(blocks, "tp", 0, 0, axis_index_groups=groups)

    x_next = lax.all_gather(saved[0, 1], "tp", axis=0)
    x_full = to_all(saved[0, 0])
    grad, x_full = lax.optimization_barrier((incoming[0], x_full))
    grad_full = to_all(grad)
    head_rows = head_gradient(advantages(rewards, sample_group), head_sample, score_grad)

    def forward(tick, rows_full):
        positions, allowed = row_layout(seg_lengths[0, tick])
        cos, sin = rotation_tables(positions)
        cos_t = lax.dynamic_slice_in_dim(cos.T, kv_start, kv_share, 0)
        sin_t = lax.dynamic_slice_in_dim(sin.T, kv_start, kv_share, 0)
        query, kv, inverse = kernel_call(
            forward_body,
            (
                jax.ShapeDtypeStruct((ROWS, wq.shape[1]), BF16),
                jax.ShapeDtypeStruct((share, 2 * kv_share, ROWS), BF16),
                jax.ShapeDtypeStruct((ROWS, 1), F32),
            ),
            rows_full, gain, wq, wkv, cos, sin, cos_t, sin_t,
        )
        return query, in_group(kv), inverse, allowed.astype(F32), cos, sin, cos_t, sin_t

    outputs = []
    for tick in range(TICKS):
        rows_full = x_full if tick == 0 else x_next
        query, kv, inverse, mask, cos, sin, cos_t, sin_t = forward(tick, rows_full)
        dquery, dkv, along = kernel_call(
            attention_body,
            (
                jax.ShapeDtypeStruct(query.shape, BF16),
                jax.ShapeDtypeStruct(kv.shape, BF16),
                jax.ShapeDtypeStruct((ROWS, 1), F32),
            ),
            grad_full, wo, query, kv, mask, cos, sin,
        )
        dkv = in_group(dkv)
        (blocks,) = kernel_call(
            partial_body,
            (jax.ShapeDtypeStruct(rows_full.shape, BF16),),
            dquery, dkv, wq, wkv, rows_full, gain, inverse, along, cos_t, sin_t,
        )
        blocks = lax.all_to_all(blocks, "tp", 0, 0)
        result = (grad.astype(F32) + jnp.sum(blocks.astype(F32), axis=0)).astype(BF16)
        outputs.append(result)
        grad = jnp.where(last_section, head_rows[tick], shifted(result, "pipe", -1))
        if tick + 1 < TICKS:
            grad_full = to_all(grad)
    return (jnp.stack(outputs, axis=0)[None], grad[None])


def solution(mesh):
    placed = (
        P("pipe", None, None, "tp"),
        P("pipe", None, "tp"),
        P("pipe", None),
        P("pipe", None, "tp"),
        P("pipe", None, "tp"),
        P("pipe", None, "tp"),
        P("pipe", "tp", None),
        P("pipe", None, None),
        P(None, None, "tp"),
        P(),
        P(),
        P(),
    )
    return jax.shard_map(
        per_device,
        mesh=mesh,
        in_specs=placed,
        out_specs=(P("pipe", None, None, "tp"), P("pipe", None, "tp")),
        check_vma=False,
    )
```

time: 545 us -> 200 us (0.37)
  waiting for transfers between devices: 394 us -> 70.5 us
  blocking collectives: 0 us -> 39.9 us
  matrix products: 33.8 us -> 0 us
  other arithmetic: 34.1 us -> 5.72 us
  Pallas kernels: 0 us -> 13.6 us
  starting transfers between devices: 56.9 us -> 43.8 us
    psum x2 -> x0, waiting for transfers between devices: 234 us -> none  [per_device(): lax.psum(partial_value.astype(jnp.bfloat16), 'tp').astype(jnp.float32)]
    all_gather x3 -> x1, waiting for transfers between devices: 143 us -> 19.1 us  [per_device(): x_next = lax.all_gather(saved[0, 1], 'tp', axis=0)]
    ppermute x16 -> x0, starting transfers between devices: 48.4 us -> none  [from_partner(): return lax.ppermute(block, axis, route)]
    all_to_all x0 -> x5, waiting for transfers between devices: none -> 48.3 us  [the longest x3 32.1 us: to_all(): lax.all_to_all(jnp.broadcast_to(block[None], (tp_count,) + block.shape),...]
    all_to_all x0 -> x4, blocking collectives: none -> 39.9 us  [the longest x3 23.1 us: in_group(): return lax.all_to_all(blocks, 'tp', 0, 0, axis_index_groups=groups)]
    dot_general x22 -> x0, matrix products: 31.9 us -> none  [the longest x2 5.5 us: per_device(): jnp.einsum('rd,cd->rc', grad_full, out_weight, preferred_element_type=jnp...]
    all_to_all x0 -> x5, starting transfers between devices: none -> 25.5 us  [the longest x3 17.5 us: to_all(): lax.all_to_all(jnp.broadcast_to(block[None], (tp_count,) + block.shape),...]
    convert_element_type x19 -> x7, other arithmetic: 16.1 us -> 0.3 us  [the longest x2 0.16 us: forward(): allowed.astype(F32)]
  transfers between devices with their start and end apart: 23 -> 8, of which waited for: 7 -> 7; matrix products, arithmetic and copies ran while one was open for 12% -> 3% of each run, Pallas kernels for 0% -> 4%
where the time goes in v1:
time: 200 us; the launch traced here: 199 us
  waiting for transfers between devices  70.5 us (35%)
  starting transfers between devices  43.8 us (22%)
  blocking collectives  39.9 us (20%)
  between operations  14.4 us (7%)
  Pallas kernels  13.6 us (7%)
  local copies, waits for them, and re-layouts  10.7 us (5%)
  other arithmetic  5.72 us (3%)
    all_to_all x3, waiting for transfers between devices, to_all(): lax.all_to_all(jnp.broadcast_to(block[None], (tp_count,) + block.shape),...  32.1 us
    all_to_all x3, blocking collectives, in_group(): return lax.all_to_all(blocks, 'tp', 0, 0, axis_index_groups=groups)  23.1 us
    all_gather x1, waiting for transfers between devices, per_device(): x_next = lax.all_gather(saved[0, 1], 'tp', axis=0)  19.1 us
    ppermute x2, starting transfers between devices, shifted(): lax.ppermute(value, axis, [(source, source + steps) for source in range(f...  18.3 us
    all_to_all x3, starting transfers between devices, to_all(): lax.all_to_all(jnp.broadcast_to(block[None], (tp_count,) + block.shape),...  17.5 us
    all_to_all x1, blocking collectives, per_device(): blocks = lax.all_to_all(blocks, 'tp', 0, 0)  16.8 us
    pallas_call x6, Pallas kernels, kernel_call(): pl.pallas_call(body, out_shape=outs, in_specs=[vmem] * len(args), out_spe...  13.6 us
    all_to_all x1, waiting for transfers between devices, per_device(): blocks = lax.all_to_all(blocks, 'tp', 0, 0)  11.8 us
  transfers between devices with their start and end apart: 8, of which 7 were waited for; matrix products, arithmetic and copies ran while one was open for 3% of the time, Pallas kernels for 4%

profile of v1, /device:TPU:1, one launch (start us, length us, event | category | flops | bytes accessed | tf_op | source)
XLA Modules:
  0.0 198.6 jit_solution(4913016512467958649)
XLA Ops:
  7.2 1.6 fusion.12
  8.7 1.1 broadcast_in_dim.53
  9.8 7.8 %all-to-all-start = ((bf16[16,128,256]{2,1,0:T(8,128)(2,1)}), bf16[16,128,256]{2,1,0:T(8,128)(2,1)}, u32[]{:S(2)}, u32[]{:S(2)}) async-start(bf16[16,128,256]{2,1,0:T(8,128)(2,1)} %broadcast_in_dim.53), calls=%async_computation | async-start | bytes 2097152 | tf_op jit(solution)/shard_map/all_to_all | solution.py:210
  17.6 0.2 reduce-window.15
  17.8 0.2 reduce-window.14
  18.3 0.6 fusion.1
  18.8 0.1 copy.31.cos_ref
  18.9 0.1 copy.32.sin_ref
  19.1 1.0 pad_maximum_fusion.wkv_ref
  20.1 9.3 %all-to-all-done.x_ref = bf16[16,128,256]{2,1,0:T(8,128)(2,1)} async-done(((bf16[16,128,256]{2,1,0:T(8,128)(2,1)}), bf16[16,128,256]{2,1,0:T(8,128)(2,1)}, u32[]{:S(2)}, u32[]{:S(2)}) %all-to-all-start) | async-done | bytes 1048608 | tf_op jit(solution)/shard_map/all_to_all | solution.py:210
  29.4 2.3 %shard_map.131 = (bf16[128,256]{1,0:T(8,128)(2,1)S(1)}, bf16[4,64,128]{2,1,0:T(8,128)(2,1)S(1)}, f32[128,1]{1,0:T(8,128)S(1)}) custom-call(bf16[16,128,256]{2,1,0:T(8,128)(2,1)} %all-to-all-done.x_ref, bf16[1,4096]{1,0:T(2,128)(2,1)S(1)} %copy-done.6, bf16[4096,256]{1,0:T(8,128)(2,1)S(1)} %bitcast.48, bf16[64,4096]{1,0:T(8,128)(2,1)S(1)} %pad_maximum_fusion.wkv_ref, ...), custom_call_target="tpu_custom_call" | custom-call | tf_op jit(solution)/shard_map/pallas_call | solution.py:46
  31.7 8.1 %all_to_all.45.kv_ref = bf16[4,64,128]{2,1,0:T(8,128)(2,1)S(1)} all-to-all(bf16[4,64,128]{2,1,0:T(8,128)(2,1)S(1)} %get-tuple-element.19), channel_id=1, replica_groups={{0,1,2,3},{4,5,6,7},{8,9,10,11},{12,13,14,15},{16,17,18,19},{20,21,22,2..., dimensions={0} | all-to-all | bytes 131072 | tf_op jit(solution)/shard_map/all_to_all | solution.py:215
  39.8 1.1 broadcast_in_dim.54
  40.9 5.4 %all-to-all-start.1 = ((bf16[16,128,256]{2,1,0:T(8,128)(2,1)}), bf16[16,128,256]{2,1,0:T(8,128)(2,1)}, u32[]{:S(2)}, u32[]{:S(2)}) async-start(bf16[16,128,256]{2,1,0:T(8,128)(2,1)} %broadcast_in_dim.54), calls=%async_computation.1 | async-start | bytes 2097152 | tf_op jit(solution)/shard_map/all_to_all | solution.py:210
  46.4 0.7 all-gather.3.cloned.1.call-update
  47.2 11.1 %all-to-all-done.1.dy_ref = bf16[16,128,256]{2,1,0:T(8,128)(2,1)} async-done(((bf16[16,128,256]{2,1,0:T(8,128)(2,1)}), bf16[16,128,256]{2,1,0:T(8,128)(2,1)}, u32[]{:S(2)}, u32[]{:S(2)}) %all-to-all-start.1) | async-done | bytes 1048608 | tf_op jit(solution)/shard_map/all_to_all | solution.py:210
  58.3 1.6 copy-done.1
  59.9 3.0 %shard_map.132 = (bf16[128,256]{1,0:T(8,128)(2,1)S(1)}, bf16[4,64,128]{2,1,0:T(8,128)(2,1)S(1)}, f32[128,1]{1,0:T(8,128)S(1)}) custom-call(bf16[16,128,256]{2,1,0:T(8,128)(2,1)} %all-to-all-done.1.dy_ref, bf16[256,4096]{1,0:T(8,128)(2,1)S(1)} %bitcast.52, bf16[128,256]{1,0:T(8,128)(2,1)S(1)} %get-tuple-element.18.q_ref, ...), custom_call_target="tpu_custom_call" | custom-call | tf_op jit(solution)/shard_map/pallas_call | solution.py:46
  62.9 6.8 %all_to_all.46.dkv_ref = bf16[4,64,128]{2,1,0:T(8,128)(2,1)S(1)} all-to-all(bf16[4,64,128]{2,1,0:T(8,128)(2,1)S(1)} %get-tuple-element.21), channel_id=1, replica_groups={{0,1,2,3},{4,5,6,7},{8,9,10,11},{12,13,14,15},{16,17,18,19},{20,21,22,2..., dimensions={0} | all-to-all | bytes 131072 | tf_op jit(solution)/shard_map/all_to_all | solution.py:215
  69.7 2.4 %shard_map.133 = bf16[16,128,256]{2,1,0:T(8,128)(2,1)S(1)} custom-call(bf16[128,256]{1,0:T(8,128)(2,1)S(1)} %get-tuple-element.20.dq_ref, bf16[4,64,128]{2,1,0:T(8,128)(2,1)S(1)} %all_to_all.46.dkv_ref, bf16[4096,256]{1,0:T(8,128)(2,1)S(1)} %bitcast.49, bf16[64,4096]{1,0:T(8,128)(2,1)S(1)} %pad_maximum_fusion.wkv_ref, ...), custom_call_target="tpu_custom_call" | custom-call | tf_op jit(solution)/shard_map/pallas_call | solution.py:46
  72.2 1.0 copy-done.3
  73.2 4.5 %all-to-all-start.4 = ((bf16[16,128,256]{2,1,0:T(8,128)(2,1)}), bf16[16,128,256]{2,1,0:T(8,128)(2,1)}, u32[]{:S(2)}, u32[]{:S(2)}) async-start(bf16[16,128,256]{2,1,0:T(8,128)(2,1)} %copy-done.3), calls=%async_computation.4 | async-start | bytes 2097152 | tf_op jit(solution)/shard_map/all_to_all | solution.py:258
  77.7 0.1 select_reduce_fusion.2
  77.8 0.1 select_reduce_fusion.1
  77.9 0.2 select_reduce_fusion
  78.2 0.1 copy.36.sin_ref
  78.4 0.1 multiply_convert_fusion
  78.5 11.8 %all-to-all-done.4 = bf16[16,128,256]{2,1,0:T(8,128)(2,1)} async-done(((bf16[16,128,256]{2,1,0:T(8,128)(2,1)}), bf16[16,128,256]{2,1,0:T(8,128)(2,1)}, u32[]{:S(2)}, u32[]{:S(2)}) %all-to-all-start.4) | async-done | bytes 1048608 | tf_op jit(solution)/shard_map/all_to_all | solution.py:258
  90.2 1.4 convert_reduce_fusion.1
  91.6 10.0 %collective-permute-start = (bf16[128,256]{1,0:T(8,128)(2,1)S(1)}, bf16[128,256]{1,0:T(8,128)(2,1)S(1)}, u32[]{:S(2)}, u32[]{:S(2)}) collective-permute-start(bf16[128,256]{1,0:T(8,128)(2,1)S(1)} %add_convert_fusion.1), channel_id=1, source_target_pairs={{16,0},{32,16},{48,32},{64,48},{80,64},{96,80},{112,96},{128,112},... | collective-permute-start | bytes 196616 | tf_op jit(solution)/shard_map/ppermute | solution.py:146
  101.7 19.1 %all-gather.3.cloned.1.call-done = bf16[16,1,128,256]{3,2,1,0:T(8,128)(2,1)} async-done(((bf16[1,1,128,256]{3,2,1,0:T(8,128)(2,1)}), bf16[16,1,128,256]{3,2,1,0:T(8,128)(2,1)}) %all-gather.3.cloned.1.call-update) | async-done | bytes 1048592 | tf_op jit(solution)/shard_map/all_gather | solution.py:217
  120.8 1.2 copy-done.4
  122.0 1.6 shard_map.134
  123.6 3.4 %all-to-all-start.6 = ((bf16[4,64,128]{2,1,0:T(8,128)(2,1)}), bf16[4,64,128]{2,1,0:T(8,128)(2,1)S(1)}, u32[]{:S(2)}, u32[]{:S(2)}) async-start(bf16[4,64,128]{2,1,0:T(8,128)(2,1)} %get-tuple-element.25), calls=%async_computation.6 | async-start | bytes 131072 | tf_op jit(solution)/shard_map/all_to_all | solution.py:215
  127.1 4.5 %all-to-all-done.6.kv_ref = bf16[4,64,128]{2,1,0:T(8,128)(2,1)S(1)} async-done(((bf16[4,64,128]{2,1,0:T(8,128)(2,1)}), bf16[4,64,128]{2,1,0:T(8,128)(2,1)S(1)}, u32[]{:S(2)}, u32[]{:S(2)}) %all-to-all-start.6) | async-done | bytes 65568 | tf_op jit(solution)/shard_map/all_to_all | solution.py:215
  131.5 1.1 broadcast_in_dim.61
  132.6 4.3 %all-to-all-start.5 = ((bf16[16,128,256]{2,1,0:T(8,128)(2,1)}), bf16[16,128,256]{2,1,0:T(8,128)(2,1)}, u32[]{:S(2)}, u32[]{:S(2)}) async-start(bf16[16,128,256]{2,1,0:T(8,128)(2,1)} %broadcast_in_dim.61), calls=%async_computation.5 | async-start | bytes 2097152 | tf_op jit(solution)/shard_map/all_to_all | solution.py:210
  137.1 11.7 %all-to-all-done.5.dy_ref = bf16[16,128,256]{2,1,0:T(8,128)(2,1)} async-done(((bf16[16,128,256]{2,1,0:T(8,128)(2,1)}), bf16[16,128,256]{2,1,0:T(8,128)(2,1)}, u32[]{:S(2)}, u32[]{:S(2)}) %all-to-all-start.5) | async-done | bytes 1048608 | tf_op jit(solution)/shard_map/all_to_all | solution.py:210
  148.8 1.6 copy-done.2
  150.4 3.1 %shard_map.135 = (bf16[128,256]{1,0:T(8,128)(2,1)S(1)}, bf16[4,64,128]{2,1,0:T(8,128)(2,1)S(1)}, f32[128,1]{1,0:T(8,128)S(1)}) custom-call(bf16[16,128,256]{2,1,0:T(8,128)(2,1)} %all-to-all-done.5.dy_ref, bf16[256,4096]{1,0:T(8,128)(2,1)S(1)} %bitcast.53, bf16[128,256]{1,0:T(8,128)(2,1)S(1)} %get-tuple-element.24.q_ref, ...), custom_call_target="tpu_custom_call" | custom-call | tf_op jit(solution)/shard_map/pallas_call | solution.py:46
  153.5 8.1 %all_to_all.47.dkv_ref = bf16[4,64,128]{2,1,0:T(8,128)(2,1)S(1)} all-to-all(bf16[4,64,128]{2,1,0:T(8,128)(2,1)S(1)} %get-tuple-element.27), channel_id=1, replica_groups={{0,1,2,3},{4,5,6,7},{8,9,10,11},{12,13,14,15},{16,17,18,19},{20,21,22,2..., dimensions={0} | all-to-all | bytes 131072 | tf_op jit(solution)/shard_map/all_to_all | solution.py:215
  161.6 1.2 shard_map.136
  162.8 16.8 %all_to_all.48 = bf16[16,128,256]{2,1,0:T(8,128)(2,1)S(1)} all-to-all(bf16[16,128,256]{2,1,0:T(8,128)(2,1)S(1)} %shard_map.136), channel_id=1, replica_groups=mesh['pipe'=32,'tp'=16] {'tp'}, dimensions={0} | all-to-all | bytes 2097152 | tf_op jit(solution)/shard_map/all_to_all | solution.py:258
  179.6 0.1 convert_reduce_fusion
  179.8 8.2 %collective-permute-start.1 = (bf16[128,256]{1,0:T(8,128)(2,1)S(1)}, bf16[128,256]{1,0:T(8,128)(2,1)S(1)}, u32[]{:S(2)}, u32[]{:S(2)}) collective-permute-start(bf16[128,256]{1,0:T(8,128)(2,1)S(1)} %add_convert_fusion), channel_id=1, source_target_pairs={{16,0},{32,16},{48,32},{64,48},{80,64},{96,80},{112,96},{128,112},... | collective-permute-start | bytes 196616 | tf_op jit(solution)/shard_map/ppermute | solution.py:146
  188.0 0.7 maximum_bitcast_fusion
  188.7 2.4 %collective-permute-done.1 = bf16[128,256]{1,0:T(8,128)(2,1)S(1)} collective-permute-done((bf16[128,256]{1,0:T(8,128)(2,1)S(1)}, bf16[128,256]{1,0:T(8,128)(2,1)S(1)}, u32[]{:S(2)}, u32[]{:S(2)}) %collective-permute-start.1) | collective-permute-done | bytes 65568 | tf_op jit(solution)/shard_map/ppermute | solution.py:146
  191.1 0.6 fusion.3
  (46 shorter events, 0.7 us)
Async XLA Ops:
  7.2 10.4 %copy-start.12 = (s32[1,2,4]{2,1,0:T(2,128)S(1)}, s32[1,2,4]{2,1,0:T(2,128)}, u32[]{:S(2)}) copy-start(s32[1,2,4]{2,1,0:T(2,128)} %param.19) | copy-start | bytes 100
  7.2 11.9 %copy-start.8 = (bf16[1,4096,32]{1,2,0:T(8,128)(2,1)S(1)}, bf16[1,4096,32]{1,2,0:T(8,128)(2,1)}, u32[]{:S(2)}) copy-start(bf16[1,4096,32]{1,2,0:T(8,128)(2,1)} %param.17) | copy-start | bytes 786436
  9.8 19.6 %copy-start = (bf16[1,4096,256]{2,1,0:T(8,128)(2,1)S(1)}, bf16[1,4096,256]{2,1,0:T(8,128)(2,1)}, u32[]{:S(2)}) copy-start(bf16[1,4096,256]{2,1,0:T(8,128)(2,1)} %param.15) | copy-start | bytes 6291460
  9.8 19.6 %copy-start.6 = (bf16[1,4096]{1,0:T(2,128)(2,1)S(1)}, bf16[1,4096]{1,0:T(2,128)(2,1)}, u32[]{:S(2)}) copy-start(bf16[1,4096]{1,0:T(2,128)(2,1)} %gain_ref.7) | copy-start | bytes 24580
  9.8 19.6 %all-to-all-start = ((bf16[16,128,256]{2,1,0:T(8,128)(2,1)}), bf16[16,128,256]{2,1,0:T(8,128)(2,1)}, u32[]{:S(2)}, u32[]{:S(2)}) async-start(bf16[16,128,256]{2,1,0:T(8,128)(2,1)} %broadcast_in_dim.53), calls=%async_computation | async-start | bytes 2097152 | tf_op jit(solution)/shard_map/all_to_all | solution.py:210
  20.1 19.8 %copy-start.7 = (bf16[1,128,256]{2,1,0:T(8,128)(2,1)S(1)}, bf16[1,128,256]{2,1,0:T(8,128)(2,1)}, u32[]{:S(2)}) copy-start(bf16[1,128,256]{2,1,0:T(8,128)(2,1)} %param.13) | copy-start | bytes 196612
  40.9 17.4 %all-to-all-start.1 = ((bf16[16,128,256]{2,1,0:T(8,128)(2,1)}), bf16[16,128,256]{2,1,0:T(8,128)(2,1)}, u32[]{:S(2)}, u32[]{:S(2)}) async-start(bf16[16,128,256]{2,1,0:T(8,128)(2,1)} %broadcast_in_dim.54), calls=%async_computation.1 | async-start | bytes 2097152 | tf_op jit(solution)/shard_map/all_to_all | solution.py:210
  46.4 74.4 %all-gather.3.cloned.1.call-start = ((), (), s32[]{:S(2)}) async-start(), calls=%async_computation.9 | async-start | bytes 1114112 | tf_op jit(solution)/shard_map/all_gather | solution.py:217
  58.3 1.6 copy-start.1
  72.2 1.0 copy-start.3
  73.2 4.5 %copy-start.10 = (f32[512]{0:T(512)S(1)}, f32[512]{0:T(512)}, u32[]{:S(2)}) copy-start(f32[512]{0:T(512)} %param.21) | copy-start | bytes 6148
  73.2 4.5 %copy-start.11 = (s32[512]{0:T(512)S(1)}, s32[512]{0:T(512)}, u32[]{:S(2)}) copy-start(s32[512]{0:T(512)} %param.22) | copy-start | bytes 6148
  73.2 4.7 %copy-start.13 = (s32[2,128]{1,0:T(2,128)S(1)}, s32[2,128]{1,0:T(2,128)}, u32[]{:S(2)}) copy-start(s32[2,128]{1,0:T(2,128)} %param.23) | copy-start | bytes 3076
  73.2 5.2 %copy-start.9 = (bf16[2,128,256]{2,1,0:T(8,128)(2,1)S(1)}, bf16[2,128,256]{2,1,0:T(8,128)(2,1)}, u32[]{:S(2)}) copy-start(bf16[2,128,256]{2,1,0:T(8,128)(2,1)} %param.20) | copy-start | bytes 393220
  73.2 17.1 %all-to-all-start.4 = ((bf16[16,128,256]{2,1,0:T(8,128)(2,1)}), bf16[16,128,256]{2,1,0:T(8,128)(2,1)}, u32[]{:S(2)}, u32[]{:S(2)}) async-start(bf16[16,128,256]{2,1,0:T(8,128)(2,1)} %copy-done.3), calls=%async_computation.4 | async-start | bytes 2097152 | tf_op jit(solution)/shard_map/all_to_all | solution.py:258
  91.6 35.4 %collective-permute-start = (bf16[128,256]{1,0:T(8,128)(2,1)S(1)}, bf16[128,256]{1,0:T(8,128)(2,1)S(1)}, u32[]{:S(2)}, u32[]{:S(2)}) collective-permute-start(bf16[128,256]{1,0:T(8,128)(2,1)S(1)} %add_convert_fusion.1), channel_id=1, source_target_pairs={{16,0},{32,16},{48,32},{64,48},{80,64},{96,80},{112,96},{128,112},... | collective-permute-start | bytes 196616 | tf_op jit(solution)/shard_map/ppermute | solution.py:146
  120.8 1.2 copy-start.4
  123.6 7.9 %all-to-all-start.6 = ((bf16[4,64,128]{2,1,0:T(8,128)(2,1)}), bf16[4,64,128]{2,1,0:T(8,128)(2,1)S(1)}, u32[]{:S(2)}, u32[]{:S(2)}) async-start(bf16[4,64,128]{2,1,0:T(8,128)(2,1)} %get-tuple-element.25), calls=%async_computation.6 | async-start | bytes 131072 | tf_op jit(solution)/shard_map/all_to_all | solution.py:215
  132.6 16.2 %all-to-all-start.5 = ((bf16[16,128,256]{2,1,0:T(8,128)(2,1)}), bf16[16,128,256]{2,1,0:T(8,128)(2,1)}, u32[]{:S(2)}, u32[]{:S(2)}) async-start(bf16[16,128,256]{2,1,0:T(8,128)(2,1)} %broadcast_in_dim.61), calls=%async_computation.5 | async-start | bytes 2097152 | tf_op jit(solution)/shard_map/all_to_all | solution.py:210
  148.8 1.6 copy-start.2
  150.4 11.2 %copy-start.5 = (bf16[16,1,128,256]{3,2,1,0:T(8,128)(2,1)S(1)}, bf16[16,1,128,256]{3,2,1,0:T(8,128)(2,1)}, u32[]{:S(2)}) copy-start(bf16[16,1,128,256]{3,2,1,0:T(8,128)(2,1)} %all-gather.3.cloned.1.call-done) | copy-start | bytes 3145732
  179.8 11.3 %collective-permute-start.1 = (bf16[128,256]{1,0:T(8,128)(2,1)S(1)}, bf16[128,256]{1,0:T(8,128)(2,1)S(1)}, u32[]{:S(2)}, u32[]{:S(2)}) collective-permute-start(bf16[128,256]{1,0:T(8,128)(2,1)S(1)} %add_convert_fusion), channel_id=1, source_target_pairs={{16,0},{32,16},{48,32},{64,48},{80,64},{96,80},{112,96},{128,112},... | collective-permute-start | bytes 196616 | tf_op jit(solution)/shard_map/ppermute | solution.py:146
Sparse Core Ops, SparseCore 0:
  50.8 69.9 all-gather.2

commit v2 on v1

--- a/solution.py
+++ b/solution.py
@@ -20,7 +20,7 @@
 SCALE = 1.0 / math.sqrt(HD)
 F32 = jnp.float32
 BF16 = jnp.bfloat16
-VMEM_LIMIT = 48 * 1024 * 1024
+VMEM_LIMIT = 12 * 1024 * 1024
 
 
 def nn(a, b):
@@ -41,19 +41,34 @@
     return jnp.where(even, pltpu.roll(v, n - 1, axis), pltpu.roll(v, 1, axis))
 
 
-def kernel_call(body, outs, *args):
+def kernel_call(body, outs, specs, args):
     vmem = pl.BlockSpec(memory_space=pltpu.VMEM)
+    kinds = {
+        "v": vmem,
+        "s": pl.BlockSpec(memory_space=pltpu.SMEM),
+    }
     return pl.pallas_call(
         body,
         out_shape=outs,
-        in_specs=[vmem] * len(args),
+        in_specs=[kinds[kind] for kind in specs],
         out_specs=[vmem] * len(outs),
         compiler_params=pltpu.CompilerParams(vmem_limit_bytes=VMEM_LIMIT),
     )(*args)
 
 
 def forward_body(
-    x_ref, gain_ref, wq_ref, wkv_ref, cos_ref, sin_ref, cost_ref, sint_ref, q_ref, kv_ref, inv_ref
+    x_ref,
+    wq_ref,
+    wk_ref,
+    wv_ref,
+    gain_ref,
+    cos_ref,
+    sin_ref,
+    cost_ref,
+    sint_ref,
+    q_ref,
+    kv_ref,
+    inv_ref,
 ):
     blocks, rows, width = x_ref.shape
     squares = jnp.zeros((rows, width), F32)
@@ -63,37 +78,58 @@
     inverse = lax.rsqrt(jnp.sum(squares, axis=1, keepdims=True) * (1.0 / D) + EPS)
     inv_ref[...] = inverse
     query = jnp.zeros(q_ref.shape, F32)
-    kvt = jnp.zeros(kv_ref.shape[1:], F32)
+    half = wk_ref.shape[0]
+    keys = jnp.zeros((half, rows), F32)
+    values = jnp.zeros((half, rows), F32)
     for j in range(blocks):
         part = slice(j * width, (j + 1) * width)
         normed = (x_ref[j].astype(F32) * inverse * gain_ref[:, part].astype(F32)).astype(BF16)
         query = query + nn(normed, wq_ref[part, :])
-        kvt = kvt + nt(wkv_ref[:, part], normed)
+        keys = keys + nt(wk_ref[:, part], normed)
+        values = values + nt(wv_ref[:, part], normed)
     for h in range(query.shape[1] // HD):
         cols = slice(h * HD, (h + 1) * HD)
         head = query[:, cols]
         q_ref[:, cols] = (head * cos_ref[...] + pair_swap(head, 1) * sin_ref[...]).astype(BF16)
-    half = kvt.shape[0] // 2
-    keys = kvt[:half]
     keys = keys * cost_ref[...] + pair_swap(keys, 0) * sint_ref[...]
-    both = jnp.concatenate([keys, kvt[half:]], axis=0).astype(BF16)
-    for i in range(kv_ref.shape[0]):
-        kv_ref[i] = both
+    kv_ref[...] = jnp.concatenate([keys, values], axis=1).astype(BF16)
+
+
+def pack_body(grad_ref, kv_ref, out_ref):
+    rows = grad_ref.shape[0]
+    for i in range(out_ref.shape[0]):
+        out_ref[i, :rows] = grad_ref[...]
+        out_ref[i, rows:] = kv_ref[...]
 
 
 def attention_body(
-    dy_ref, wo_ref, q_ref, kv_ref, mask_ref, cos_ref, sin_ref, dq_ref, dkv_ref, t_ref
+    place_ref,
+    got_ref,
+    wo_ref,
+    q_ref,
+    mask_ref,
+    cos_ref,
+    sin_ref,
+    dq_ref,
+    dkv_ref,
+    t_ref,
 ):
-    blocks, rows, width = dy_ref.shape
+    blocks, _, width = got_ref.shape
+    rows = q_ref.shape[0]
+    shares, half = dkv_ref.shape[0], dkv_ref.shape[1] // 2
+    kv = [got_ref[place_ref[0] + i, rows:] for i in range(shares)]
+    keys = jnp.concatenate([part[:, :rows] for part in kv], axis=0)
+    values = jnp.concatenate([part[:, rows:] for part in kv], axis=0)
+    allowed = mask_ref[...] > 0.0
+    soft = []
+    for h in range(dq_ref.shape[1] // HD):
+        query = q_ref[:, h * HD : (h + 1) * HD]
+        weights = jnp.where(allowed, jnp.exp(nn(query, keys) * SCALE), 0.0)
+        soft.append(weights / jnp.sum(weights, axis=1, keepdims=True))
     dout = jnp.zeros(dq_ref.shape, F32)
     for j in range(blocks):
-        dout = dout + nt(dy_ref[j], wo_ref[:, j * width : (j + 1) * width])
+        dout = dout + nt(got_ref[j, :rows], wo_ref[:, j * width : (j + 1) * width])
     dout = dout.astype(BF16)
-    shares, both, _ = kv_ref.shape
-    half = both // 2
-    keys = jnp.concatenate([kv_ref[i, :half] for i in range(shares)], axis=0)
-    values = jnp.concatenate([kv_ref[i, half:] for i in range(shares)], axis=0)
-    allowed = mask_ref[...] > 0.0
     dkeys = jnp.zeros((HD, rows), F32)
     dvalues = jnp.zeros((HD, rows), F32)
     own = jnp.zeros((rows, HD), F32)
@@ -101,8 +137,7 @@
         cols = slice(h * HD, (h + 1) * HD)
         query = q_ref[:, cols]
         dhead = dout[:, cols]
-        weights = jnp.where(allowed, jnp.exp(nn(query, keys) * SCALE), 0.0)
-        softmax = weights / jnp.sum(weights, axis=1, keepdims=True)
+        softmax = soft[h]
         dprobs = nn(dhead, values)
         delta = jnp.sum(softmax * dprobs, axis=1, keepdims=True)
         dscores = (softmax * (dprobs - delta) * SCALE).astype(BF16)
@@ -120,7 +155,18 @@
 
 
 def partial_body(
-    dq_ref, dkv_ref, wq_ref, wkv_ref, x_ref, gain_ref, inv_ref, t_ref, cost_ref, sint_ref, out_ref
+    x_ref,
+    dq_ref,
+    dkv_ref,
+    wq_ref,
+    wk_ref,
+    wv_ref,
+    gain_ref,
+    inv_ref,
+    t_ref,
+    cost_ref,
+    sint_ref,
+    out_ref,
 ):
     blocks, _, width = x_ref.shape
     dkv = dkv_ref[0].astype(F32)
@@ -128,14 +174,15 @@
         dkv = dkv + dkv_ref[i].astype(F32)
     half = dkv.shape[0] // 2
     dkeys = dkv[:half]
-    dkeys = dkeys * cost_ref[...] - pair_swap(dkeys, 0) * sint_ref[...]
-    dkv = jnp.concatenate([dkeys, dkv[half:]], axis=0).astype(BF16)
+    dkeys = (dkeys * cost_ref[...] - pair_swap(dkeys, 0) * sint_ref[...]).astype(BF16)
+    dvalues = dkv[half:].astype(BF16)
     dq = dq_ref[...]
     inverse = inv_ref[...]
     along = inverse * inverse * t_ref[...] * (1.0 / D)
     for j in range(blocks):
         part = slice(j * width, (j + 1) * width)
-        total = nt(dq, wq_ref[part, :]) + tn(dkv, wkv_ref[:, part])
+        total = nt(dq, wq_ref[part, :])
+        total = total + tn(dkeys, wk_ref[:, part]) + tn(dvalues, wv_ref[:, part])
         scaled = total * (inverse * gain_ref[:, part].astype(F32))
         out_ref[j] = (scaled - x_ref[j].astype(F32) * along).astype(BF16)
 
@@ -200,67 +247,76 @@
     last_section = lax.axis_index("pipe") == lax.axis_size("pipe") - 1
     share = tp_count // KV
     groups = [list(range(g * share, (g + 1) * share)) for g in range(KV)]
-    kv_share = w_key.shape[2]
-    kv_start = (tp_index % share) * kv_share
-    wq = w_query[0]
-    wkv = jnp.concatenate([w_key[0].T, w_value[0].T], axis=0)
-    wo = w_out[0]
-
-    def to_all(block):
-        return lax.all_to_all(
-            jnp.broadcast_to(block[None], (tp_count,) + block.shape), "tp", 0, 0
-        )
-
-    def in_group(blocks):
-        return lax.all_to_all(blocks, "tp", 0, 0, axis_index_groups=groups)
-
-    x_next = lax.all_gather(saved[0, 1], "tp", axis=0)
-    x_full = to_all(saved[0, 0])
-    grad, x_full = lax.optimization_barrier((incoming[0], x_full))
-    grad_full = to_all(grad)
-    head_rows = head_gradient(advantages(rewards, sample_group), head_sample, score_grad)
-
-    def forward(tick, rows_full):
+    wq, wk, wv, wo = w_query[0], w_key[0].T, w_value[0].T, w_out[0]
+    kv_share = wk.shape[0]
+    base = (tp_index // share * share).astype(jnp.int32)[None]
+    kv_start = tp_index % share * kv_share
+    full_shape = (tp_count, ROWS, saved.shape[3])
+
+    def tables_of(tick):
         positions, allowed = row_layout(seg_lengths[0, tick])
         cos, sin = rotation_tables(positions)
         cos_t = lax.dynamic_slice_in_dim(cos.T, kv_start, kv_share, 0)
         sin_t = lax.dynamic_slice_in_dim(sin.T, kv_start, kv_share, 0)
-        query, kv, inverse = kernel_call(
+        return allowed.astype(F32), cos, sin, cos_t, sin_t
+
+    def forward(rows_full, cos, sin, cos_t, sin_t):
+        return kernel_call(
             forward_body,
             (
                 jax.ShapeDtypeStruct((ROWS, wq.shape[1]), BF16),
-                jax.ShapeDtypeStruct((share, 2 * kv_share, ROWS), BF16),
+                jax.ShapeDtypeStruct((kv_share, 2 * ROWS), BF16),
                 jax.ShapeDtypeStruct((ROWS, 1), F32),
             ),
-            rows_full, gain, wq, wkv, cos, sin, cos_t, sin_t,
+            "v" * 9,
+            (rows_full, wq, wk, wv, gain, cos, sin, cos_t, sin_t),
         )
-        return query, in_group(kv), inverse, allowed.astype(F32), cos, sin, cos_t, sin_t
+
+    x_all = lax.all_gather(saved[0], "tp", axis=1)
+    x_first = lax.all_to_all(
+        jnp.broadcast_to(saved[0, 0][None], full_shape), "tp", 0, 0
+    )
+    head_rows = head_gradient(advantages(rewards, sample_group), head_sample, score_grad)
+    tables = [tables_of(tick) for tick in range(TICKS)]
+    x_first, head_rows, tables, base, last_section = lax.optimization_barrier(
+        (x_first, head_rows, tables, base, last_section)
+    )
+    grad = incoming[0]
 
     outputs = []
     for tick in range(TICKS):
-        rows_full = x_full if tick == 0 else x_next
-        query, kv, inverse, mask, cos, sin, cos_t, sin_t = forward(tick, rows_full)
+        rows_full = x_first if tick == 0 else x_all[tick]
+        mask, cos, sin, cos_t, sin_t = tables[tick]
+        query, kv, inverse = forward(rows_full, cos, sin, cos_t, sin_t)
+        (packed,) = kernel_call(
+            pack_body,
+            (jax.ShapeDtypeStruct((tp_count, ROWS + kv_share, grad.shape[1]), BF16),),
+            "vv",
+            (grad, kv),
+        )
+        got = lax.all_to_all(packed, "tp", 0, 0)
         dquery, dkv, along = kernel_call(
             attention_body,
             (
                 jax.ShapeDtypeStruct(query.shape, BF16),
-                jax.ShapeDtypeStruct(kv.shape, BF16),
+                jax.ShapeDtypeStruct((share, 2 * kv_share, ROWS), BF16),
                 jax.ShapeDtypeStruct((ROWS, 1), F32),
             ),
-            grad_full, wo, query, kv, mask, cos, sin,
+            "s" + "v" * 6,
+            (base, got, wo, query, mask, cos, sin),
         )
-        dkv = in_group(dkv)
+        dkv = lax.all_to_all(dkv, "tp", 0, 0, axis_index_groups=groups)
         (blocks,) = kernel_call(
             partial_body,
-            (jax.ShapeDtypeStruct(rows_full.shape, BF16),),
-            dquery, dkv, wq, wkv, rows_full, gain, inverse, along, cos_t, sin_t,
+            (jax.ShapeDtypeStruct(full_shape, BF16),),
+            "v" * 11,
+            (rows_full, dquery, dkv, wq, wk, wv, gain, inverse, along, cos_t, sin_t),
         )
         blocks = lax.all_to_all(blocks, "tp", 0, 0)
         result = (grad.astype(F32) + jnp.sum(blocks.astype(F32), axis=0)).astype(BF16)
+        grad = jnp.where(last_section, head_rows[tick], shifted(result, "pipe", -1))
+        result, grad = lax.optimization_barrier((result, grad))
         outputs.append(result)
-        grad = jnp.where(last_section, head_rows[tick], shifted(result, "pipe", -1))
-        if tick + 1 < TICKS:
-            grad_full = to_all(grad)
     return (jnp.stack(outputs, axis=0)[None], grad[None])
 
 

time: 200 us -> 168 us (0.84)
  waiting for transfers between devices: 70.5 us -> 9.24 us
  blocking collectives: 39.9 us -> 91.4 us
  starting transfers between devices: 43.8 us -> 20.6 us
  Pallas kernels: 13.6 us -> 8.91 us
  other arithmetic: 5.72 us -> 10.1 us
    all_to_all x5 -> x1, waiting for transfers between devices: 48.3 us -> 1.44 us  [per_device(): lax.all_to_all(jnp.broadcast_to(saved[0, 0][None], full_shape), 'tp', 0, 0)]
    all_to_all x3 -> x4, blocking collectives: 23.1 us -> 57.4 us  [the longest x2 42.9 us: per_device(): got = lax.all_to_all(packed, 'tp', 0, 0)]
    all_gather x1, waiting for transfers between devices: 19.1 us -> 0.02 us  [per_device(): x_all = lax.all_gather(saved[0], 'tp', axis=1)]
    all_to_all x5 -> x1, starting transfers between devices: 25.5 us -> 7.58 us  [per_device(): lax.all_to_all(jnp.broadcast_to(saved[0, 0][None], full_shape), 'tp', 0, 0)]
    all_to_all x1 -> x2, blocking collectives: 16.8 us -> 34.1 us  [per_device(): blocks = lax.all_to_all(blocks, 'tp', 0, 0)]
    ppermute x2, starting transfers between devices: 18.3 us -> 12.9 us  [shifted(): lax.ppermute(value, axis, [(source, source + steps) for source in range(f...]
    pallas_call x6 -> x8, Pallas kernels: 13.6 us -> 8.91 us  [kernel_call(): pl.pallas_call(body, out_shape=outs, in_specs=[kinds[kind] for kind in sp...]
    ppermute x2, waiting for transfers between devices: 2.42 us -> 7.1 us  [shifted(): lax.ppermute(value, axis, [(source, source + steps) for source in range(f...]
  transfers between devices with their start and end apart: 8 -> 4, of which waited for: 7 -> 3; matrix products, arithmetic and copies ran while one was open for 3% -> 10% of each run, Pallas kernels for 4% -> 3%
where the time goes in v2:
time: 168 us; the launch traced here: 167 us
  blocking collectives  91.4 us (54%)
  starting transfers between devices  20.6 us (12%)
  between operations  14.4 us (9%)
  local copies, waits for them, and re-layouts  12 us (7%)
  other arithmetic  10.1 us (6%)
  waiting for transfers between devices  9.24 us (6%)
  Pallas kernels  8.91 us (5%)
    all_to_all x2, blocking collectives, per_device(): got = lax.all_to_all(packed, 'tp', 0, 0)  42.9 us
    all_to_all x2, blocking collectives, per_device(): blocks = lax.all_to_all(blocks, 'tp', 0, 0)  34.1 us
    all_to_all x2, blocking collectives, per_device(): dkv = lax.all_to_all(dkv, 'tp', 0, 0, axis_index_groups=groups)  14.5 us
    ppermute x2, starting transfers between devices, shifted(): lax.ppermute(value, axis, [(source, source + steps) for source in range(f...  12.9 us
    pallas_call x8, Pallas kernels, kernel_call(): pl.pallas_call(body, out_shape=outs, in_specs=[kinds[kind] for kind in sp...  8.91 us
    all_to_all x1, starting transfers between devices, per_device(): lax.all_to_all(jnp.broadcast_to(saved[0, 0][None], full_shape), 'tp', 0, 0)  7.58 us
    ppermute x2, waiting for transfers between devices, shifted(): lax.ppermute(value, axis, [(source, source + steps) for source in range(f...  7.1 us
  transfers between devices with their start and end apart: 4, of which 3 were waited for; matrix products, arithmetic and copies ran while one was open for 10% of the time, Pallas kernels for 3%

profile of v2, /device:TPU:1, one launch (start us, length us, event | category | flops | bytes accessed | tf_op | source)
XLA Modules:
  0.0 166.7 jit_solution(8372131774179624445)
XLA Ops:
  7.2 0.7 all-gather.3.cloned.1.call-update
  7.9 0.8 slice_bitcast_fusion
  8.8 1.1 broadcast_in_dim.51
  9.9 7.6 %all-to-all-start = ((bf16[16,128,256]{2,1,0:T(8,128)(2,1)}), bf16[16,128,256]{2,1,0:T(8,128)(2,1)S(1)}, u32[]{:S(2)}, u32[]{:S(2)}) async-start(bf16[16,128,256]{2,1,0:T(8,128)(2,1)} %broadcast_in_dim.51), calls=%async_computation | async-start | bytes 2097152 | tf_op jit(solution)/shard_map/all_to_all | solution.py:276
  17.5 0.6 compare_select_fusion
  18.1 0.1 select_reduce_fusion.2
  18.2 0.1 select_reduce_fusion.1
  18.3 0.6 multiply_subtract_fusion
  18.9 0.2 reduce-window.14
  19.1 0.2 reduce-window.15
  19.5 0.1 copy-done.24
  19.6 0.3 copy-done.25
  19.9 1.9 %fusion.1 = (f32[128,128]{0,1:T(8,128)S(1)}, f32[128,128]{0,1:T(8,128)}, f32[128,128]{0,1:T(8,128)}, f32[128,128]{0,1:T(8,128)S(1)}) fusion(f32[128]{0:T(128)S(1)} %subtract_convert_fusion, f32[128]{0:T(128)} %get-tuple-element.70, f32[128]{0:T(128)} %get-tuple-element.71, f32[128]{0:T(128)S(1)} %subtract_convert_fusion.1), kind=kLoop, calls=%fused_computation.13 | loop fusion | flops 65536 | bytes 264192 | tf_op jit(solution)/shard_map/mul | solution.py:202
  21.8 0.9 select_reduce_fusion
  22.7 0.6 neg.8
  23.3 1.3 dynamic-slice_bitcast_fusion.3.cost_ref
  24.6 1.3 dynamic-slice_bitcast_fusion.2.sint_ref
  26.0 0.6 dynamic-slice_bitcast_fusion.1.cost_ref
  26.6 0.6 dynamic-slice_bitcast_fusion.sint_ref
  27.2 1.4 fusion.4
  28.6 1.7 multiply_convert_fusion
  30.3 1.4 all-to-all-done.x_ref
  31.7 0.9 copy.22.cos_ref
  32.6 0.9 copy.23.sin_ref
  33.6 0.9 copy-done.4
  34.6 0.7 copy-done.13
  35.3 0.7 copy-done.15
  36.0 1.3 shard_map.131
  37.5 21.3 %all_to_all.35.got_ref = bf16[16,160,256]{2,1,0:T(8,128)(2,1)S(1)} all-to-all(bf16[16,160,256]{2,1,0:T(8,128)(2,1)S(1)} %shard_map.132), channel_id=1, replica_groups=mesh['pipe'=32,'tp'=16] {'tp'}, dimensions={0} | all-to-all | bytes 2621440 | tf_op jit(solution)/shard_map/all_to_all | solution.py:297
  58.8 1.6 shard_map.133
  60.3 7.4 %all_to_all.36.dkv_ref = bf16[4,64,128]{2,1,0:T(8,128)(2,1)S(1)} all-to-all(bf16[4,64,128]{2,1,0:T(8,128)(2,1)S(1)} %get-tuple-element.42), channel_id=1, replica_groups={{0,1,2,3},{4,5,6,7},{8,9,10,11},{12,13,14,15},{16,17,18,19},{20,21,22,2..., dimensions={0} | all-to-all | bytes 131072 | tf_op jit(solution)/shard_map/all_to_all | solution.py:308
  67.8 1.5 shard_map.134
  69.3 15.0 %all_to_all.37 = bf16[16,128,256]{2,1,0:T(8,128)(2,1)S(1)} all-to-all(bf16[16,128,256]{2,1,0:T(8,128)(2,1)S(1)} %shard_map.134), channel_id=1, replica_groups=mesh['pipe'=32,'tp'=16] {'tp'}, dimensions={0} | all-to-all | bytes 2097152 | tf_op jit(solution)/shard_map/all_to_all | solution.py:315
  84.3 0.1 convert_reduce_fusion.1
  84.4 9.1 %collective-permute-start = (bf16[128,256]{1,0:T(8,128)(2,1)S(1)}, bf16[128,256]{1,0:T(8,128)(2,1)S(1)}, u32[]{:S(2)}, u32[]{:S(2)}) collective-permute-start(bf16[128,256]{1,0:T(8,128)(2,1)S(1)} %add_convert_fusion.1), channel_id=1, source_target_pairs={{16,0},{32,16},{48,32},{64,48},{80,64},{96,80},{112,96},{128,112},... | collective-permute-start | bytes 196616 | tf_op jit(solution)/shard_map/ppermute | solution.py:193
  93.8 3.2 %collective-permute-done = bf16[128,256]{1,0:T(8,128)(2,1)S(1)} collective-permute-done((bf16[128,256]{1,0:T(8,128)(2,1)S(1)}, bf16[128,256]{1,0:T(8,128)(2,1)S(1)}, u32[]{:S(2)}, u32[]{:S(2)}) %collective-permute-start) | collective-permute-done | bytes 65568 | tf_op jit(solution)/shard_map/ppermute | solution.py:193
  97.1 1.3 slice.25
  98.4 1.3 shard_map.135
  99.9 21.6 %all_to_all.38.got_ref = bf16[16,160,256]{2,1,0:T(8,128)(2,1)S(1)} all-to-all(bf16[16,160,256]{2,1,0:T(8,128)(2,1)S(1)} %shard_map.136), channel_id=1, replica_groups=mesh['pipe'=32,'tp'=16] {'tp'}, dimensions={0} | all-to-all | bytes 2621440 | tf_op jit(solution)/shard_map/all_to_all | solution.py:297
  121.5 1.6 shard_map.137
  123.0 7.0 %all_to_all.39.dkv_ref = bf16[4,64,128]{2,1,0:T(8,128)(2,1)S(1)} all-to-all(bf16[4,64,128]{2,1,0:T(8,128)(2,1)S(1)} %get-tuple-element.57), channel_id=1, replica_groups={{0,1,2,3},{4,5,6,7},{8,9,10,11},{12,13,14,15},{16,17,18,19},{20,21,22,2..., dimensions={0} | all-to-all | bytes 131072 | tf_op jit(solution)/shard_map/all_to_all | solution.py:308
  130.1 1.5 shard_map.138
  131.6 19.1 %all_to_all.40 = bf16[16,128,256]{2,1,0:T(8,128)(2,1)S(1)} all-to-all(bf16[16,128,256]{2,1,0:T(8,128)(2,1)S(1)} %shard_map.138), channel_id=1, replica_groups=mesh['pipe'=32,'tp'=16] {'tp'}, dimensions={0} | all-to-all | bytes 2097152 | tf_op jit(solution)/shard_map/all_to_all | solution.py:315
  150.7 0.1 convert_reduce_fusion
  150.9 3.8 %collective-permute-start.1 = (bf16[128,256]{1,0:T(8,128)(2,1)S(1)}, bf16[128,256]{1,0:T(8,128)(2,1)S(1)}, u32[]{:S(2)}, u32[]{:S(2)}) collective-permute-start(bf16[128,256]{1,0:T(8,128)(2,1)S(1)} %add_convert_fusion), channel_id=1, source_target_pairs={{16,0},{32,16},{48,32},{64,48},{80,64},{96,80},{112,96},{128,112},... | collective-permute-start | bytes 196616 | tf_op jit(solution)/shard_map/ppermute | solution.py:193
  154.7 3.9 %collective-permute-done.1 = bf16[128,256]{1,0:T(8,128)(2,1)S(1)} collective-permute-done((bf16[128,256]{1,0:T(8,128)(2,1)S(1)}, bf16[128,256]{1,0:T(8,128)(2,1)S(1)}, u32[]{:S(2)}, u32[]{:S(2)}) %collective-permute-start.1) | collective-permute-done | bytes 65568 | tf_op jit(solution)/shard_map/ppermute | solution.py:193
  158.5 0.6 bitcast_select_fusion
  159.2 0.7 maximum_bitcast_fusion
  (65 shorter events, 0.8 us)
Async XLA Ops:
  7.2 10.9 %copy-start.22 = (f32[512]{0:T(512)S(1)}, f32[512]{0:T(512)}, u32[]{:S(2)}) copy-start(f32[512]{0:T(512)} %param.21) | copy-start | bytes 6148
  7.2 10.9 %copy-start.23 = (s32[512]{0:T(512)S(1)}, s32[512]{0:T(512)}, u32[]{:S(2)}) copy-start(s32[512]{0:T(512)} %param.22) | copy-start | bytes 6148
  7.2 11.7 %copy-start.26 = (s32[1,2,4]{2,1,0:T(2,128)S(1)}, s32[1,2,4]{2,1,0:T(2,128)}, u32[]{:S(2)}) copy-start(s32[1,2,4]{2,1,0:T(2,128)} %param.19) | copy-start | bytes 100
  7.2 89.9 %all-gather.3.cloned.1.call-start = ((), (), s32[]{:S(2)}) async-start(), calls=%async_computation.7 | async-start | bytes 2228224 | tf_op jit(solution)/shard_map/all_gather | solution.py:275
  8.8 24.8 %copy-start = (bf16[1,4096,256]{2,1,0:T(8,128)(2,1)S(1)}, bf16[1,4096,256]{2,1,0:T(8,128)(2,1)}, u32[]{:S(2)}) copy-start(bf16[1,4096,256]{2,1,0:T(8,128)(2,1)} %param.15) | copy-start | bytes 6291460
  8.8 24.8 %copy-start.3 = (bf16[1,4096,32]{1,2,0:T(8,128)(2,1)S(1)}, bf16[1,4096,32]{1,2,0:T(8,128)(2,1)}, u32[]{:S(2)}) copy-start(bf16[1,4096,32]{1,2,0:T(8,128)(2,1)} %param.16) | copy-start | bytes 786436
  8.8 24.8 %copy-start.7 = (bf16[1,4096]{1,0:T(2,128)(2,1)S(1)}, bf16[1,4096]{1,0:T(2,128)(2,1)}, u32[]{:S(2)}) copy-start(bf16[1,4096]{1,0:T(2,128)(2,1)} %gain_ref.7) | copy-start | bytes 24580
  9.9 21.8 %all-to-all-start = ((bf16[16,128,256]{2,1,0:T(8,128)(2,1)}), bf16[16,128,256]{2,1,0:T(8,128)(2,1)S(1)}, u32[]{:S(2)}, u32[]{:S(2)}) async-start(bf16[16,128,256]{2,1,0:T(8,128)(2,1)} %broadcast_in_dim.51), calls=%async_computation | async-start | bytes 2097152 | tf_op jit(solution)/shard_map/all_to_all | solution.py:276
  19.1 0.5 copy-start.24
  19.4 0.5 copy-start.25
  21.8 9.9 %copy-start.18 = (f32[128,128]{0,1:T(8,128)}, f32[128,128]{0,1:T(8,128)S(1)}, u32[]{:S(2)}) copy-start(f32[128,128]{0,1:T(8,128)S(1)} %get-tuple-element.50) | copy-start | bytes 196612
  21.8 9.9 %copy-start.20 = (f32[128,128]{0,1:T(8,128)}, f32[128,128]{0,1:T(8,128)S(1)}, u32[]{:S(2)}) copy-start(f32[128,128]{0,1:T(8,128)S(1)} %get-tuple-element.49) | copy-start | bytes 196612
  33.6 1.0 copy-start.4
  34.6 0.7 copy-start.13
  35.3 0.7 copy-start.15
  36.0 1.4 copy-start.10
  37.3 21.4 %copy-start.1 = (bf16[1,256,4096]{2,1,0:T(8,128)(2,1)S(1)}, bf16[1,256,4096]{2,1,0:T(8,128)(2,1)}, u32[]{:S(2)}) copy-start(bf16[1,256,4096]{2,1,0:T(8,128)(2,1)} %param.18) | copy-start | bytes 6291460
  37.4 21.4 %copy-start.9 = (f32[128,128]{1,0:T(8,128)S(1)}, f32[128,128]{1,0:T(8,128)}, u32[]{:S(2)}) copy-start(f32[128,128]{1,0:T(8,128)} %get-tuple-element.40.mask_ref) | copy-start | bytes 196612
  58.7 9.0 %copy-start.5 = (bf16[1,4096,32]{1,2,0:T(8,128)(2,1)S(1)}, bf16[1,4096,32]{1,2,0:T(8,128)(2,1)}, u32[]{:S(2)}) copy-start(bf16[1,4096,32]{1,2,0:T(8,128)(2,1)} %param.17) | copy-start | bytes 786436
  58.7 9.0 %copy-start.14 = (f32[32,128]{1,0:T(8,128)S(1)}, f32[32,128]{1,0:T(8,128)}, u32[]{:S(2)}) copy-start(f32[32,128]{1,0:T(8,128)} %dynamic-slice_bitcast_fusion.3.cost_ref) | copy-start | bytes 49156
  58.8 9.0 %copy-start.16 = (f32[32,128]{1,0:T(8,128)S(1)}, f32[32,128]{1,0:T(8,128)}, u32[]{:S(2)}) copy-start(f32[32,128]{1,0:T(8,128)} %dynamic-slice_bitcast_fusion.2.sint_ref) | copy-start | bytes 49156
  69.3 24.3 %copy-start.21 = (f32[128,128]{0,1:T(8,128)S(1)}, f32[128,128]{0,1:T(8,128)}, u32[]{:S(2)}) copy-start(f32[128,128]{0,1:T(8,128)} %copy-done.20) | copy-start | bytes 196612
  69.3 24.4 %copy-start.19 = (f32[128,128]{0,1:T(8,128)S(1)}, f32[128,128]{0,1:T(8,128)}, u32[]{:S(2)}) copy-start(f32[128,128]{0,1:T(8,128)} %copy-done.18) | copy-start | bytes 196612
  69.3 27.8 %copy-start.17 = (bf16[2,128,256]{2,1,0:T(8,128)(2,1)S(1)}, bf16[2,128,256]{2,1,0:T(8,128)(2,1)}, u32[]{:S(2)}) copy-start(bf16[2,128,256]{2,1,0:T(8,128)(2,1)} %multiply_convert_fusion) | copy-start | bytes 393220
  84.3 14.1 %copy-start.6 = (bf16[1,4096,32]{1,2,0:T(8,128)(2,1)S(1)}, bf16[1,4096,32]{1,2,0:T(8,128)(2,1)}, u32[]{:S(2)}) copy-start(bf16[1,4096,32]{1,2,0:T(8,128)(2,1)} %param.17) | copy-start | bytes 786436
  84.3 14.1 %copy-start.11 = (f32[32,128]{1,0:T(8,128)S(1)}, f32[32,128]{1,0:T(8,128)}, u32[]{:S(2)}) copy-start(f32[32,128]{1,0:T(8,128)} %dynamic-slice_bitcast_fusion.1.cost_ref) | copy-start | bytes 49156
  84.3 14.1 %copy-start.12 = (f32[32,128]{1,0:T(8,128)S(1)}, f32[32,128]{1,0:T(8,128)}, u32[]{:S(2)}) copy-start(f32[32,128]{1,0:T(8,128)} %dynamic-slice_bitcast_fusion.sint_ref) | copy-start | bytes 49156
  84.4 12.6 %collective-permute-start = (bf16[128,256]{1,0:T(8,128)(2,1)S(1)}, bf16[128,256]{1,0:T(8,128)(2,1)S(1)}, u32[]{:S(2)}, u32[]{:S(2)}) collective-permute-start(bf16[128,256]{1,0:T(8,128)(2,1)S(1)} %add_convert_fusion.1), channel_id=1, source_target_pairs={{16,0},{32,16},{48,32},{64,48},{80,64},{96,80},{112,96},{128,112},... | collective-permute-start | bytes 196616 | tf_op jit(solution)/shard_map/ppermute | solution.py:193
  99.7 21.7 %copy-start.2 = (bf16[1,256,4096]{2,1,0:T(8,128)(2,1)S(1)}, bf16[1,256,4096]{2,1,0:T(8,128)(2,1)}, u32[]{:S(2)}) copy-start(bf16[1,256,4096]{2,1,0:T(8,128)(2,1)} %param.18) | copy-start | bytes 6291460
  99.8 21.7 %copy-start.8 = (f32[128,128]{1,0:T(8,128)S(1)}, f32[128,128]{1,0:T(8,128)}, u32[]{:S(2)}) copy-start(f32[128,128]{1,0:T(8,128)} %get-tuple-element.55.mask_ref) | copy-start | bytes 196612
  150.9 7.7 %collective-permute-start.1 = (bf16[128,256]{1,0:T(8,128)(2,1)S(1)}, bf16[128,256]{1,0:T(8,128)(2,1)S(1)}, u32[]{:S(2)}, u32[]{:S(2)}) collective-permute-start(bf16[128,256]{1,0:T(8,128)(2,1)S(1)} %add_convert_fusion), channel_id=1, source_target_pairs={{16,0},{32,16},{48,32},{64,48},{80,64},{96,80},{112,96},{128,112},... | collective-permute-start | bytes 196616 | tf_op jit(solution)/shard_map/ppermute | solution.py:193
Sparse Core Ops, SparseCore 0:
  11.1 65.3 all-gather.2

commit v3 on v2

v3 whole, which is shorter than its diff:
```python
import functools
import math

import jax
import jax.numpy as jnp
import ml_dtypes
import numpy as np
from jax import lax
from jax.experimental import pallas as pl
from jax.experimental.pallas import tpu as pltpu
from jax.sharding import PartitionSpec as P

D = 4096
KV = 4
HD = 128
ROWS = 128
TICKS = 2
GROUP_SIZE = 16
GROUPS = 32

EPS = 1e-05
THETA = 500000.0
SCALE = 1.0 / math.sqrt(HD)
F32 = jnp.float32
BF16 = jnp.bfloat16
VMEM_LIMIT = 16 * 1024 * 1024
FIRST_ROWS = 64
MORE_ROWS = 32


def nn(a, b):
    return lax.dot_general(a, b, (((1,), (0,)), ((), ())), preferred_element_type=F32)


def nt(a, b):
    return lax.dot_general(a, b, (((1,), (1,)), ((), ())), preferred_element_type=F32)


def tn(a, b):
    return lax.dot_general(a, b, (((0,), (0,)), ((), ())), preferred_element_type=F32)


def pair_swap(v, axis):
    n = v.shape[axis]
    even = lax.broadcasted_iota(jnp.int32, v.shape, axis) % 2 == 0
    return jnp.where(even, pltpu.roll(v, n - 1, axis), pltpu.roll(v, 1, axis))


def kernel_call(body, outs, specs, args):
    vmem = pl.BlockSpec(memory_space=pltpu.VMEM)
    kinds = {
        "v": vmem,
        "s": pl.BlockSpec(memory_space=pltpu.SMEM),
    }
    return pl.pallas_call(
        body,
        out_shape=outs,
        in_specs=[kinds[kind] for kind in specs],
        out_specs=[vmem] * len(outs),
        compiler_params=pltpu.CompilerParams(vmem_limit_bytes=VMEM_LIMIT),
    )(*args)


def segment_starts(seg_ref, tick):
    lengths = seg_ref[0, tick : tick + 1, :].astype(F32)
    index = lax.broadcasted_iota(jnp.int32, lengths.shape, 1)
    return [
        jnp.sum(jnp.where(index < g, lengths, 0.0), axis=1, keepdims=True)
        for g in range(1, lengths.shape[1])
    ]


def iotas():
    row = lax.broadcasted_iota(jnp.int32, (ROWS, ROWS), 0).astype(F32)
    column = lax.broadcasted_iota(jnp.int32, (ROWS, ROWS), 1).astype(F32)
    return row, column


def position_match(seg_ref, tick):
    row, column = iotas()
    begin = jnp.zeros(row.shape, F32)
    for start in segment_starts(seg_ref, tick):
        begin = jnp.where(row >= start, start, begin)
    return jnp.where(column == row - begin, 1.0, 0.0).astype(BF16)


def spread_body(saved_ref, out_ref):
    rows = saved_ref.shape[2]
    for i in range(out_ref.shape[0]):
        out_ref[i, :rows] = saved_ref[0, 0]
        out_ref[i, rows:] = saved_ref[0, 1, : out_ref.shape[1] - rows]


def forward_body(
    tick,
    place_ref,
    seg_ref,
    wq_ref,
    wk_ref,
    wv_ref,
    gain_ref,
    ctab_ref,
    stab_ref,
    ctabt_ref,
    stabt_ref,
    *refs,
):
    if tick == 0:
        x_ref, q_ref, kv_ref, inv_ref, cos_ref, sin_ref, cost_ref, sint_ref = refs
    else:
        first, second, third, q_ref, kv_ref, inv_ref, cos_ref, sin_ref, cost_ref, sint_ref, x_ref = (
            refs
        )
        low = first.shape[1] - ROWS
        mid = low + second.shape[1] - ROWS - kv_ref.shape[0]
        for j in range(x_ref.shape[0]):
            x_ref[j, :low] = first[j, ROWS:]
            x_ref[j, low:mid] = second[j, ROWS + kv_ref.shape[0] :]
            x_ref[j, mid:] = third[j, ROWS:]
    blocks, _, width = x_ref.shape
    half = wk_ref.shape[0]
    match = position_match(seg_ref, tick)
    own = pl.ds(pl.multiple_of(place_ref[0] * half, half), half)
    cos = sum(nn(match, ctab_ref[i]) for i in range(3))
    sin = sum(nn(match, stab_ref[i]) for i in range(3))
    cos_t = sum(nt(ctabt_ref[i, own, :], match) for i in range(3))
    sin_t = sum(nt(stabt_ref[i, own, :], match) for i in range(3))
    cos_ref[...] = cos
    sin_ref[...] = sin
    cost_ref[...] = cos_t
    sint_ref[...] = sin_t
    squares = jnp.zeros((ROWS, width), F32)
    for j in range(blocks):
        xj = x_ref[j, :ROWS].astype(F32)
        squares = squares + xj * xj
    inverse = lax.rsqrt(jnp.sum(squares, axis=1, keepdims=True) * (1.0 / D) + EPS)
    inv_ref[...] = inverse
    query = jnp.zeros(q_ref.shape, F32)
    keys = jnp.zeros((half, ROWS), F32)
    values = jnp.zeros((half, ROWS), F32)
    for j in range(blocks):
        part = slice(j * width, (j + 1) * width)
        normed = x_ref[j, :ROWS].astype(F32) * inverse * gain_ref[:, part].astype(F32)
        normed = normed.astype(BF16)
        query = query + nn(normed, wq_ref[part, :])
        keys = keys + nt(wk_ref[:, part], normed)
        values = values + nt(wv_ref[:, part], normed)
    for h in range(query.shape[1] // HD):
        cols = slice(h * HD, (h + 1) * HD)
        head = query[:, cols]
        q_ref[:, cols] = (head * cos + pair_swap(head, 1) * sin).astype(BF16)
    keys = keys * cos_t + pair_swap(keys, 0) * sin_t
    kv_ref[...] = jnp.concatenate([keys, values], axis=1).astype(BF16)


def first_pack_body(early, grad_ref, kv_ref, saved_ref, out_ref):
    start = grad_ref.shape[0] + kv_ref.shape[0]
    for i in range(out_ref.shape[0]):
        out_ref[i, : grad_ref.shape[0]] = grad_ref[...]
        out_ref[i, grad_ref.shape[0] : start] = kv_ref[...]
        out_ref[i, start:] = saved_ref[0, 1, early : early + out_ref.shape[1] - start]


def pack_body(*refs):
    parts, out_ref = refs[:-1], refs[-1]
    for i in range(out_ref.shape[0]):
        start = 0
        for part in parts:
            out_ref[i, start : start + part.shape[0]] = part[...]
            start += part.shape[0]


def next_gradient(tick, last_ref, received_ref, score_ref, rewards_ref, group_ref, sample_ref, grad_ref):
    grad_ref[...] = received_ref[...]

    @pl.when(last_ref[0] > 0)
    def _():
        rewards = rewards_ref[...]
        samples = rewards.shape[1]
        prompt = lax.broadcasted_iota(jnp.int32, (GROUPS, samples), 0)
        member = prompt == group_ref[...]
        totals = jnp.sum(jnp.where(member, rewards, 0.0), axis=1, keepdims=True)
        own_total = jnp.sum(jnp.where(member, totals, 0.0), axis=0, keepdims=True)
        advantage = rewards - (own_total - rewards) / (GROUP_SIZE - 1)
        sample = lax.broadcasted_iota(jnp.int32, (ROWS, samples), 1)
        row, column = iotas()
        own = jnp.where(row == column, sample_ref[tick : tick + 1, :].astype(F32), 0.0)
        chosen = sample.astype(F32) == jnp.sum(own, axis=1, keepdims=True)
        row_adv = jnp.sum(jnp.where(chosen, advantage, 0.0), axis=1, keepdims=True)
        grad_ref[...] = (-row_adv * score_ref[tick].astype(F32)).astype(BF16)


def turn_body(
    tick,
    last_ref,
    received_ref,
    score_ref,
    rewards_ref,
    group_ref,
    sample_ref,
    kv_ref,
    grad_ref,
    out_ref,
):
    next_gradient(
        tick, last_ref, received_ref, score_ref, rewards_ref, group_ref, sample_ref, grad_ref
    )
    pack_body(grad_ref, kv_ref, out_ref)


def attention_body(
    tick,
    base_ref,
    seg_ref,
    got_ref,
    wo_ref,
    q_ref,
    cos_ref,
    sin_ref,
    dq_ref,
    dkv_ref,
    t_ref,
):
    blocks, _, width = got_ref.shape
    shares, half = dkv_ref.shape[0], dkv_ref.shape[1] // 2
    kv = [got_ref[base_ref[0] + i, ROWS : ROWS + half] for i in range(shares)]
    keys = jnp.concatenate([part[:, :ROWS] for part in kv], axis=0)
    values = jnp.concatenate([part[:, ROWS:] for part in kv], axis=0)
    row, column = iotas()
    allowed = column <= row
    for start in segment_starts(seg_ref, tick):
        allowed = allowed & ((row < start) | (column >= start))
    dout = jnp.zeros(dq_ref.shape, F32)
    for j in range(blocks):
        dout = dout + nt(got_ref[j, :ROWS], wo_ref[:, j * width : (j + 1) * width])
    dout = dout.astype(BF16)
    dkeys = jnp.zeros((HD, ROWS), F32)
    dvalues = jnp.zeros((HD, ROWS), F32)
    own = jnp.zeros((ROWS, HD), F32)
    for h in range(dq_ref.shape[1] // HD):
        cols = slice(h * HD, (h + 1) * HD)
        query = q_ref[:, cols]
        dhead = dout[:, cols]
        weights = jnp.where(allowed, jnp.exp(nn(query, keys) * SCALE), 0.0)
        softmax = weights / jnp.sum(weights, axis=1, keepdims=True)
        dprobs = nn(dhead, values)
        delta = jnp.sum(softmax * dprobs, axis=1, keepdims=True)
        dscores = (softmax * (dprobs - delta) * SCALE).astype(BF16)
        dquery = nt(dscores, keys)
        dkeys = dkeys + tn(query, dscores)
        dvalues = dvalues + tn(dhead, softmax.astype(BF16))
        own = own + dquery * query.astype(F32)
        dq_ref[:, cols] = (dquery * cos_ref[...] - pair_swap(dquery, 1) * sin_ref[...]).astype(BF16)
    shared = dkeys * keys.astype(F32) + dvalues * values.astype(F32)
    t_ref[...] = jnp.sum(own + shared.T, axis=1, keepdims=True)
    for i in range(shares):
        part = slice(i * half, (i + 1) * half)
        dkv_ref[i, :half] = dkeys[part].astype(BF16)
        dkv_ref[i, half:] = dvalues[part].astype(BF16)


def partial_body(
    middle,
    x_ref,
    dq_ref,
    dkv_ref,
    wq_ref,
    wk_ref,
    wv_ref,
    gain_ref,
    inv_ref,
    t_ref,
    cost_ref,
    sint_ref,
    *refs,
):
    out_ref = refs[-1]
    blocks, _, width = x_ref.shape
    dkv = dkv_ref[0].astype(F32)
    for i in range(1, dkv_ref.shape[0]):
        dkv = dkv + dkv_ref[i].astype(F32)
    half = dkv.shape[0] // 2
    dkeys = dkv[:half]
    dkeys = (dkeys * cost_ref[...] - pair_swap(dkeys, 0) * sint_ref[...]).astype(BF16)
    dvalues = dkv[half:].astype(BF16)
    dq = dq_ref[...]
    inverse = inv_ref[...]
    along = inverse * inverse * t_ref[...] * (1.0 / D)
    for j in range(blocks):
        part = slice(j * width, (j + 1) * width)
        total = nt(dq, wq_ref[part, :])
        total = total + tn(dkeys, wk_ref[:, part]) + tn(dvalues, wv_ref[:, part])
        scaled = total * (inverse * gain_ref[:, part].astype(F32))
        out_ref[j, :ROWS] = (scaled - x_ref[j, :ROWS].astype(F32) * along).astype(BF16)
        for saved_ref in refs[:-1]:
            out_ref[j, ROWS:] = saved_ref[0, 1, middle:]


def shifted(value, axis, steps):
    count = lax.axis_size(axis)
    first, last = (max(0, -steps), min(count, count - steps))
    return lax.ppermute(value, axis, [(source, source + steps) for source in range(first, last)])


def thirds(table):
    parts = []
    for _ in range(3):
        part = table.astype(ml_dtypes.bfloat16)
        parts.append(part)
        table = table - part.astype(np.float32)
    return jnp.asarray(np.stack(parts))


def rotation_tables():
    column = np.arange(HD)
    frequency = np.exp((column // 2).astype(np.float32) * np.float32(-2.0 * math.log(THETA) / HD))
    angles = np.arange(ROWS).astype(np.float32)[:, None] * frequency[None, :].astype(np.float32)
    parity = np.where(column % 2 == 0, -1.0, 1.0).astype(np.float32)
    cos = np.cos(angles).astype(np.float32)
    sin = (np.sin(angles) * parity).astype(np.float32)
    return [thirds(table) for table in (cos, sin, cos.T, sin.T)]


def per_device(
    saved,
    incoming,
    gain,
    w_query,
    w_key,
    w_value,
    w_out,
    seg_lengths,
    score_grad,
    rewards,
    sample_group,
    head_sample,
):
    tp_index = lax.axis_index("tp")
    tp_count = lax.axis_size("tp")
    last_section = lax.axis_index("pipe") == lax.axis_size("pipe") - 1
    share = tp_count // KV
    groups = [list(range(g * share, (g + 1) * share)) for g in range(KV)]
    wq, wk, wv, wo = w_query[0], w_key[0].T, w_value[0].T, w_out[0]
    kv_share = wk.shape[0]
    width = saved.shape[3]
    base = (tp_index // share * share).astype(jnp.int32)[None]
    place = (tp_index % share).astype(jnp.int32)[None]
    early, middle = FIRST_ROWS, FIRST_ROWS + MORE_ROWS
    tables = rotation_tables()

    def blocks_of(rows):
        return (jax.ShapeDtypeStruct((tp_count, rows, width), BF16),)

    def forward(tick, *rows):
        outs = (
            jax.ShapeDtypeStruct((ROWS, wq.shape[1]), BF16),
            jax.ShapeDtypeStruct((kv_share, 2 * ROWS), BF16),
            jax.ShapeDtypeStruct((ROWS, 1), F32),
            jax.ShapeDtypeStruct((ROWS, HD), F32),
            jax.ShapeDtypeStruct((ROWS, HD), F32),
            jax.ShapeDtypeStruct((kv_share, ROWS), F32),
            jax.ShapeDtypeStruct((kv_share, ROWS), F32),
        )
        return kernel_call(
            functools.partial(forward_body, tick),
            outs + (blocks_of(ROWS) if tick else ()),
            "s" + "v" * (9 + len(rows)),
            (place, seg_lengths, wq, wk, wv, gain, *tables, *rows),
        )

    def exchange(rows):
        return lax.all_to_all(rows, "tp", 0, 0)

    last_flag = last_section.astype(jnp.int32)[None]
    saved, base, place, last_flag = lax.optimization_barrier((saved, base, place, last_flag))
    (spread,) = kernel_call(spread_body, blocks_of(ROWS + early), "v", (saved,))
    first = exchange(spread)

    def chooser(received):
        return (last_flag, received, score_grad, rewards[None], sample_group[None], head_sample)

    grad = incoming[0]

    outputs = []
    for tick in range(TICKS):
        if tick == 0:
            pieces = forward(0, first)
            rows_full = first
            last = (saved,)
        else:
            rows_full = pieces[7]
            last = ()
        query, kv, inverse, cos, sin, cos_t, sin_t = pieces[:7]
        if tick == 0:
            (packed,) = kernel_call(
                functools.partial(first_pack_body, early),
                blocks_of(ROWS + kv_share + MORE_ROWS),
                "vvv",
                (grad, kv, saved),
            )
        else:
            grad, packed = kernel_call(
                functools.partial(turn_body, tick - 1),
                (jax.ShapeDtypeStruct(grad.shape, BF16),) + blocks_of(ROWS + kv_share),
                "s" + "v" * 6,
                (*chooser(received), kv),
            )
        got = exchange(packed)
        dquery, dkv, along = kernel_call(
            functools.partial(attention_body, tick),
            (
                jax.ShapeDtypeStruct(query.shape, BF16),
                jax.ShapeDtypeStruct((share, 2 * kv_share, ROWS), BF16),
                jax.ShapeDtypeStruct((ROWS, 1), F32),
            ),
            "s" + "v" * 6,
            (base, seg_lengths, got, wo, query, cos, sin),
        )
        dkv = lax.all_to_all(dkv, "tp", 0, 0, axis_index_groups=groups)
        (blocks,) = kernel_call(
            functools.partial(partial_body, middle),
            blocks_of(ROWS if tick else 2 * ROWS - middle),
            "v" * (11 + len(last)),
            (rows_full, dquery, dkv, wq, wk, wv, gain, inverse, along, cos_t, sin_t, *last),
        )
        blocks = exchange(blocks)
        total = jnp.sum(blocks[:, :ROWS].astype(F32), axis=0)
        result = (grad.astype(F32) + total).astype(BF16)
        received = shifted(result, "pipe", -1)
        if tick == 0:
            pieces = forward(1, first, got, blocks)
            received, pieces, result = lax.optimization_barrier((received, pieces, result))
        outputs.append(result)
    (carried,) = kernel_call(
        functools.partial(next_gradient, TICKS - 1),
        (jax.ShapeDtypeStruct(grad.shape, BF16),),
        "s" + "v" * 5,
        chooser(received),
    )
    return (jnp.stack(outputs, axis=0)[None], carried[None])


def solution(mesh):
    placed = (
        P("pipe", None, None, "tp"),
        P("pipe", None, "tp"),
        P("pipe", None),
        P("pipe", None, "tp"),
        P("pipe", None, "tp"),
        P("pipe", None, "tp"),
        P("pipe", "tp", None),
        P("pipe", None, None),
        P(None, None, "tp"),
        P(),
        P(),
        P(),
    )
    return jax.shard_map(
        per_device,
        mesh=mesh,
        in_specs=placed,
        out_specs=(P("pipe", None, None, "tp"), P("pipe", None, "tp")),
        check_vma=False,
    )
```

time: 168 us -> 157 us (0.935)
  blocking collectives: 91.4 us -> 120 us
  between operations: 14.4 us -> 0.95 us
  local copies, waits for them, and re-layouts: 12 us -> 1 us
  starting transfers between devices: 20.6 us -> 11.1 us
  other arithmetic: 10.1 us -> 0.99 us
  waiting for transfers between devices: 9.24 us -> 11.5 us
  Pallas kernels: 8.91 us -> 10.6 us
    all_to_all x4 -> x5, blocking collectives: 77 us -> 106 us  [exchange(): return lax.all_to_all(rows, 'tp', 0, 0)]
    all_to_all x1 -> x0, starting transfers between devices: 7.58 us -> none  [per_device(): lax.all_to_all(jnp.broadcast_to(saved[0, 0][None], full_shape), 'tp', 0, 0)]
    ppermute x2, waiting for transfers between devices: 7.1 us -> 11.5 us  [shifted(): lax.ppermute(value, axis, [(source, source + steps) for source in range(f...]
    dynamic_slice x4 -> x0, local copies, waits for them, and re-layouts: 3.83 us -> none  [the longest x2 1.92 us: tables_of(): sin_t = lax.dynamic_slice_in_dim(sin.T, kv_start, kv_share, 0)]
    convert_element_type x6 -> x2, other arithmetic: 3.14 us -> 0.03 us  [per_device(): result = (grad.astype(F32) + total).astype(BF16)]
    optimization_barrier x4 -> x0, local copies, waits for them, and re-layouts: 2.04 us -> none  [per_device(): lax.optimization_barrier((x_first, head_rows, tables, base, last_section))]
    broadcast_in_dim x2 -> x0, local copies, waits for them, and re-layouts: 1.94 us -> none  [per_device(): jnp.broadcast_to(saved[0, 0][None], full_shape)]
    unnamed x54 -> x34, local copies, waits for them, and re-layouts: 2.89 us -> 1 us
  transfers between devices with their start and end apart: 4 -> 2, of which waited for: 3 -> 2; matrix products, arithmetic and copies ran while one was open for 10% -> 0% of each run, Pallas kernels for 3% -> 1%
where the time goes in v3:
time: 157 us; the launch traced here: 156 us
  blocking collectives  120 us (76%)
  waiting for transfers between devices  11.5 us (7%)
  starting transfers between devices  11.1 us (7%)
  Pallas kernels  10.6 us (7%)
    all_to_all x5, blocking collectives, exchange(): return lax.all_to_all(rows, 'tp', 0, 0)  106 us
    all_to_all x2, blocking collectives, per_device(): dkv = lax.all_to_all(dkv, 'tp', 0, 0, axis_index_groups=groups)  14.1 us
    ppermute x2, waiting for transfers between devices, shifted(): lax.ppermute(value, axis, [(source, source + steps) for source in range(f...  11.5 us
    ppermute x2, starting transfers between devices, shifted(): lax.ppermute(value, axis, [(source, source + steps) for source in range(f...  11.1 us
    pallas_call x10, Pallas kernels, kernel_call(): pl.pallas_call(body, out_shape=outs, in_specs=[kinds[kind] for kind in sp...  10.6 us
  transfers between devices with their start and end apart: 2, of which 2 were waited for; matrix products, arithmetic and copies ran while one was open for 0% of the time, Pallas kernels for 1%

profile of v3, /device:TPU:1, one launch (start us, length us, event | category | flops | bytes accessed | tf_op | source)
XLA Modules:
  0.0 156.2 jit_solution(10821043008380486808)
XLA Ops:
  0.7 0.0 copy-start.4
  0.7 0.9 copy-done.4
  1.6 0.1 shard_map.167
  1.7 0.0 copy-start
  1.7 0.0 copy-start.2
  1.7 0.0 copy-start.3
  1.7 0.0 copy-start.7
  1.7 0.0 copy-start.8
  1.7 0.0 copy-start.9
  1.7 0.0 copy-start.10
  1.8 0.0 copy-start.11
  1.8 0.0 copy-start.13
  1.8 28.3 %all_to_all.35.refs_0_.x_ref = bf16[16,192,256]{2,1,0:T(8,128)(2,1)S(1)} all-to-all(bf16[16,192,256]{2,1,0:T(8,128)(2,1)S(1)} %shard_map.167), channel_id=1, replica_groups=mesh['pipe'=32,'tp'=16] {'tp'}, dimensions={0} | all-to-all | bytes 3145728 | tf_op jit(solution)/shard_map/all_to_all | solution.py:372
  30.0 0.0 copy-done
  30.0 0.0 copy-done.2
  30.1 0.0 copy-start.5
  30.1 0.0 copy-start.12
  30.1 1.5 shard_map.168
  31.7 0.0 copy-done.5
  31.7 0.0 copy-done.12
  31.7 0.1 shard_map.169
  31.8 0.0 copy-start.1
  31.8 22.1 %all_to_all.36.got_ref.refs_1_ = bf16[16,192,256]{2,1,0:T(8,128)(2,1)S(1)} all-to-all(bf16[16,192,256]{2,1,0:T(8,128)(2,1)S(1)} %shard_map.169), channel_id=1, replica_groups=mesh['pipe'=32,'tp'=16] {'tp'}, dimensions={0} | all-to-all | bytes 3145728 | tf_op jit(solution)/shard_map/all_to_all | solution.py:372
  53.9 0.0 copy-done.1
  53.9 1.8 %shard_map.170 = (bf16[128,256]{1,0:T(8,128)(2,1)S(1)}, bf16[4,64,128]{2,1,0:T(8,128)(2,1)S(1)}, f32[128,1]{1,0:T(8,128)S(1)}) custom-call(s32[1]{0:T(128)} %bitcast.1.base_ref, s32[1,2,4]{2,1,0:T(2,128)S(1)} %copy-done.13, bf16[16,192,256]{2,1,0:T(8,128)(2,1)S(1)} %all_to_all.36.got_ref.refs_1_, bf16[256,4096]{1,0:T(8,128)(2,1)S(1)} %bitcast.24, ...), custom_call_target="tpu_custom_call" | custom-call | tf_op jit(solution)/shard_map/pallas_call | solution.py:55
  55.7 7.2 %all_to_all.37.dkv_ref = bf16[4,64,128]{2,1,0:T(8,128)(2,1)S(1)} all-to-all(bf16[4,64,128]{2,1,0:T(8,128)(2,1)S(1)} %get-tuple-element.47), channel_id=1, replica_groups={{0,1,2,3},{4,5,6,7},{8,9,10,11},{12,13,14,15},{16,17,18,19},{20,21,22,2..., dimensions={0} | all-to-all | bytes 131072 | tf_op jit(solution)/shard_map/all_to_all | solution.py:419
  63.0 1.5 shard_map.171
  64.5 16.8 %all_to_all.38.refs_2_ = bf16[16,160,256]{2,1,0:T(8,128)(2,1)S(1)} all-to-all(bf16[16,160,256]{2,1,0:T(8,128)(2,1)S(1)} %shard_map.171), channel_id=1, replica_groups=mesh['pipe'=32,'tp'=16] {'tp'}, dimensions={0} | all-to-all | bytes 2621440 | tf_op jit(solution)/shard_map/all_to_all | solution.py:372
  81.3 0.1 convert_reduce_fusion.1
  81.5 0.0 copy-start.6
  81.5 0.0 copy-start.14
  81.5 0.0 copy-start.15
  81.5 0.0 copy-start.16
  81.5 9.2 %collective-permute-start = (bf16[128,256]{1,0:T(8,128)(2,1)S(1)}, bf16[128,256]{1,0:T(8,128)(2,1)S(1)}, u32[]{:S(2)}, u32[]{:S(2)}) collective-permute-start(bf16[128,256]{1,0:T(8,128)(2,1)S(1)} %add_convert_fusion.1), channel_id=1, source_target_pairs={{16,0},{32,16},{48,32},{64,48},{80,64},{96,80},{112,96},{128,112},... | collective-permute-start | bytes 196616 | tf_op jit(solution)/shard_map/ppermute | solution.py:302
  90.8 1.6 %shard_map.172 = (bf16[128,256]{1,0:T(8,128)(2,1)S(1)}, bf16[32,256]{1,0:T(8,128)(2,1)S(1)}, f32[128,1]{1,0:T(8,128)S(1)}, f32[128,128]{1,0:T(8,128)S(1)}, f32[1...) custom-call(s32[1]{0:T(128)} %bitcast.2.place_ref, ...), custom_call_target="tpu_custom_call" | custom-call | tf_op jit(solution)/shard_map/pallas_call | solution.py:55
  92.4 4.1 %collective-permute-done.received_ref = bf16[128,256]{1,0:T(8,128)(2,1)S(1)} collective-permute-done((bf16[128,256]{1,0:T(8,128)(2,1)S(1)}, bf16[128,256]{1,0:T(8,128)(2,1)S(1)}, u32[]{:S(2)}, u32[]{:S(2)}) %collective-permute-start) | collective-permute-done | bytes 65568 | tf_op jit(solution)/shard_map/ppermute | solution.py:302
  96.4 0.0 copy-done.14
  96.4 0.1 shard_map.173
  96.6 19.5 %all_to_all.39.got_ref = bf16[16,160,256]{2,1,0:T(8,128)(2,1)S(1)} all-to-all(bf16[16,160,256]{2,1,0:T(8,128)(2,1)S(1)} %get-tuple-element.66), channel_id=1, replica_groups=mesh['pipe'=32,'tp'=16] {'tp'}, dimensions={0} | all-to-all | bytes 2621440 | tf_op jit(solution)/shard_map/all_to_all | solution.py:372
  116.0 1.8 %shard_map.174 = (bf16[128,256]{1,0:T(8,128)(2,1)S(1)}, bf16[4,64,128]{2,1,0:T(8,128)(2,1)S(1)}, f32[128,1]{1,0:T(8,128)S(1)}) custom-call(s32[1]{0:T(128)} %bitcast.1.base_ref, s32[1,2,4]{2,1,0:T(2,128)S(1)} %copy-done.13, bf16[16,160,256]{2,1,0:T(8,128)(2,1)S(1)} %all_to_all.39.got_ref, bf16[256,4096]{1,0:T(8,128)(2,1)S(1)} %bitcast.25, ...), custom_call_target="tpu_custom_call" | custom-call | tf_op jit(solution)/shard_map/pallas_call | solution.py:55
  117.8 6.8 %all_to_all.40.dkv_ref = bf16[4,64,128]{2,1,0:T(8,128)(2,1)S(1)} all-to-all(bf16[4,64,128]{2,1,0:T(8,128)(2,1)S(1)} %get-tuple-element.71), channel_id=1, replica_groups={{0,1,2,3},{4,5,6,7},{8,9,10,11},{12,13,14,15},{16,17,18,19},{20,21,22,2..., dimensions={0} | all-to-all | bytes 131072 | tf_op jit(solution)/shard_map/all_to_all | solution.py:419
  124.6 1.5 shard_map.175
  126.2 19.2 %all_to_all.41 = bf16[16,128,256]{2,1,0:T(8,128)(2,1)S(1)} all-to-all(bf16[16,128,256]{2,1,0:T(8,128)(2,1)S(1)} %shard_map.175), channel_id=1, replica_groups=mesh['pipe'=32,'tp'=16] {'tp'}, dimensions={0} | all-to-all | bytes 2097152 | tf_op jit(solution)/shard_map/all_to_all | solution.py:372
  145.4 0.1 convert_reduce_fusion
  145.5 1.9 %collective-permute-start.1 = (bf16[128,256]{1,0:T(8,128)(2,1)S(1)}, bf16[128,256]{1,0:T(8,128)(2,1)S(1)}, u32[]{:S(2)}, u32[]{:S(2)}) collective-permute-start(bf16[128,256]{1,0:T(8,128)(2,1)S(1)} %add_convert_fusion), channel_id=1, source_target_pairs={{16,0},{32,16},{48,32},{64,48},{80,64},{96,80},{112,96},{128,112},... | collective-permute-start | bytes 196616 | tf_op jit(solution)/shard_map/ppermute | solution.py:302
  147.5 0.7 maximum_bitcast_fusion
  148.1 7.5 %collective-permute-done.1.received_ref = bf16[128,256]{1,0:T(8,128)(2,1)S(1)} collective-permute-done((bf16[128,256]{1,0:T(8,128)(2,1)S(1)}, bf16[128,256]{1,0:T(8,128)(2,1)S(1)}, u32[]{:S(2)}, u32[]{:S(2)}) %collective-permute-start.1) | collective-permute-done | bytes 65568 | tf_op jit(solution)/shard_map/ppermute | solution.py:302
  155.6 0.6 shard_map.176
  (12 shorter events, 0.1 us)
Async XLA Ops:
  0.7 0.9 copy-start.4
  1.7 28.4 %copy-start = (bf16[1,4096,256]{2,1,0:T(8,128)(2,1)S(1)}, bf16[1,4096,256]{2,1,0:T(8,128)(2,1)}, u32[]{:S(2)}) copy-start(bf16[1,4096,256]{2,1,0:T(8,128)(2,1)} %param.19) | copy-start | bytes 6291460
  1.7 28.4 %copy-start.2 = (bf16[1,4096,32]{1,2,0:T(8,128)(2,1)S(1)}, bf16[1,4096,32]{1,2,0:T(8,128)(2,1)}, u32[]{:S(2)}) copy-start(bf16[1,4096,32]{1,2,0:T(8,128)(2,1)} %param.20) | copy-start | bytes 786436
  1.7 28.4 %copy-start.3 = (bf16[1,4096,32]{1,2,0:T(8,128)(2,1)S(1)}, bf16[1,4096,32]{1,2,0:T(8,128)(2,1)}, u32[]{:S(2)}) copy-start(bf16[1,4096,32]{1,2,0:T(8,128)(2,1)} %param.21) | copy-start | bytes 786436
  1.7 28.4 %copy-start.7 = (bf16[3,128,128]{2,1,0:T(8,128)(2,1)S(1)}, bf16[3,128,128]{2,1,0:T(8,128)(2,1)}, u32[]{:S(2)}) copy-start(bf16[3,128,128]{2,1,0:T(8,128)(2,1)} %constant.50.clone.stabt_ref) | copy-start | bytes 294916
  1.7 28.4 %copy-start.8 = (bf16[3,128,128]{2,1,0:T(8,128)(2,1)S(1)}, bf16[3,128,128]{2,1,0:T(8,128)(2,1)}, u32[]{:S(2)}) copy-start(bf16[3,128,128]{2,1,0:T(8,128)(2,1)} %constant.49.clone.ctabt_ref) | copy-start | bytes 294916
  1.7 28.4 %copy-start.9 = (bf16[3,128,128]{2,1,0:T(8,128)(2,1)S(1)}, bf16[3,128,128]{2,1,0:T(8,128)(2,1)}, u32[]{:S(2)}) copy-start(bf16[3,128,128]{2,1,0:T(8,128)(2,1)} %constant.48.clone.stab_ref) | copy-start | bytes 294916
  1.7 28.3 %copy-start.10 = (bf16[3,128,128]{2,1,0:T(8,128)(2,1)S(1)}, bf16[3,128,128]{2,1,0:T(8,128)(2,1)}, u32[]{:S(2)}) copy-start(bf16[3,128,128]{2,1,0:T(8,128)(2,1)} %constant.47.clone.ctab_ref) | copy-start | bytes 294916
  1.8 28.3 %copy-start.11 = (bf16[1,4096]{1,0:T(2,128)(2,1)S(1)}, bf16[1,4096]{1,0:T(2,128)(2,1)}, u32[]{:S(2)}) copy-start(bf16[1,4096]{1,0:T(2,128)(2,1)} %gain_ref.7) | copy-start | bytes 24580
  1.8 28.3 %copy-start.13 = (s32[1,2,4]{2,1,0:T(2,128)S(1)}, s32[1,2,4]{2,1,0:T(2,128)}, u32[]{:S(2)}) copy-start(s32[1,2,4]{2,1,0:T(2,128)} %seg_ref.7) | copy-start | bytes 100
  30.1 1.6 %copy-start.5 = (bf16[1,2,128,256]{3,2,1,0:T(8,128)(2,1)S(1)}, bf16[1,2,128,256]{3,2,1,0:T(8,128)(2,1)}, u32[]{:S(2)}) copy-start(bf16[1,2,128,256]{3,2,1,0:T(8,128)(2,1)} %refs_0_) | copy-start | bytes 393220
  30.1 1.6 %copy-start.12 = (bf16[1,128,256]{2,1,0:T(8,128)(2,1)S(1)}, bf16[1,128,256]{2,1,0:T(8,128)(2,1)}, u32[]{:S(2)}) copy-start(bf16[1,128,256]{2,1,0:T(8,128)(2,1)} %param.17) | copy-start | bytes 196612
  31.8 22.1 %copy-start.1 = (bf16[1,256,4096]{2,1,0:T(8,128)(2,1)S(1)}, bf16[1,256,4096]{2,1,0:T(8,128)(2,1)}, u32[]{:S(2)}) copy-start(bf16[1,256,4096]{2,1,0:T(8,128)(2,1)} %param.22) | copy-start | bytes 6291460
  81.5 14.9 %copy-start.6 = (bf16[2,128,256]{2,1,0:T(8,128)(2,1)S(1)}, bf16[2,128,256]{2,1,0:T(8,128)(2,1)}, u32[]{:S(2)}) copy-start(bf16[2,128,256]{2,1,0:T(8,128)(2,1)} %score_ref.3) | copy-start | bytes 393220
  81.5 14.9 %copy-start.14 = (f32[512]{0:T(512)S(1)}, f32[512]{0:T(512)}, u32[]{:S(2)}) copy-start(f32[512]{0:T(512)} %param.25) | copy-start | bytes 6148
  81.5 14.9 %copy-start.15 = (s32[512]{0:T(512)S(1)}, s32[512]{0:T(512)}, u32[]{:S(2)}) copy-start(s32[512]{0:T(512)} %param.26) | copy-start | bytes 6148
  81.5 14.9 %copy-start.16 = (s32[2,128]{1,0:T(2,128)S(1)}, s32[2,128]{1,0:T(2,128)}, u32[]{:S(2)}) copy-start(s32[2,128]{1,0:T(2,128)} %sample_ref.3) | copy-start | bytes 3076
  81.5 14.9 %collective-permute-start = (bf16[128,256]{1,0:T(8,128)(2,1)S(1)}, bf16[128,256]{1,0:T(8,128)(2,1)S(1)}, u32[]{:S(2)}, u32[]{:S(2)}) collective-permute-start(bf16[128,256]{1,0:T(8,128)(2,1)S(1)} %add_convert_fusion.1), channel_id=1, source_target_pairs={{16,0},{32,16},{48,32},{64,48},{80,64},{96,80},{112,96},{128,112},... | collective-permute-start | bytes 196616 | tf_op jit(solution)/shard_map/ppermute | solution.py:302
  145.5 10.1 %collective-permute-start.1 = (bf16[128,256]{1,0:T(8,128)(2,1)S(1)}, bf16[128,256]{1,0:T(8,128)(2,1)S(1)}, u32[]{:S(2)}, u32[]{:S(2)}) collective-permute-start(bf16[128,256]{1,0:T(8,128)(2,1)S(1)} %add_convert_fusion), channel_id=1, source_target_pairs={{16,0},{32,16},{48,32},{64,48},{80,64},{96,80},{112,96},{128,112},... | collective-permute-start | bytes 196616 | tf_op jit(solution)/shard_map/ppermute | solution.py:302

commit v4 on v3

v4 whole, which is shorter than its diff:
```python
import functools
import math

import jax
import jax.numpy as jnp
import ml_dtypes
import numpy as np
from jax import lax
from jax.experimental import pallas as pl
from jax.experimental.pallas import tpu as pltpu
from jax.sharding import PartitionSpec as P

D = 4096
KV = 4
HD = 128
ROWS = 128
TICKS = 2
GROUP_SIZE = 16
GROUPS = 32

EPS = 1e-05
THETA = 500000.0
SCALE = 1.0 / math.sqrt(HD)
F32 = jnp.float32
BF16 = jnp.bfloat16
VMEM_LIMIT = 16 * 1024 * 1024


def nn(a, b):
    return lax.dot_general(a, b, (((1,), (0,)), ((), ())), preferred_element_type=F32)


def nt(a, b):
    return lax.dot_general(a, b, (((1,), (1,)), ((), ())), preferred_element_type=F32)


def tn(a, b):
    return lax.dot_general(a, b, (((0,), (0,)), ((), ())), preferred_element_type=F32)


def pair_swap(v, axis):
    n = v.shape[axis]
    even = lax.broadcasted_iota(jnp.int32, v.shape, axis) % 2 == 0
    return jnp.where(even, pltpu.roll(v, n - 1, axis), pltpu.roll(v, 1, axis))


def kernel_call(body, outs, specs, args):
    vmem = pl.BlockSpec(memory_space=pltpu.VMEM)
    kinds = {
        "v": vmem,
        "s": pl.BlockSpec(memory_space=pltpu.SMEM),
    }
    return pl.pallas_call(
        body,
        out_shape=outs,
        in_specs=[kinds[kind] for kind in specs],
        out_specs=[vmem] * len(outs),
        compiler_params=pltpu.CompilerParams(vmem_limit_bytes=VMEM_LIMIT),
    )(*args)


def segment_starts(seg_ref, tick):
    lengths = seg_ref[0, tick : tick + 1, :].astype(F32)
    index = lax.broadcasted_iota(jnp.int32, lengths.shape, 1)
    return [
        jnp.sum(jnp.where(index < g, lengths, 0.0), axis=1, keepdims=True)
        for g in range(1, lengths.shape[1])
    ]


def iotas():
    row = lax.broadcasted_iota(jnp.int32, (ROWS, ROWS), 0).astype(F32)
    column = lax.broadcasted_iota(jnp.int32, (ROWS, ROWS), 1).astype(F32)
    return row, column


def position_match(seg_ref, tick):
    row, column = iotas()
    begin = jnp.zeros(row.shape, F32)
    for start in segment_starts(seg_ref, tick):
        begin = jnp.where(row >= start, start, begin)
    return jnp.where(column == row - begin, 1.0, 0.0).astype(BF16)


def spread_body(saved_ref, grad_ref, out_ref):
    for i in range(out_ref.shape[0]):
        for tick in range(TICKS):
            out_ref[i, tick * ROWS : (tick + 1) * ROWS] = saved_ref[0, tick]
        out_ref[i, TICKS * ROWS :] = grad_ref[0]


def forward_body(
    place_ref,
    seg_ref,
    wq_ref,
    wk_ref,
    wv_ref,
    gain_ref,
    ctab_ref,
    stab_ref,
    ctabt_ref,
    stabt_ref,
    x_ref,
    q_ref,
    kv_ref,
    inv_ref,
    cos_ref,
    sin_ref,
    cost_ref,
    sint_ref,
    wkv_ref,
):
    half = wk_ref.shape[0]
    wkv_ref[:half] = wk_ref[...]
    wkv_ref[half:] = wv_ref[...]
    blocks, _, width = x_ref.shape
    rows = TICKS * ROWS
    own = pl.ds(pl.multiple_of(place_ref[0] * half, half), half)
    squares = jnp.zeros((rows, width), F32)
    for j in range(blocks):
        xj = x_ref[j, :rows].astype(F32)
        squares = squares + xj * xj
    inverse = lax.rsqrt(jnp.sum(squares, axis=1, keepdims=True) * (1.0 / D) + EPS)
    query = jnp.zeros((rows, wq_ref.shape[1]), F32)
    kvt = jnp.zeros((2 * half, rows), F32)
    for j in range(blocks):
        part = slice(j * width, (j + 1) * width)
        normed = x_ref[j, :rows].astype(F32) * inverse * gain_ref[:, part].astype(F32)
        normed = normed.astype(BF16)
        query = query + nn(normed, wq_ref[part, :])
        kvt = kvt + nt(wkv_ref[:, part], normed)
    for tick in range(TICKS):
        here = slice(tick * ROWS, (tick + 1) * ROWS)
        inv_ref[tick] = inverse[here]
        match = position_match(seg_ref, tick)
        cos = sum(nn(match, ctab_ref[i]) for i in range(3))
        sin = sum(nn(match, stab_ref[i]) for i in range(3))
        cos_t = sum(nt(ctabt_ref[i, own, :], match) for i in range(3))
        sin_t = sum(nt(stabt_ref[i, own, :], match) for i in range(3))
        cos_ref[tick] = cos
        sin_ref[tick] = sin
        cost_ref[tick] = cos_t
        sint_ref[tick] = sin_t
        for h in range(query.shape[1] // HD):
            cols = slice(h * HD, (h + 1) * HD)
            head = query[here, cols]
            q_ref[tick, :, cols] = (head * cos + pair_swap(head, 1) * sin).astype(BF16)
        keys = kvt[:half, here]
        keys = keys * cos_t + pair_swap(keys, 0) * sin_t
        both = jnp.concatenate([keys, kvt[half:, here]], axis=0).astype(BF16)
        for i in range(kv_ref.shape[0]):
            kv_ref[i, tick] = both


def next_gradient(tick, last_ref, received_ref, score_ref, rewards_ref, group_ref, sample_ref, grad_ref):
    grad_ref[...] = received_ref[...]

    @pl.when(last_ref[0] > 0)
    def _():
        rewards = rewards_ref[...]
        samples = rewards.shape[1]
        prompt = lax.broadcasted_iota(jnp.int32, (GROUPS, samples), 0)
        member = prompt == group_ref[...]
        totals = jnp.sum(jnp.where(member, rewards, 0.0), axis=1, keepdims=True)
        own_total = jnp.sum(jnp.where(member, totals, 0.0), axis=0, keepdims=True)
        advantage = rewards - (own_total - rewards) / (GROUP_SIZE - 1)
        sample = lax.broadcasted_iota(jnp.int32, (ROWS, samples), 1)
        row, column = iotas()
        own = jnp.where(row == column, sample_ref[tick : tick + 1, :].astype(F32), 0.0)
        chosen = sample.astype(F32) == jnp.sum(own, axis=1, keepdims=True)
        row_adv = jnp.sum(jnp.where(chosen, advantage, 0.0), axis=1, keepdims=True)
        grad_ref[...] = (-row_adv * score_ref[tick].astype(F32)).astype(BF16)


def turn_body(
    tick,
    last_ref,
    received_ref,
    score_ref,
    rewards_ref,
    group_ref,
    sample_ref,
    grad_ref,
    out_ref,
):
    next_gradient(
        tick, last_ref, received_ref, score_ref, rewards_ref, group_ref, sample_ref, grad_ref
    )
    for i in range(out_ref.shape[0]):
        out_ref[i] = grad_ref[...]


def attention_body(
    tick, got_at, seg_ref, got_ref, wo_ref, q_ref, kv_ref, cos_ref, sin_ref, dq_ref, dkv_ref, t_ref
):
    blocks, _, width = got_ref.shape
    shares, half = dkv_ref.shape[0], dkv_ref.shape[1] // 2
    keys = jnp.concatenate([kv_ref[i, tick, :half] for i in range(shares)], axis=0)
    values = jnp.concatenate([kv_ref[i, tick, half:] for i in range(shares)], axis=0)
    cos = cos_ref[tick]
    sin = sin_ref[tick]
    row, column = iotas()
    allowed = column <= row
    for start in segment_starts(seg_ref, tick):
        allowed = allowed & ((row < start) | (column >= start))
    dout = jnp.zeros(dq_ref.shape, F32)
    for j in range(blocks):
        dout = dout + nt(got_ref[j, got_at : got_at + ROWS], wo_ref[:, j * width : (j + 1) * width])
    dout = dout.astype(BF16)
    dkeys = jnp.zeros((HD, ROWS), F32)
    dvalues = jnp.zeros((HD, ROWS), F32)
    own = jnp.zeros((ROWS, HD), F32)
    for h in range(dq_ref.shape[1] // HD):
        cols = slice(h * HD, (h + 1) * HD)
        query = q_ref[tick, :, cols]
        dhead = dout[:, cols]
        weights = jnp.where(allowed, jnp.exp(nn(query, keys) * SCALE), 0.0)
        softmax = weights / jnp.sum(weights, axis=1, keepdims=True)
        dprobs = nn(dhead, values)
        delta = jnp.sum(softmax * dprobs, axis=1, keepdims=True)
        dscores = (softmax * (dprobs - delta) * SCALE).astype(BF16)
        dquery = nt(dscores, keys)
        dkeys = dkeys + tn(query, dscores)
        dvalues = dvalues + tn(dhead, softmax.astype(BF16))
        own = own + dquery * query.astype(F32)
        dq_ref[:, cols] = (dquery * cos - pair_swap(dquery, 1) * sin).astype(BF16)
    shared = dkeys * keys.astype(F32) + dvalues * values.astype(F32)
    t_ref[...] = jnp.sum(own + shared.T, axis=1, keepdims=True)
    for i in range(shares):
        part = slice(i * half, (i + 1) * half)
        dkv_ref[i, :half] = dkeys[part].astype(BF16)
        dkv_ref[i, half:] = dvalues[part].astype(BF16)


def partial_body(
    tick,
    x_ref,
    dq_ref,
    dkv_ref,
    wq_ref,
    wkv_ref,
    gain_ref,
    inv_ref,
    t_ref,
    cost_ref,
    sint_ref,
    out_ref,
):
    blocks, _, width = out_ref.shape
    both = wkv_ref.shape[0]
    half = both // 2
    dkv = dkv_ref[0, :both].astype(F32)
    for i in range(1, dkv_ref.shape[0]):
        dkv = dkv + dkv_ref[i, :both].astype(F32)
    dkeys = dkv[:half]
    dkeys = dkeys * cost_ref[tick] - pair_swap(dkeys, 0) * sint_ref[tick]
    dkv = jnp.concatenate([dkeys, dkv[half:]], axis=0).T.astype(BF16)
    dq = dq_ref[...]
    inverse = inv_ref[tick]
    along = inverse * inverse * t_ref[...] * (1.0 / D)
    for j in range(blocks):
        part = slice(j * width, (j + 1) * width)
        total = nt(dq, wq_ref[part, :]) + nn(dkv, wkv_ref[:, part])
        scaled = total * (inverse * gain_ref[:, part].astype(F32))
        out_ref[j] = (scaled - x_ref[j, tick * ROWS : (tick + 1) * ROWS].astype(F32) * along).astype(BF16)


def shifted(value, axis, steps):
    count = lax.axis_size(axis)
    first, last = (max(0, -steps), min(count, count - steps))
    return lax.ppermute(value, axis, [(source, source + steps) for source in range(first, last)])


def thirds(table):
    parts = []
    for _ in range(3):
        part = table.astype(ml_dtypes.bfloat16)
        parts.append(part)
        table = table - part.astype(np.float32)
    return jnp.asarray(np.stack(parts))


def rotation_tables():
    column = np.arange(HD)
    frequency = np.exp((column // 2).astype(np.float32) * np.float32(-2.0 * math.log(THETA) / HD))
    angles = np.arange(ROWS).astype(np.float32)[:, None] * frequency[None, :].astype(np.float32)
    parity = np.where(column % 2 == 0, -1.0, 1.0).astype(np.float32)
    cos = np.cos(angles).astype(np.float32)
    sin = (np.sin(angles) * parity).astype(np.float32)
    return [thirds(table) for table in (cos, sin, cos.T, sin.T)]


def per_device(
    saved,
    incoming,
    gain,
    w_query,
    w_key,
    w_value,
    w_out,
    seg_lengths,
    score_grad,
    rewards,
    sample_group,
    head_sample,
):
    tp_index = lax.axis_index("tp")
    tp_count = lax.axis_size("tp")
    last_section = lax.axis_index("pipe") == lax.axis_size("pipe") - 1
    share = tp_count // KV
    groups = [list(range(g * share, (g + 1) * share)) for g in range(KV)]
    wq, wk, wv, wo = w_query[0], w_key[0].T, w_value[0].T, w_out[0]
    kv_share = wk.shape[0]
    width = saved.shape[3]
    place = (tp_index % share).astype(jnp.int32)[None]
    tables = rotation_tables()

    def blocks_of(rows):
        return (jax.ShapeDtypeStruct((tp_count, rows, width), BF16),)

    def exchange(rows):
        return lax.all_to_all(rows, "tp", 0, 0)

    last_flag = last_section.astype(jnp.int32)[None]
    saved, place, last_flag = lax.optimization_barrier((saved, place, last_flag))
    (spread,) = kernel_call(spread_body, blocks_of((TICKS + 1) * ROWS), "vv", (saved, incoming))
    first = exchange(spread)

    def chooser(received):
        return (last_flag, received, score_grad, rewards[None], sample_group[None], head_sample)

    grad = incoming[0]
    query, kv, inverse, cos, sin, cos_t, sin_t, wkv = kernel_call(
        forward_body,
        (
            jax.ShapeDtypeStruct((TICKS, ROWS, wq.shape[1]), BF16),
            jax.ShapeDtypeStruct((share, TICKS, 2 * kv_share, ROWS), BF16),
            jax.ShapeDtypeStruct((TICKS, ROWS, 1), F32),
            jax.ShapeDtypeStruct((TICKS, ROWS, HD), F32),
            jax.ShapeDtypeStruct((TICKS, ROWS, HD), F32),
            jax.ShapeDtypeStruct((TICKS, kv_share, ROWS), F32),
            jax.ShapeDtypeStruct((TICKS, kv_share, ROWS), F32),
            jax.ShapeDtypeStruct((2 * kv_share, wk.shape[1]), BF16),
        ),
        "s" + "v" * 10,
        (place, seg_lengths, wq, wk, wv, gain, *tables, first),
    )
    kv = lax.all_to_all(kv, "tp", 0, 0, axis_index_groups=groups)

    outputs = []
    for tick in range(TICKS):
        if tick == 0:
            got, got_at = first, TICKS * ROWS
        else:
            grad, packed = kernel_call(
                functools.partial(turn_body, tick - 1),
                (jax.ShapeDtypeStruct(grad.shape, BF16),) + blocks_of(ROWS),
                "s" + "v" * 5,
                chooser(received),
            )
            got, got_at = exchange(packed), 0
        dquery, dkv, along = kernel_call(
            functools.partial(attention_body, tick, got_at),
            (
                jax.ShapeDtypeStruct(query.shape[1:], BF16),
                jax.ShapeDtypeStruct((share, 2 * kv_share, ROWS), BF16),
                jax.ShapeDtypeStruct((ROWS, 1), F32),
            ),
            "v" * 7,
            (seg_lengths, got, wo, query, kv, cos, sin),
        )
        dkv = lax.all_to_all(dkv, "tp", 0, 0, axis_index_groups=groups)
        (blocks,) = kernel_call(
            functools.partial(partial_body, tick),
            blocks_of(ROWS),
            "v" * 10,
            (first, dquery, dkv, wq, wkv, gain, inverse, along, cos_t, sin_t),
        )
        blocks = exchange(blocks)
        total = jnp.sum(blocks.astype(F32), axis=0)
        result = (grad.astype(F32) + total).astype(BF16)
        received = shifted(result, "pipe", -1)
        if tick == 0:
            received, result = lax.optimization_barrier((received, result))
        outputs.append(result)
    (carried,) = kernel_call(
        functools.partial(next_gradient, TICKS - 1),
        (jax.ShapeDtypeStruct(grad.shape, BF16),),
        "s" + "v" * 5,
        chooser(received),
    )
    return (jnp.stack(outputs, axis=0)[None], carried[None])


def solution(mesh):
    placed = (
        P("pipe", None, None, "tp"),
        P("pipe", None, "tp"),
        P("pipe", None),
        P("pipe", None, "tp"),
        P("pipe", None, "tp"),
        P("pipe", None, "tp"),
        P("pipe", "tp", None),
        P("pipe", None, None),
        P(None, None, "tp"),
        P(),
        P(),
        P(),
    )
    return jax.shard_map(
        per_device,
        mesh=mesh,
        in_specs=placed,
        out_specs=(P("pipe", None, None, "tp"), P("pipe", None, "tp")),
        check_vma=False,
    )
```

time: 157 us -> 153 us (0.975)
  waiting for transfers between devices: 11.5 us -> 8.18 us
  blocking collectives: 120 us -> 118 us
  starting transfers between devices: 11.1 us -> 13 us
  Pallas kernels: 10.6 us -> 8.93 us
    all_to_all x5 -> x4, blocking collectives: 106 us -> 96.2 us  [exchange(): return lax.all_to_all(rows, 'tp', 0, 0)]
    all_to_all x0 -> x1, blocking collectives: none -> 7.81 us  [per_device(): kv = lax.all_to_all(kv, 'tp', 0, 0, axis_index_groups=groups)]
    ppermute x2, waiting for transfers between devices: 11.5 us -> 8.18 us  [shifted(): lax.ppermute(value, axis, [(source, source + steps) for source in range(f...]
    ppermute x2, starting transfers between devices: 11.1 us -> 13 us  [shifted(): lax.ppermute(value, axis, [(source, source + steps) for source in range(f...]
    pallas_call x10 -> x8, Pallas kernels: 10.6 us -> 8.93 us  [kernel_call(): pl.pallas_call(body, out_shape=outs, in_specs=[kinds[kind] for kind in sp...]
  transfers between devices with their start and end apart: 2 -> 2, of which waited for: 2 -> 2; matrix products, arithmetic and copies ran while one was open for 0% -> 0% of each run, Pallas kernels for 1% -> 0%
where the time goes in v4:
time: 153 us; the launch traced here: 152 us
  blocking collectives  118 us (77%)
  starting transfers between devices  13 us (8%)
  Pallas kernels  8.93 us (6%)
  waiting for transfers between devices  8.18 us (5%)
  local copies, waits for them, and re-layouts  1.83 us (1%)
    all_to_all x4, blocking collectives, exchange(): return lax.all_to_all(rows, 'tp', 0, 0)  96.2 us
    all_to_all x2, blocking collectives, per_device(): dkv = lax.all_to_all(dkv, 'tp', 0, 0, axis_index_groups=groups)  13.7 us
    ppermute x2, starting transfers between devices, shifted(): lax.ppermute(value, axis, [(source, source + steps) for source in range(f...  13 us
    pallas_call x8, Pallas kernels, kernel_call(): pl.pallas_call(body, out_shape=outs, in_specs=[kinds[kind] for kind in sp...  8.93 us
    ppermute x2, waiting for transfers between devices, shifted(): lax.ppermute(value, axis, [(source, source + steps) for source in range(f...  8.18 us
    all_to_all x1, blocking collectives, per_device(): kv = lax.all_to_all(kv, 'tp', 0, 0, axis_index_groups=groups)  7.81 us
  transfers between devices with their start and end apart: 2, of which 2 were waited for; matrix products, arithmetic and copies ran while one was open for 0% of the time, Pallas kernels for 0%

profile of v4, /device:TPU:1, one launch (start us, length us, event | category | flops | bytes accessed | tf_op | source)
XLA Modules:
  0.0 151.5 jit_solution(11625873591746935827)
XLA Ops:
  0.6 0.0 copy-start.3
  0.7 0.8 copy-done.3
  1.5 0.9 copy-done.7
  2.4 0.2 shard_map.167
  2.6 0.0 copy-start
  2.6 0.0 copy-start.4
  2.6 0.0 copy-start.5
  2.6 0.0 copy-start.6
  2.6 0.0 copy-start.8
  2.7 0.0 copy-start.9
  2.7 0.0 copy-start.10
  2.7 0.0 copy-start.11
  2.7 0.0 copy-start.12
  2.7 44.0 %all_to_all.35.x_ref.got_ref = bf16[16,384,256]{2,1,0:T(8,128)(2,1)S(1)} all-to-all(bf16[16,384,256]{2,1,0:T(8,128)(2,1)S(1)} %shard_map.167), channel_id=1, replica_groups=mesh['pipe'=32,'tp'=16] {'tp'}, dimensions={0} | all-to-all | bytes 6291456 | tf_op jit(solution)/shard_map/all_to_all | solution.py:322
  46.8 0.0 copy-done
  46.8 0.0 copy-done.4
  46.8 0.0 copy-done.5
  46.8 0.0 copy-done.6
  46.8 0.0 copy-done.8
  46.8 0.0 copy-done.9
  46.8 0.0 copy-done.10
  46.8 0.0 copy-start.1
  46.8 2.0 %shard_map.168 = (bf16[2,128,256]{2,1,0:T(8,128)(2,1)S(1)}, bf16[4,2,64,128]{3,2,1,0:T(8,128)(2,1)S(1)}, f32[2,128,1]{2,1,0:T(8,128)S(1)}, f32[2,128,128]{2,1,0:...) custom-call(s32[1]{0:T(128)} %bitcast.1.place_ref, ...), custom_call_target="tpu_custom_call" | custom-call | tf_op jit(solution)/shard_map/pallas_call | solution.py:53
  48.9 7.8 %all_to_all.36.kv_ref = bf16[4,2,64,128]{3,2,1,0:T(8,128)(2,1)S(1)} all-to-all(bf16[4,2,64,128]{3,2,1,0:T(8,128)(2,1)S(1)} %get-tuple-element.26), channel_id=1, replica_groups={{0,1,2,3},{4,5,6,7},{8,9,10,11},{12,13,14,15},{16,17,18,19},{20,21,22,2..., dimensions={0} | all-to-all | bytes 262144 | tf_op jit(solution)/shard_map/all_to_all | solution.py:348
  56.7 1.8 %shard_map.169 = (bf16[128,256]{1,0:T(8,128)(2,1)S(1)}, bf16[4,64,128]{2,1,0:T(8,128)(2,1)S(1)}, f32[128,1]{1,0:T(8,128)S(1)}) custom-call(s32[1,2,4]{2,1,0:T(2,128)S(1)} %copy-done.12, bf16[16,384,256]{2,1,0:T(8,128)(2,1)S(1)} %all_to_all.35.x_ref.got_ref, bf16[256,4096]{1,0:T(8,128)(2,1)S(1)} %bitcast.23, ...), custom_call_target="tpu_custom_call" | custom-call | tf_op jit(solution)/shard_map/pallas_call | solution.py:53
  58.4 6.8 %all_to_all.37.dkv_ref = bf16[4,64,128]{2,1,0:T(8,128)(2,1)S(1)} all-to-all(bf16[4,64,128]{2,1,0:T(8,128)(2,1)S(1)} %get-tuple-element.30), channel_id=1, replica_groups={{0,1,2,3},{4,5,6,7},{8,9,10,11},{12,13,14,15},{16,17,18,19},{20,21,22,2..., dimensions={0} | all-to-all | bytes 131072 | tf_op jit(solution)/shard_map/all_to_all | solution.py:372
  65.3 1.2 shard_map.170
  66.5 0.0 copy-start.2
  66.5 0.0 copy-start.13
  66.5 0.0 copy-start.14
  66.6 0.0 copy-start.15
  66.6 15.4 %all_to_all.38 = bf16[16,128,256]{2,1,0:T(8,128)(2,1)S(1)} all-to-all(bf16[16,128,256]{2,1,0:T(8,128)(2,1)S(1)} %shard_map.170), channel_id=1, replica_groups=mesh['pipe'=32,'tp'=16] {'tp'}, dimensions={0} | all-to-all | bytes 2097152 | tf_op jit(solution)/shard_map/all_to_all | solution.py:322
  82.0 0.1 convert_reduce_fusion.1
  82.1 8.9 %collective-permute-start = (bf16[128,256]{1,0:T(8,128)(2,1)S(1)}, bf16[128,256]{1,0:T(8,128)(2,1)S(1)}, u32[]{:S(2)}, u32[]{:S(2)}) collective-permute-start(bf16[128,256]{1,0:T(8,128)(2,1)S(1)} %fusion), channel_id=1, source_target_pairs={{16,0},{32,16},{48,32},{64,48},{80,64},{96,80},{112,96},{128,112},... | collective-permute-start | bytes 196616 | tf_op jit(solution)/shard_map/ppermute | solution.py:271
  91.0 4.0 %collective-permute-done.received_ref = bf16[128,256]{1,0:T(8,128)(2,1)S(1)} collective-permute-done((bf16[128,256]{1,0:T(8,128)(2,1)S(1)}, bf16[128,256]{1,0:T(8,128)(2,1)S(1)}, u32[]{:S(2)}, u32[]{:S(2)}) %collective-permute-start) | collective-permute-done | bytes 65568 | tf_op jit(solution)/shard_map/ppermute | solution.py:271
  95.0 0.0 copy-done.2
  95.0 0.0 copy-done.14
  95.0 0.1 shard_map.171
  95.1 18.3 %all_to_all.39.got_ref = bf16[16,128,256]{2,1,0:T(8,128)(2,1)S(1)} all-to-all(bf16[16,128,256]{2,1,0:T(8,128)(2,1)S(1)} %get-tuple-element.40), channel_id=1, replica_groups=mesh['pipe'=32,'tp'=16] {'tp'}, dimensions={0} | all-to-all | bytes 2097152 | tf_op jit(solution)/shard_map/all_to_all | solution.py:322
  113.4 1.8 %shard_map.172 = (bf16[128,256]{1,0:T(8,128)(2,1)S(1)}, bf16[4,64,128]{2,1,0:T(8,128)(2,1)S(1)}, f32[128,1]{1,0:T(8,128)S(1)}) custom-call(s32[1,2,4]{2,1,0:T(2,128)S(1)} %copy-done.12, bf16[16,128,256]{2,1,0:T(8,128)(2,1)S(1)} %all_to_all.39.got_ref, bf16[256,4096]{1,0:T(8,128)(2,1)S(1)} %bitcast.24, bf16[2,128,256]{2,1,0:T(8,128)(2,1)S(1)} %get-tuple-element.25.q_ref, ...), custom_call_target="tpu_custom_call" | custom-call | tf_op jit(solution)/shard_map/pallas_call | solution.py:53
  115.2 6.8 %all_to_all.40.dkv_ref = bf16[4,64,128]{2,1,0:T(8,128)(2,1)S(1)} all-to-all(bf16[4,64,128]{2,1,0:T(8,128)(2,1)S(1)} %get-tuple-element.42), channel_id=1, replica_groups={{0,1,2,3},{4,5,6,7},{8,9,10,11},{12,13,14,15},{16,17,18,19},{20,21,22,2..., dimensions={0} | all-to-all | bytes 131072 | tf_op jit(solution)/shard_map/all_to_all | solution.py:372
  122.0 1.2 shard_map.173
  123.3 18.5 %all_to_all.41 = bf16[16,128,256]{2,1,0:T(8,128)(2,1)S(1)} all-to-all(bf16[16,128,256]{2,1,0:T(8,128)(2,1)S(1)} %shard_map.173), channel_id=1, replica_groups=mesh['pipe'=32,'tp'=16] {'tp'}, dimensions={0} | all-to-all | bytes 2097152 | tf_op jit(solution)/shard_map/all_to_all | solution.py:322
  141.7 0.1 convert_reduce_fusion
  141.9 4.1 %collective-permute-start.1 = (bf16[128,256]{1,0:T(8,128)(2,1)S(1)}, bf16[128,256]{1,0:T(8,128)(2,1)S(1)}, u32[]{:S(2)}, u32[]{:S(2)}) collective-permute-start(bf16[128,256]{1,0:T(8,128)(2,1)S(1)} %add_convert_fusion), channel_id=1, source_target_pairs={{16,0},{32,16},{48,32},{64,48},{80,64},{96,80},{112,96},{128,112},... | collective-permute-start | bytes 196616 | tf_op jit(solution)/shard_map/ppermute | solution.py:271
  146.0 0.7 maximum_bitcast_fusion
  146.7 4.2 %collective-permute-done.1.received_ref = bf16[128,256]{1,0:T(8,128)(2,1)S(1)} collective-permute-done((bf16[128,256]{1,0:T(8,128)(2,1)S(1)}, bf16[128,256]{1,0:T(8,128)(2,1)S(1)}, u32[]{:S(2)}, u32[]{:S(2)}) %collective-permute-start.1) | collective-permute-done | bytes 65568 | tf_op jit(solution)/shard_map/ppermute | solution.py:271
  150.9 0.6 shard_map.174
  (8 shorter events, 0.0 us)
Async XLA Ops:
  0.6 0.8 copy-start.3
  1.5 0.9 copy-start.7
  2.6 44.2 %copy-start = (bf16[1,4096,256]{2,1,0:T(8,128)(2,1)S(1)}, bf16[1,4096,256]{2,1,0:T(8,128)(2,1)}, u32[]{:S(2)}) copy-start(bf16[1,4096,256]{2,1,0:T(8,128)(2,1)} %param.19) | copy-start | bytes 6291460
  2.6 44.2 %copy-start.4 = (bf16[1,4096,32]{1,2,0:T(8,128)(2,1)S(1)}, bf16[1,4096,32]{1,2,0:T(8,128)(2,1)}, u32[]{:S(2)}) copy-start(bf16[1,4096,32]{1,2,0:T(8,128)(2,1)} %param.20) | copy-start | bytes 786436
  2.6 44.1 %copy-start.5 = (bf16[1,4096,32]{1,2,0:T(8,128)(2,1)S(1)}, bf16[1,4096,32]{1,2,0:T(8,128)(2,1)}, u32[]{:S(2)}) copy-start(bf16[1,4096,32]{1,2,0:T(8,128)(2,1)} %param.21) | copy-start | bytes 786436
  2.6 44.1 %copy-start.6 = (bf16[1,4096]{1,0:T(2,128)(2,1)S(1)}, bf16[1,4096]{1,0:T(2,128)(2,1)}, u32[]{:S(2)}) copy-start(bf16[1,4096]{1,0:T(2,128)(2,1)} %gain_ref.5) | copy-start | bytes 24580
  2.6 44.1 %copy-start.8 = (bf16[3,128,128]{2,1,0:T(8,128)(2,1)S(1)}, bf16[3,128,128]{2,1,0:T(8,128)(2,1)}, u32[]{:S(2)}) copy-start(bf16[3,128,128]{2,1,0:T(8,128)(2,1)} %constant.37.clone.stabt_ref) | copy-start | bytes 294916
  2.7 44.1 %copy-start.9 = (bf16[3,128,128]{2,1,0:T(8,128)(2,1)S(1)}, bf16[3,128,128]{2,1,0:T(8,128)(2,1)}, u32[]{:S(2)}) copy-start(bf16[3,128,128]{2,1,0:T(8,128)(2,1)} %constant.36.clone.ctabt_ref) | copy-start | bytes 294916
  2.7 44.1 %copy-start.10 = (bf16[3,128,128]{2,1,0:T(8,128)(2,1)S(1)}, bf16[3,128,128]{2,1,0:T(8,128)(2,1)}, u32[]{:S(2)}) copy-start(bf16[3,128,128]{2,1,0:T(8,128)(2,1)} %constant.35.clone.stab_ref) | copy-start | bytes 294916
  2.7 44.1 %copy-start.11 = (bf16[3,128,128]{2,1,0:T(8,128)(2,1)S(1)}, bf16[3,128,128]{2,1,0:T(8,128)(2,1)}, u32[]{:S(2)}) copy-start(bf16[3,128,128]{2,1,0:T(8,128)(2,1)} %constant.34.clone.ctab_ref) | copy-start | bytes 294916
  2.7 44.1 %copy-start.12 = (s32[1,2,4]{2,1,0:T(2,128)S(1)}, s32[1,2,4]{2,1,0:T(2,128)}, u32[]{:S(2)}) copy-start(s32[1,2,4]{2,1,0:T(2,128)} %seg_ref.5) | copy-start | bytes 100
  46.8 9.8 %copy-start.1 = (bf16[1,256,4096]{2,1,0:T(8,128)(2,1)S(1)}, bf16[1,256,4096]{2,1,0:T(8,128)(2,1)}, u32[]{:S(2)}) copy-start(bf16[1,256,4096]{2,1,0:T(8,128)(2,1)} %param.22) | copy-start | bytes 6291460
  66.5 28.5 %copy-start.2 = (bf16[2,128,256]{2,1,0:T(8,128)(2,1)S(1)}, bf16[2,128,256]{2,1,0:T(8,128)(2,1)}, u32[]{:S(2)}) copy-start(bf16[2,128,256]{2,1,0:T(8,128)(2,1)} %score_ref.3) | copy-start | bytes 393220
  66.5 28.5 %copy-start.13 = (f32[512]{0:T(512)S(1)}, f32[512]{0:T(512)}, u32[]{:S(2)}) copy-start(f32[512]{0:T(512)} %param.25) | copy-start | bytes 6148
  66.5 28.5 %copy-start.14 = (s32[512]{0:T(512)S(1)}, s32[512]{0:T(512)}, u32[]{:S(2)}) copy-start(s32[512]{0:T(512)} %param.26) | copy-start | bytes 6148
  66.6 28.5 %copy-start.15 = (s32[2,128]{1,0:T(2,128)S(1)}, s32[2,128]{1,0:T(2,128)}, u32[]{:S(2)}) copy-start(s32[2,128]{1,0:T(2,128)} %sample_ref.3) | copy-start | bytes 3076
  82.1 12.9 %collective-permute-start = (bf16[128,256]{1,0:T(8,128)(2,1)S(1)}, bf16[128,256]{1,0:T(8,128)(2,1)S(1)}, u32[]{:S(2)}, u32[]{:S(2)}) collective-permute-start(bf16[128,256]{1,0:T(8,128)(2,1)S(1)} %fusion), channel_id=1, source_target_pairs={{16,0},{32,16},{48,32},{64,48},{80,64},{96,80},{112,96},{128,112},... | collective-permute-start | bytes 196616 | tf_op jit(solution)/shard_map/ppermute | solution.py:271
  141.9 9.0 %collective-permute-start.1 = (bf16[128,256]{1,0:T(8,128)(2,1)S(1)}, bf16[128,256]{1,0:T(8,128)(2,1)S(1)}, u32[]{:S(2)}, u32[]{:S(2)}) collective-permute-start(bf16[128,256]{1,0:T(8,128)(2,1)S(1)} %add_convert_fusion), channel_id=1, source_target_pairs={{16,0},{32,16},{48,32},{64,48},{80,64},{96,80},{112,96},{128,112},... | collective-permute-start | bytes 196616 | tf_op jit(solution)/shard_map/ppermute | solution.py:271

commit v5 on v4

--- a/solution.py
+++ b/solution.py
@@ -82,6 +82,16 @@
     return jnp.where(column == row - begin, 1.0, 0.0).astype(BF16)
 
 
+def located(odd_ref, block, share):
+    across = block % share * share + block // share
+    return jnp.where(odd_ref[0] > 0, across, block)
+
+
+def relay_body(got_ref, out_ref):
+    for i in range(out_ref.shape[0]):
+        out_ref[i] = got_ref[...]
+
+
 def spread_body(saved_ref, grad_ref, out_ref):
     for i in range(out_ref.shape[0]):
         for tick in range(TICKS):
@@ -91,6 +101,7 @@
 
 def forward_body(
     place_ref,
+    odd_ref,
     seg_ref,
     wq_ref,
     wk_ref,
@@ -118,14 +129,15 @@
     own = pl.ds(pl.multiple_of(place_ref[0] * half, half), half)
     squares = jnp.zeros((rows, width), F32)
     for j in range(blocks):
-        xj = x_ref[j, :rows].astype(F32)
+        xj = x_ref[located(odd_ref, j, kv_ref.shape[0]), :rows].astype(F32)
         squares = squares + xj * xj
     inverse = lax.rsqrt(jnp.sum(squares, axis=1, keepdims=True) * (1.0 / D) + EPS)
     query = jnp.zeros((rows, wq_ref.shape[1]), F32)
     kvt = jnp.zeros((2 * half, rows), F32)
     for j in range(blocks):
         part = slice(j * width, (j + 1) * width)
-        normed = x_ref[j, :rows].astype(F32) * inverse * gain_ref[:, part].astype(F32)
+        xj = x_ref[located(odd_ref, j, kv_ref.shape[0]), :rows].astype(F32)
+        normed = xj * inverse * gain_ref[:, part].astype(F32)
         normed = normed.astype(BF16)
         query = query + nn(normed, wq_ref[part, :])
         kvt = kvt + nt(wkv_ref[:, part], normed)
@@ -191,7 +203,7 @@
 
 
 def attention_body(
-    tick, got_at, seg_ref, got_ref, wo_ref, q_ref, kv_ref, cos_ref, sin_ref, dq_ref, dkv_ref, t_ref
+    tick, got_at, odd_ref, seg_ref, got_ref, wo_ref, q_ref, kv_ref, cos_ref, sin_ref, dq_ref, dkv_ref, t_ref
 ):
     blocks, _, width = got_ref.shape
     shares, half = dkv_ref.shape[0], dkv_ref.shape[1] // 2
@@ -205,7 +217,9 @@
         allowed = allowed & ((row < start) | (column >= start))
     dout = jnp.zeros(dq_ref.shape, F32)
     for j in range(blocks):
-        dout = dout + nt(got_ref[j, got_at : got_at + ROWS], wo_ref[:, j * width : (j + 1) * width])
+        at = located(odd_ref, j, shares) if tick == 0 else j
+        dout = dout + nt(
+            got_ref[at, got_at : got_at + ROWS], wo_ref[:, j * width : (j + 1) * width])
     dout = dout.astype(BF16)
     dkeys = jnp.zeros((HD, ROWS), F32)
     dvalues = jnp.zeros((HD, ROWS), F32)
@@ -234,6 +248,7 @@
 
 def partial_body(
     tick,
+    odd_ref,
     x_ref,
     dq_ref,
     dkv_ref,
@@ -262,7 +277,9 @@
         part = slice(j * width, (j + 1) * width)
         total = nt(dq, wq_ref[part, :]) + nn(dkv, wkv_ref[:, part])
         scaled = total * (inverse * gain_ref[:, part].astype(F32))
-        out_ref[j] = (scaled - x_ref[j, tick * ROWS : (tick + 1) * ROWS].astype(F32) * along).astype(BF16)
+        at = located(odd_ref, j, dkv_ref.shape[0])
+        xj = x_ref[at, tick * ROWS : (tick + 1) * ROWS].astype(F32)
+        out_ref[j] = (scaled - xj * along).astype(BF16)
 
 
 def shifted(value, axis, steps):
@@ -322,9 +339,33 @@
         return lax.all_to_all(rows, "tp", 0, 0)
 
     last_flag = last_section.astype(jnp.int32)[None]
-    saved, place, last_flag = lax.optimization_barrier((saved, place, last_flag))
-    (spread,) = kernel_call(spread_body, blocks_of((TICKS + 1) * ROWS), "vv", (saved, incoming))
-    first = exchange(spread)
+    odd = (lax.axis_index("pipe") % 2).astype(jnp.int32)[None]
+    saved, place, odd, last_flag = lax.optimization_barrier((saved, place, odd, last_flag))
+    def stage(blocks, along):
+        lines = []
+        for section in range(lax.axis_size("pipe")):
+            for line in range(share):
+                chosen = [
+                    line * share + i if (section + along) % 2 == 0 else i * share + line
+                    for i in range(share)
+                ]
+                lines.append([section * tp_count + member for member in chosen])
+        return lax.all_to_all(blocks, ("pipe", "tp"), 0, 0, axis_index_groups=lines)
+
+    rows_in = (TICKS + 1) * ROWS
+    (spread,) = kernel_call(
+        spread_body,
+        (jax.ShapeDtypeStruct((share, rows_in, width), BF16),),
+        "vv",
+        (saved, incoming),
+    )
+    (relay,) = kernel_call(
+        relay_body,
+        (jax.ShapeDtypeStruct((share, share, rows_in, width), BF16),),
+        "v",
+        (stage(spread, 0),),
+    )
+    first = stage(relay, 1).reshape(tp_count, rows_in, width)
 
     def chooser(received):
         return (last_flag, received, score_grad, rewards[None], sample_group[None], head_sample)
@@ -342,8 +383,8 @@
             jax.ShapeDtypeStruct((TICKS, kv_share, ROWS), F32),
             jax.ShapeDtypeStruct((2 * kv_share, wk.shape[1]), BF16),
         ),
-        "s" + "v" * 10,
-        (place, seg_lengths, wq, wk, wv, gain, *tables, first),
+        "ss" + "v" * 10,
+        (place, odd, seg_lengths, wq, wk, wv, gain, *tables, first),
     )
     kv = lax.all_to_all(kv, "tp", 0, 0, axis_index_groups=groups)
 
@@ -366,15 +407,15 @@
                 jax.ShapeDtypeStruct((share, 2 * kv_share, ROWS), BF16),
                 jax.ShapeDtypeStruct((ROWS, 1), F32),
             ),
-            "v" * 7,
-            (seg_lengths, got, wo, query, kv, cos, sin),
+            "s" + "v" * 7,
+            (odd, seg_lengths, got, wo, query, kv, cos, sin),
         )
         dkv = lax.all_to_all(dkv, "tp", 0, 0, axis_index_groups=groups)
         (blocks,) = kernel_call(
             functools.partial(partial_body, tick),
             blocks_of(ROWS),
-            "v" * 10,
-            (first, dquery, dkv, wq, wkv, gain, inverse, along, cos_t, sin_t),
+            "s" + "v" * 10,
+            (odd, first, dquery, dkv, wq, wkv, gain, inverse, along, cos_t, sin_t),
         )
         blocks = exchange(blocks)
         total = jnp.sum(blocks.astype(F32), axis=0)

time: 153 us -> 145 us (0.948)
  blocking collectives: 118 us -> 110 us
  starting transfers between devices: 13 us -> 17.1 us
  waiting for transfers between devices: 8.18 us -> 4.21 us
    all_to_all x4 -> x3, blocking collectives: 96.2 us -> 51.1 us  [exchange(): return lax.all_to_all(rows, 'tp', 0, 0)]
    all_to_all x0 -> x2, blocking collectives: none -> 38.4 us  [stage(): return lax.all_to_all(blocks, ('pipe', 'tp'), 0, 0, axis_index_groups=lines)]
    ppermute x2, starting transfers between devices: 13 us -> 17.1 us  [shifted(): lax.ppermute(value, axis, [(source, source + steps) for source in range(f...]
    ppermute x2, waiting for transfers between devices: 8.18 us -> 4.21 us  [shifted(): lax.ppermute(value, axis, [(source, source + steps) for source in range(f...]
    pallas_call x8 -> x9, Pallas kernels: 8.93 us -> 9.01 us  [kernel_call(): pl.pallas_call(body, out_shape=outs, in_specs=[kinds[kind] for kind in sp...]
where the time goes in v5:
time: 145 us; the launch traced here: 144 us
  blocking collectives  110 us (76%)
  starting transfers between devices  17.1 us (12%)
  Pallas kernels  9.01 us (6%)
  waiting for transfers between devices  4.21 us (3%)
  local copies, waits for them, and re-layouts  1.83 us (1%)
    all_to_all x3, blocking collectives, exchange(): return lax.all_to_all(rows, 'tp', 0, 0)  51.1 us
    all_to_all x2, blocking collectives, stage(): return lax.all_to_all(blocks, ('pipe', 'tp'), 0, 0, axis_index_groups=lines)  38.4 us
    ppermute x2, starting transfers between devices, shifted(): lax.ppermute(value, axis, [(source, source + steps) for source in range(f...  17.1 us
    all_to_all x2, blocking collectives, per_device(): dkv = lax.all_to_all(dkv, 'tp', 0, 0, axis_index_groups=groups)  13.7 us
    pallas_call x9, Pallas kernels, kernel_call(): pl.pallas_call(body, out_shape=outs, in_specs=[kinds[kind] for kind in sp...  9.01 us
    all_to_all x1, blocking collectives, per_device(): kv = lax.all_to_all(kv, 'tp', 0, 0, axis_index_groups=groups)  7.2 us
    ppermute x2, waiting for transfers between devices, shifted(): lax.ppermute(value, axis, [(source, source + steps) for source in range(f...  4.21 us
  transfers between devices with their start and end apart: 2, of which 2 were waited for; matrix products, arithmetic and copies ran while one was open for 0% of the time, Pallas kernels for 0%

profile of v5, /device:TPU:1, one launch (start us, length us, event | category | flops | bytes accessed | tf_op | source)
XLA Modules:
  0.0 144.4 jit_solution(14644511127939927552)
XLA Ops:
  0.7 0.8 copy-done.5
  1.5 0.9 copy-done.7
  2.4 0.1 shard_map.167
  2.5 13.0 %all_to_all.40.got_ref = bf16[4,384,256]{2,1,0:T(8,128)(2,1)S(1)} all-to-all(bf16[4,384,256]{2,1,0:T(8,128)(2,1)S(1)} %shard_map.167), channel_id=1, replica_groups={{0,1,2,3},{4,5,6,7},{8,9,10,11},{12,13,14,15},{16,20,24,28},{17,21,25,2..., dimensions={0} | all-to-all | bytes 1572864 | tf_op jit(solution)/shard_map/all_to_all | solution.py:353
  15.4 0.2 shard_map.168
  15.6 0.0 copy-start
  15.7 0.0 copy-start.3
  15.7 0.0 copy-start.4
  15.7 0.0 copy-start.6
  15.7 0.0 copy-start.8
  15.7 0.0 copy-start.9
  15.7 0.0 copy-start.10
  15.7 0.0 copy-start.11
  15.7 0.0 copy-start.12
  15.8 25.4 %all_to_all.41 = bf16[4,4,384,256]{3,2,1,0:T(8,128)(2,1)S(1)} all-to-all(bf16[4,4,384,256]{3,2,1,0:T(8,128)(2,1)S(1)} %shard_map.168), channel_id=1, replica_groups={{0,4,8,12},{1,5,9,13},{2,6,10,14},{3,7,11,15},{16,17,18,19},{20,21,22,2..., dimensions={0} | all-to-all | bytes 6291456 | tf_op jit(solution)/shard_map/all_to_all | solution.py:353
  41.2 0.0 copy-done.6
  41.2 0.0 copy-done.8
  41.2 0.0 copy-done.9
  41.2 0.0 copy-done.10
  41.2 0.0 copy-done.11
  41.2 0.0 copy-done.12
  41.2 0.0 copy-start.1
  41.2 2.0 %shard_map.169 = (bf16[2,128,256]{2,1,0:T(8,128)(2,1)S(1)}, bf16[4,2,64,128]{3,2,1,0:T(8,128)(2,1)S(1)}, f32[2,128,1]{2,1,0:T(8,128)S(1)}, f32[2,128,128]{2,1,0:...) custom-call(s32[1]{0:T(128)} %bitcast.1.place_ref, ...), custom_call_target="tpu_custom_call" | custom-call | tf_op jit(solution)/shard_map/pallas_call | solution.py:53
  43.2 7.2 %all_to_all.42.kv_ref = bf16[4,2,64,128]{3,2,1,0:T(8,128)(2,1)S(1)} all-to-all(bf16[4,2,64,128]{3,2,1,0:T(8,128)(2,1)S(1)} %get-tuple-element.28), channel_id=1, replica_groups={{0,1,2,3},{4,5,6,7},{8,9,10,11},{12,13,14,15},{16,17,18,19},{20,21,22,2..., dimensions={0} | all-to-all | bytes 262144 | tf_op jit(solution)/shard_map/all_to_all | solution.py:389
  50.4 0.0 copy-done.1
  50.4 1.8 %shard_map.170 = (bf16[128,256]{1,0:T(8,128)(2,1)S(1)}, bf16[4,64,128]{2,1,0:T(8,128)(2,1)S(1)}, f32[128,1]{1,0:T(8,128)S(1)}) custom-call(s32[1]{0:T(128)} %bitcast.2.odd_ref, s32[1,2,4]{2,1,0:T(2,128)S(1)} %copy-done.12, bf16[16,384,256]{2,1,0:T(8,128)(2,1)S(1)} %bitcast.23, bf16[256,4096]{1,0:T(8,128)(2,1)S(1)} %bitcast.29, ...), custom_call_target="tpu_custom_call" | custom-call | tf_op jit(solution)/shard_map/pallas_call | solution.py:53
  52.2 6.8 %all_to_all.43.dkv_ref = bf16[4,64,128]{2,1,0:T(8,128)(2,1)S(1)} all-to-all(bf16[4,64,128]{2,1,0:T(8,128)(2,1)S(1)} %get-tuple-element.32), channel_id=1, replica_groups={{0,1,2,3},{4,5,6,7},{8,9,10,11},{12,13,14,15},{16,17,18,19},{20,21,22,2..., dimensions={0} | all-to-all | bytes 131072 | tf_op jit(solution)/shard_map/all_to_all | solution.py:413
  59.1 1.2 shard_map.171
  60.3 0.0 copy-start.2
  60.3 0.0 copy-start.13
  60.3 0.0 copy-start.14
  60.3 0.0 copy-start.15
  60.3 14.6 %all_to_all.44 = bf16[16,128,256]{2,1,0:T(8,128)(2,1)S(1)} all-to-all(bf16[16,128,256]{2,1,0:T(8,128)(2,1)S(1)} %shard_map.171), channel_id=1, replica_groups=mesh['pipe'=32,'tp'=16] {'tp'}, dimensions={0} | all-to-all | bytes 2097152 | tf_op jit(solution)/shard_map/all_to_all | solution.py:339
  74.9 0.1 convert_reduce_fusion.1
  75.1 10.9 %collective-permute-start = (bf16[128,256]{1,0:T(8,128)(2,1)S(1)}, bf16[128,256]{1,0:T(8,128)(2,1)S(1)}, u32[]{:S(2)}, u32[]{:S(2)}) collective-permute-start(bf16[128,256]{1,0:T(8,128)(2,1)S(1)} %fusion), channel_id=1, source_target_pairs={{16,0},{32,16},{48,32},{64,48},{80,64},{96,80},{112,96},{128,112},... | collective-permute-start | bytes 196616 | tf_op jit(solution)/shard_map/ppermute | solution.py:288
  86.0 1.5 %collective-permute-done.received_ref = bf16[128,256]{1,0:T(8,128)(2,1)S(1)} collective-permute-done((bf16[128,256]{1,0:T(8,128)(2,1)S(1)}, bf16[128,256]{1,0:T(8,128)(2,1)S(1)}, u32[]{:S(2)}, u32[]{:S(2)}) %collective-permute-start) | collective-permute-done | bytes 65568 | tf_op jit(solution)/shard_map/ppermute | solution.py:288
  87.6 0.0 copy-done.13
  87.6 0.1 shard_map.172
  87.7 19.6 %all_to_all.45.got_ref = bf16[16,128,256]{2,1,0:T(8,128)(2,1)S(1)} all-to-all(bf16[16,128,256]{2,1,0:T(8,128)(2,1)S(1)} %get-tuple-element.42), channel_id=1, replica_groups=mesh['pipe'=32,'tp'=16] {'tp'}, dimensions={0} | all-to-all | bytes 2097152 | tf_op jit(solution)/shard_map/all_to_all | solution.py:339
  107.3 1.8 %shard_map.173 = (bf16[128,256]{1,0:T(8,128)(2,1)S(1)}, bf16[4,64,128]{2,1,0:T(8,128)(2,1)S(1)}, f32[128,1]{1,0:T(8,128)S(1)}) custom-call(s32[1]{0:T(128)} %bitcast.2.odd_ref, s32[1,2,4]{2,1,0:T(2,128)S(1)} %copy-done.12, bf16[16,128,256]{2,1,0:T(8,128)(2,1)S(1)} %all_to_all.45.got_ref, bf16[256,4096]{1,0:T(8,128)(2,1)S(1)} %bitcast.30, ...), custom_call_target="tpu_custom_call" | custom-call | tf_op jit(solution)/shard_map/pallas_call | solution.py:53
  109.0 6.8 %all_to_all.46.dkv_ref = bf16[4,64,128]{2,1,0:T(8,128)(2,1)S(1)} all-to-all(bf16[4,64,128]{2,1,0:T(8,128)(2,1)S(1)} %get-tuple-element.44), channel_id=1, replica_groups={{0,1,2,3},{4,5,6,7},{8,9,10,11},{12,13,14,15},{16,17,18,19},{20,21,22,2..., dimensions={0} | all-to-all | bytes 131072 | tf_op jit(solution)/shard_map/all_to_all | solution.py:413
  115.9 1.2 shard_map.174
  117.1 17.0 %all_to_all.47 = bf16[16,128,256]{2,1,0:T(8,128)(2,1)S(1)} all-to-all(bf16[16,128,256]{2,1,0:T(8,128)(2,1)S(1)} %shard_map.174), channel_id=1, replica_groups=mesh['pipe'=32,'tp'=16] {'tp'}, dimensions={0} | all-to-all | bytes 2097152 | tf_op jit(solution)/shard_map/all_to_all | solution.py:339
  134.1 0.1 convert_reduce_fusion
  134.3 6.1 %collective-permute-start.1 = (bf16[128,256]{1,0:T(8,128)(2,1)S(1)}, bf16[128,256]{1,0:T(8,128)(2,1)S(1)}, u32[]{:S(2)}, u32[]{:S(2)}) collective-permute-start(bf16[128,256]{1,0:T(8,128)(2,1)S(1)} %add_convert_fusion), channel_id=1, source_target_pairs={{16,0},{32,16},{48,32},{64,48},{80,64},{96,80},{112,96},{128,112},... | collective-permute-start | bytes 196616 | tf_op jit(solution)/shard_map/ppermute | solution.py:288
  140.4 0.7 maximum_bitcast_fusion
  141.1 2.7 %collective-permute-done.1.received_ref = bf16[128,256]{1,0:T(8,128)(2,1)S(1)} collective-permute-done((bf16[128,256]{1,0:T(8,128)(2,1)S(1)}, bf16[128,256]{1,0:T(8,128)(2,1)S(1)}, u32[]{:S(2)}, u32[]{:S(2)}) %collective-permute-start.1) | collective-permute-done | bytes 65568 | tf_op jit(solution)/shard_map/ppermute | solution.py:288
  143.8 0.6 shard_map.175
  (10 shorter events, 0.0 us)
Async XLA Ops:
  0.7 0.8 copy-start.5
  1.5 0.9 copy-start.7
  15.6 25.5 %copy-start = (bf16[1,4096,256]{2,1,0:T(8,128)(2,1)S(1)}, bf16[1,4096,256]{2,1,0:T(8,128)(2,1)}, u32[]{:S(2)}) copy-start(bf16[1,4096,256]{2,1,0:T(8,128)(2,1)} %param.19) | copy-start | bytes 6291460
  15.7 25.5 %copy-start.3 = (bf16[1,4096,32]{1,2,0:T(8,128)(2,1)S(1)}, bf16[1,4096,32]{1,2,0:T(8,128)(2,1)}, u32[]{:S(2)}) copy-start(bf16[1,4096,32]{1,2,0:T(8,128)(2,1)} %param.20) | copy-start | bytes 786436
  15.7 25.5 %copy-start.4 = (bf16[1,4096,32]{1,2,0:T(8,128)(2,1)S(1)}, bf16[1,4096,32]{1,2,0:T(8,128)(2,1)}, u32[]{:S(2)}) copy-start(bf16[1,4096,32]{1,2,0:T(8,128)(2,1)} %param.21) | copy-start | bytes 786436
  15.7 25.5 %copy-start.6 = (bf16[1,4096]{1,0:T(2,128)(2,1)S(1)}, bf16[1,4096]{1,0:T(2,128)(2,1)}, u32[]{:S(2)}) copy-start(bf16[1,4096]{1,0:T(2,128)(2,1)} %gain_ref.5) | copy-start | bytes 24580
  15.7 25.5 %copy-start.8 = (bf16[3,128,128]{2,1,0:T(8,128)(2,1)S(1)}, bf16[3,128,128]{2,1,0:T(8,128)(2,1)}, u32[]{:S(2)}) copy-start(bf16[3,128,128]{2,1,0:T(8,128)(2,1)} %constant.47.clone.stabt_ref) | copy-start | bytes 294916
  15.7 25.5 %copy-start.9 = (bf16[3,128,128]{2,1,0:T(8,128)(2,1)S(1)}, bf16[3,128,128]{2,1,0:T(8,128)(2,1)}, u32[]{:S(2)}) copy-start(bf16[3,128,128]{2,1,0:T(8,128)(2,1)} %constant.46.clone.ctabt_ref) | copy-start | bytes 294916
  15.7 25.5 %copy-start.10 = (bf16[3,128,128]{2,1,0:T(8,128)(2,1)S(1)}, bf16[3,128,128]{2,1,0:T(8,128)(2,1)}, u32[]{:S(2)}) copy-start(bf16[3,128,128]{2,1,0:T(8,128)(2,1)} %constant.45.clone.stab_ref) | copy-start | bytes 294916
  15.7 25.5 %copy-start.11 = (bf16[3,128,128]{2,1,0:T(8,128)(2,1)S(1)}, bf16[3,128,128]{2,1,0:T(8,128)(2,1)}, u32[]{:S(2)}) copy-start(bf16[3,128,128]{2,1,0:T(8,128)(2,1)} %constant.44.clone.ctab_ref) | copy-start | bytes 294916
  15.7 25.5 %copy-start.12 = (s32[1,2,4]{2,1,0:T(2,128)S(1)}, s32[1,2,4]{2,1,0:T(2,128)}, u32[]{:S(2)}) copy-start(s32[1,2,4]{2,1,0:T(2,128)} %seg_ref.5) | copy-start | bytes 100
  41.2 9.2 %copy-start.1 = (bf16[1,256,4096]{2,1,0:T(8,128)(2,1)S(1)}, bf16[1,256,4096]{2,1,0:T(8,128)(2,1)}, u32[]{:S(2)}) copy-start(bf16[1,256,4096]{2,1,0:T(8,128)(2,1)} %param.22) | copy-start | bytes 6291460
  60.3 27.3 %copy-start.2 = (bf16[2,128,256]{2,1,0:T(8,128)(2,1)S(1)}, bf16[2,128,256]{2,1,0:T(8,128)(2,1)}, u32[]{:S(2)}) copy-start(bf16[2,128,256]{2,1,0:T(8,128)(2,1)} %score_ref.3) | copy-start | bytes 393220
  60.3 27.2 %copy-start.13 = (f32[512]{0:T(512)S(1)}, f32[512]{0:T(512)}, u32[]{:S(2)}) copy-start(f32[512]{0:T(512)} %param.25) | copy-start | bytes 6148
  60.3 27.2 %copy-start.14 = (s32[512]{0:T(512)S(1)}, s32[512]{0:T(512)}, u32[]{:S(2)}) copy-start(s32[512]{0:T(512)} %param.26) | copy-start | bytes 6148
  60.3 27.2 %copy-start.15 = (s32[2,128]{1,0:T(2,128)S(1)}, s32[2,128]{1,0:T(2,128)}, u32[]{:S(2)}) copy-start(s32[2,128]{1,0:T(2,128)} %sample_ref.3) | copy-start | bytes 3076
  75.1 12.5 %collective-permute-start = (bf16[128,256]{1,0:T(8,128)(2,1)S(1)}, bf16[128,256]{1,0:T(8,128)(2,1)S(1)}, u32[]{:S(2)}, u32[]{:S(2)}) collective-permute-start(bf16[128,256]{1,0:T(8,128)(2,1)S(1)} %fusion), channel_id=1, source_target_pairs={{16,0},{32,16},{48,32},{64,48},{80,64},{96,80},{112,96},{128,112},... | collective-permute-start | bytes 196616 | tf_op jit(solution)/shard_map/ppermute | solution.py:288
  134.3 9.5 %collective-permute-start.1 = (bf16[128,256]{1,0:T(8,128)(2,1)S(1)}, bf16[128,256]{1,0:T(8,128)(2,1)S(1)}, u32[]{:S(2)}, u32[]{:S(2)}) collective-permute-start(bf16[128,256]{1,0:T(8,128)(2,1)S(1)} %add_convert_fusion), channel_id=1, source_target_pairs={{16,0},{32,16},{48,32},{64,48},{80,64},{96,80},{112,96},{128,112},... | collective-permute-start | bytes 196616 | tf_op jit(solution)/shard_map/ppermute | solution.py:288

commit v6 on v5

--- a/solution.py
+++ b/solution.py
@@ -92,11 +92,16 @@
         out_ref[i] = got_ref[...]
 
 
-def spread_body(saved_ref, grad_ref, out_ref):
+def spread_body(rows_ref, out_ref):
     for i in range(out_ref.shape[0]):
-        for tick in range(TICKS):
-            out_ref[i, tick * ROWS : (tick + 1) * ROWS] = saved_ref[0, tick]
-        out_ref[i, TICKS * ROWS :] = grad_ref[0]
+        out_ref[i] = rows_ref[...]
+
+
+def rotate_heads(query, cos, sin, q_ref):
+    for h in range(query.shape[1] // HD):
+        cols = slice(h * HD, (h + 1) * HD)
+        head = query[:, cols]
+        q_ref[:, cols] = (head * cos + pair_swap(head, 1) * sin).astype(BF16)
 
 
 def forward_body(
@@ -126,21 +131,24 @@
     wkv_ref[half:] = wv_ref[...]
     blocks, _, width = x_ref.shape
     rows = TICKS * ROWS
+    q_rows = ROWS
     own = pl.ds(pl.multiple_of(place_ref[0] * half, half), half)
     squares = jnp.zeros((rows, width), F32)
-    for j in range(blocks):
-        xj = x_ref[located(odd_ref, j, kv_ref.shape[0]), :rows].astype(F32)
-        squares = squares + xj * xj
-    inverse = lax.rsqrt(jnp.sum(squares, axis=1, keepdims=True) * (1.0 / D) + EPS)
-    query = jnp.zeros((rows, wq_ref.shape[1]), F32)
+    query = jnp.zeros((q_rows, wq_ref.shape[1]), F32)
     kvt = jnp.zeros((2 * half, rows), F32)
     for j in range(blocks):
         part = slice(j * width, (j + 1) * width)
         xj = x_ref[located(odd_ref, j, kv_ref.shape[0]), :rows].astype(F32)
-        normed = xj * inverse * gain_ref[:, part].astype(F32)
-        normed = normed.astype(BF16)
-        query = query + nn(normed, wq_ref[part, :])
-        kvt = kvt + nt(wkv_ref[:, part], normed)
+        squares = squares + xj * xj
+        gained = (xj * gain_ref[:, part].astype(F32)).astype(BF16)
+        query = query + nn(gained[:q_rows], wq_ref[part, :])
+        kvt = kvt + nt(wkv_ref[:, part], gained)
+    inverse = lax.rsqrt(jnp.sum(squares, axis=1, keepdims=True) * (1.0 / D) + EPS)
+    eye = lax.broadcasted_iota(jnp.int32, (rows, rows), 0) == lax.broadcasted_iota(
+        jnp.int32, (rows, rows), 1
+    )
+    kvt = kvt * jnp.sum(jnp.where(eye, inverse, 0.0), axis=0, keepdims=True)
+    query = query * inverse[:q_rows]
     for tick in range(TICKS):
         here = slice(tick * ROWS, (tick + 1) * ROWS)
         inv_ref[tick] = inverse[here]
@@ -153,10 +161,8 @@
         sin_ref[tick] = sin
         cost_ref[tick] = cos_t
         sint_ref[tick] = sin_t
-        for h in range(query.shape[1] // HD):
-            cols = slice(h * HD, (h + 1) * HD)
-            head = query[here, cols]
-            q_ref[tick, :, cols] = (head * cos + pair_swap(head, 1) * sin).astype(BF16)
+        if tick == 0:
+            rotate_heads(query, cos, sin, q_ref)
         keys = kvt[:half, here]
         keys = keys * cos_t + pair_swap(keys, 0) * sin_t
         both = jnp.concatenate([keys, kvt[half:, here]], axis=0).astype(BF16)
@@ -202,19 +208,72 @@
         out_ref[i] = grad_ref[...]
 
 
+def softmaxes(tick, seg_ref, q_ref, keys):
+    row, column = iotas()
+    allowed = column <= row
+    for start in segment_starts(seg_ref, tick):
+        allowed = allowed & ((row < start) | (column >= start))
+    out = []
+    for h in range(q_ref.shape[1] // HD):
+        query = q_ref[:, h * HD : (h + 1) * HD]
+        weights = jnp.where(allowed, jnp.exp(nn(query, keys) * SCALE), 0.0)
+        out.append(weights / jnp.sum(weights, axis=1, keepdims=True))
+    return out
+
+
+def query_body(
+    tick,
+    odd_ref,
+    seg_ref,
+    wq_ref,
+    gain_ref,
+    x_ref,
+    kv_ref,
+    inv_ref,
+    cos_ref,
+    sin_ref,
+    q_ref,
+    soft_ref,
+):
+    blocks, _, width = x_ref.shape
+    shares, half = kv_ref.shape[0], kv_ref.shape[2] // 2
+    here = slice(tick * ROWS, (tick + 1) * ROWS)
+    query = jnp.zeros(q_ref.shape, F32)
+    for j in range(blocks):
+        part = slice(j * width, (j + 1) * width)
+        xj = x_ref[located(odd_ref, j, shares), here].astype(F32)
+        gained = (xj * gain_ref[:, part].astype(F32)).astype(BF16)
+        query = query + nn(gained, wq_ref[part, :])
+    rotate_heads(query * inv_ref[tick], cos_ref[tick], sin_ref[tick], q_ref)
+    keys = jnp.concatenate([kv_ref[i, tick, :half] for i in range(shares)], axis=0)
+    for h, softmax in enumerate(softmaxes(tick, seg_ref, q_ref, keys)):
+        soft_ref[h] = softmax
+
+
 def attention_body(
-    tick, got_at, odd_ref, seg_ref, got_ref, wo_ref, q_ref, kv_ref, cos_ref, sin_ref, dq_ref, dkv_ref, t_ref
+    tick,
+    got_at,
+    odd_ref,
+    seg_ref,
+    got_ref,
+    wo_ref,
+    q_ref,
+    kv_ref,
+    cos_ref,
+    sin_ref,
+    *refs,
 ):
+    *ready, dq_ref, dkv_ref, t_ref = refs
     blocks, _, width = got_ref.shape
     shares, half = dkv_ref.shape[0], dkv_ref.shape[1] // 2
     keys = jnp.concatenate([kv_ref[i, tick, :half] for i in range(shares)], axis=0)
     values = jnp.concatenate([kv_ref[i, tick, half:] for i in range(shares)], axis=0)
     cos = cos_ref[tick]
     sin = sin_ref[tick]
-    row, column = iotas()
-    allowed = column <= row
-    for start in segment_starts(seg_ref, tick):
-        allowed = allowed & ((row < start) | (column >= start))
+    if ready:
+        soft = [ready[0][h] for h in range(ready[0].shape[0])]
+    else:
+        soft = softmaxes(tick, seg_ref, q_ref, keys)
     dout = jnp.zeros(dq_ref.shape, F32)
     for j in range(blocks):
         at = located(odd_ref, j, shares) if tick == 0 else j
@@ -226,10 +285,9 @@
     own = jnp.zeros((ROWS, HD), F32)
     for h in range(dq_ref.shape[1] // HD):
         cols = slice(h * HD, (h + 1) * HD)
-        query = q_ref[tick, :, cols]
+        query = q_ref[:, cols]
         dhead = dout[:, cols]
-        weights = jnp.where(allowed, jnp.exp(nn(query, keys) * SCALE), 0.0)
-        softmax = weights / jnp.sum(weights, axis=1, keepdims=True)
+        softmax = soft[h]
         dprobs = nn(dhead, values)
         delta = jnp.sum(softmax * dprobs, axis=1, keepdims=True)
         dscores = (softmax * (dprobs - delta) * SCALE).astype(BF16)
@@ -329,7 +387,7 @@
     wq, wk, wv, wo = w_query[0], w_key[0].T, w_value[0].T, w_out[0]
     kv_share = wk.shape[0]
     width = saved.shape[3]
-    place = (tp_index % share).astype(jnp.int32)[None]
+    place = (tp_index & (share - 1)).astype(jnp.int32)[None]
     tables = rotation_tables()
 
     def blocks_of(rows):
@@ -339,7 +397,7 @@
         return lax.all_to_all(rows, "tp", 0, 0)
 
     last_flag = last_section.astype(jnp.int32)[None]
-    odd = (lax.axis_index("pipe") % 2).astype(jnp.int32)[None]
+    odd = (lax.axis_index("pipe") & 1).astype(jnp.int32)[None]
     saved, place, odd, last_flag = lax.optimization_barrier((saved, place, odd, last_flag))
     def stage(blocks, along):
         lines = []
@@ -356,8 +414,8 @@
     (spread,) = kernel_call(
         spread_body,
         (jax.ShapeDtypeStruct((share, rows_in, width), BF16),),
-        "vv",
-        (saved, incoming),
+        "v",
+        (jnp.concatenate([saved[0].reshape(TICKS * ROWS, width), incoming[0]], axis=0),),
     )
     (relay,) = kernel_call(
         relay_body,
@@ -374,7 +432,7 @@
     query, kv, inverse, cos, sin, cos_t, sin_t, wkv = kernel_call(
         forward_body,
         (
-            jax.ShapeDtypeStruct((TICKS, ROWS, wq.shape[1]), BF16),
+            jax.ShapeDtypeStruct((ROWS, wq.shape[1]), BF16),
             jax.ShapeDtypeStruct((share, TICKS, 2 * kv_share, ROWS), BF16),
             jax.ShapeDtypeStruct((TICKS, ROWS, 1), F32),
             jax.ShapeDtypeStruct((TICKS, ROWS, HD), F32),
@@ -388,6 +446,7 @@
     )
     kv = lax.all_to_all(kv, "tp", 0, 0, axis_index_groups=groups)
 
+    ready = []
     outputs = []
     for tick in range(TICKS):
         if tick == 0:
@@ -403,12 +462,12 @@
         dquery, dkv, along = kernel_call(
             functools.partial(attention_body, tick, got_at),
             (
-                jax.ShapeDtypeStruct(query.shape[1:], BF16),
+                jax.ShapeDtypeStruct(query.shape, BF16),
                 jax.ShapeDtypeStruct((share, 2 * kv_share, ROWS), BF16),
                 jax.ShapeDtypeStruct((ROWS, 1), F32),
             ),
-            "s" + "v" * 7,
-            (odd, seg_lengths, got, wo, query, kv, cos, sin),
+            "s" + "v" * (7 + len(ready)),
+            (odd, seg_lengths, got, wo, query, kv, cos, sin, *ready),
         )
         dkv = lax.all_to_all(dkv, "tp", 0, 0, axis_index_groups=groups)
         (blocks,) = kernel_call(
@@ -418,11 +477,23 @@
             (odd, first, dquery, dkv, wq, wkv, gain, inverse, along, cos_t, sin_t),
         )
         blocks = exchange(blocks)
+        if tick == 0:
+            blocks, inverse = lax.optimization_barrier((blocks, inverse))
         total = jnp.sum(blocks.astype(F32), axis=0)
         result = (grad.astype(F32) + total).astype(BF16)
         received = shifted(result, "pipe", -1)
         if tick == 0:
-            received, result = lax.optimization_barrier((received, result))
+            later = kernel_call(
+                functools.partial(query_body, 1),
+                (
+                    jax.ShapeDtypeStruct(query.shape, BF16),
+                    jax.ShapeDtypeStruct((query.shape[1] // HD, ROWS, ROWS), F32),
+                ),
+                "s" + "v" * 8,
+                (odd, seg_lengths, wq, gain, first, kv, inverse, cos, sin),
+            )
+            received, result, later = lax.optimization_barrier((received, result, later))
+            query, *ready = later
         outputs.append(result)
     (carried,) = kernel_call(
         functools.partial(next_gradient, TICKS - 1),

time: 145 us -> 144 us (level)
  local copies, waits for them, and re-layouts: 1.83 us -> 0.1 us
    unnamed x32 -> x30, local copies, waits for them, and re-layouts: 1.83 us -> 0.1 us
    pallas_call x9 -> x10, Pallas kernels: 9.01 us -> 8.93 us  [kernel_call(): pl.pallas_call(body, out_shape=outs, in_specs=[kinds[kind] for kind in sp...]
  transfers between devices with their start and end apart: 2 -> 2, of which waited for: 2 -> 2; matrix products, arithmetic and copies ran while one was open for 0% -> 0% of each run, Pallas kernels for 0% -> 1%
where the time goes in v6:
time: 144 us; the launch traced here: 143 us
  blocking collectives  110 us (76%)
  starting transfers between devices  17.2 us (12%)
  Pallas kernels  8.93 us (6%)
  waiting for transfers between devices  3.06 us (2%)
  other arithmetic  1.94 us (1%)
    all_to_all x3, blocking collectives, exchange(): return lax.all_to_all(rows, 'tp', 0, 0)  51.1 us
    all_to_all x2, blocking collectives, stage(): return lax.all_to_all(blocks, ('pipe', 'tp'), 0, 0, axis_index_groups=lines)  38.4 us
    ppermute x2, starting transfers between devices, shifted(): lax.ppermute(value, axis, [(source, source + steps) for source in range(f...  17.2 us
    all_to_all x2, blocking collectives, per_device(): dkv = lax.all_to_all(dkv, 'tp', 0, 0, axis_index_groups=groups)  13.7 us
    pallas_call x10, Pallas kernels, kernel_call(): pl.pallas_call(body, out_shape=outs, in_specs=[kinds[kind] for kind in sp...  8.93 us
    all_to_all x1, blocking collectives, per_device(): kv = lax.all_to_all(kv, 'tp', 0, 0, axis_index_groups=groups)  7.21 us
    ppermute x2, waiting for transfers between devices, shifted(): lax.ppermute(value, axis, [(source, source + steps) for source in range(f...  3.06 us
  transfers between devices with their start and end apart: 2, of which 2 were waited for; matrix products, arithmetic and copies ran while one was open for 0% of the time, Pallas kernels for 1%

profile of v6, /device:TPU:1, one launch (start us, length us, event | category | flops | bytes accessed | tf_op | source)
XLA Modules:
  0.0 142.5 jit_solution(6172090926558735757)
XLA Ops:
  0.6 1.0 pad_maximum_fusion.rows_ref
  1.6 0.1 shard_map.167
  1.7 13.0 %all_to_all.40.got_ref = bf16[4,384,256]{2,1,0:T(8,128)(2,1)S(1)} all-to-all(bf16[4,384,256]{2,1,0:T(8,128)(2,1)S(1)} %shard_map.167), channel_id=1, replica_groups={{0,1,2,3},{4,5,6,7},{8,9,10,11},{12,13,14,15},{16,20,24,28},{17,21,25,2..., dimensions={0} | all-to-all | bytes 1572864 | tf_op jit(solution)/shard_map/all_to_all | solution.py:411
  14.6 0.2 shard_map.168
  14.8 0.0 copy-start
  14.9 0.0 copy-start.3
  14.9 0.0 copy-start.4
  14.9 0.0 copy-start.5
  14.9 0.0 copy-start.6
  14.9 0.0 copy-start.7
  14.9 0.0 copy-start.8
  14.9 0.0 copy-start.9
  14.9 0.0 copy-start.10
  15.0 25.4 %all_to_all.41 = bf16[4,4,384,256]{3,2,1,0:T(8,128)(2,1)S(1)} all-to-all(bf16[4,4,384,256]{3,2,1,0:T(8,128)(2,1)S(1)} %shard_map.168), channel_id=1, replica_groups={{0,4,8,12},{1,5,9,13},{2,6,10,14},{3,7,11,15},{16,17,18,19},{20,21,22,2..., dimensions={0} | all-to-all | bytes 6291456 | tf_op jit(solution)/shard_map/all_to_all | solution.py:411
  40.4 0.0 copy-done
  40.4 0.0 copy-done.3
  40.4 0.0 copy-done.4
  40.4 0.0 copy-done.5
  40.4 0.0 copy-done.6
  40.4 0.0 copy-start.1
  40.4 1.5 %shard_map.169 = (bf16[128,256]{1,0:T(8,128)(2,1)S(1)}, bf16[4,2,64,128]{3,2,1,0:T(8,128)(2,1)S(1)}, f32[2,128,1]{2,1,0:T(8,128)S(1)}, f32[2,128,128]{2,1,0:T(8,...) custom-call(s32[1]{0:T(128)} %bitcast.1.place_ref, ...), custom_call_target="tpu_custom_call" | custom-call | tf_op jit(solution)/shard_map/pallas_call | solution.py:53
  41.9 7.2 %all_to_all.42.kv_ref = bf16[4,2,64,128]{3,2,1,0:T(8,128)(2,1)S(1)} all-to-all(bf16[4,2,64,128]{3,2,1,0:T(8,128)(2,1)S(1)} %get-tuple-element.34), channel_id=1, replica_groups={{0,1,2,3},{4,5,6,7},{8,9,10,11},{12,13,14,15},{16,17,18,19},{20,21,22,2..., dimensions={0} | all-to-all | bytes 262144 | tf_op jit(solution)/shard_map/all_to_all | solution.py:447
  49.1 0.0 copy-done.1
  49.1 1.6 %shard_map.170 = (bf16[128,256]{1,0:T(8,128)(2,1)S(1)}, bf16[4,64,128]{2,1,0:T(8,128)(2,1)S(1)}, f32[128,1]{1,0:T(8,128)S(1)}) custom-call(s32[1]{0:T(128)} %bitcast.2.odd_ref, s32[1,2,4]{2,1,0:T(2,128)S(1)} %copy-done.10, bf16[16,384,256]{2,1,0:T(8,128)(2,1)S(1)} %bitcast.23, bf16[256,4096]{1,0:T(8,128)(2,1)S(1)} %bitcast.31, ...), custom_call_target="tpu_custom_call" | custom-call | tf_op jit(solution)/shard_map/pallas_call | solution.py:53
  50.7 6.8 %all_to_all.43.dkv_ref = bf16[4,64,128]{2,1,0:T(8,128)(2,1)S(1)} all-to-all(bf16[4,64,128]{2,1,0:T(8,128)(2,1)S(1)} %get-tuple-element.38), channel_id=1, replica_groups={{0,1,2,3},{4,5,6,7},{8,9,10,11},{12,13,14,15},{16,17,18,19},{20,21,22,2..., dimensions={0} | all-to-all | bytes 131072 | tf_op jit(solution)/shard_map/all_to_all | solution.py:472
  57.5 1.2 shard_map.171
  58.8 0.0 copy-start.14
  58.8 14.6 %all_to_all.44 = bf16[16,128,256]{2,1,0:T(8,128)(2,1)S(1)} all-to-all(bf16[16,128,256]{2,1,0:T(8,128)(2,1)S(1)} %shard_map.171), channel_id=1, replica_groups=mesh['pipe'=32,'tp'=16] {'tp'}, dimensions={0} | all-to-all | bytes 2097152 | tf_op jit(solution)/shard_map/all_to_all | solution.py:397
  73.3 0.1 convert_reduce_fusion.1
  73.5 0.0 copy-start.2
  73.5 0.0 copy-start.11
  73.5 0.0 copy-start.12
  73.5 0.0 copy-start.13
  73.6 11.1 %collective-permute-start = (bf16[128,256]{1,0:T(8,128)(2,1)S(1)}, bf16[128,256]{1,0:T(8,128)(2,1)S(1)}, u32[]{:S(2)}, u32[]{:S(2)}) collective-permute-start(bf16[128,256]{1,0:T(8,128)(2,1)S(1)} %add_convert_fusion.1), channel_id=1, source_target_pairs={{16,0},{32,16},{48,32},{64,48},{80,64},{96,80},{112,96},{128,112},... | collective-permute-start | bytes 196616 | tf_op jit(solution)/shard_map/ppermute | solution.py:346
  84.7 0.8 shard_map.172
  85.5 0.7 collective-permute-done.received_ref
  86.2 0.0 copy-done.11
  86.2 0.1 shard_map.173
  86.3 19.6 %all_to_all.45.got_ref = bf16[16,128,256]{2,1,0:T(8,128)(2,1)S(1)} all-to-all(bf16[16,128,256]{2,1,0:T(8,128)(2,1)S(1)} %get-tuple-element.52), channel_id=1, replica_groups=mesh['pipe'=32,'tp'=16] {'tp'}, dimensions={0} | all-to-all | bytes 2097152 | tf_op jit(solution)/shard_map/all_to_all | solution.py:397
  105.9 1.6 %shard_map.174 = (bf16[128,256]{1,0:T(8,128)(2,1)S(1)}, bf16[4,64,128]{2,1,0:T(8,128)(2,1)S(1)}, f32[128,1]{1,0:T(8,128)S(1)}) custom-call(s32[1]{0:T(128)} %bitcast.2.odd_ref, s32[1,2,4]{2,1,0:T(2,128)S(1)} %copy-done.10, bf16[16,128,256]{2,1,0:T(8,128)(2,1)S(1)} %all_to_all.45.got_ref, bf16[256,4096]{1,0:T(8,128)(2,1)S(1)} %bitcast.32, ...), custom_call_target="tpu_custom_call" | custom-call | tf_op jit(solution)/shard_map/pallas_call | solution.py:53
  107.5 6.8 %all_to_all.46.dkv_ref = bf16[4,64,128]{2,1,0:T(8,128)(2,1)S(1)} all-to-all(bf16[4,64,128]{2,1,0:T(8,128)(2,1)S(1)} %get-tuple-element.56), channel_id=1, replica_groups={{0,1,2,3},{4,5,6,7},{8,9,10,11},{12,13,14,15},{16,17,18,19},{20,21,22,2..., dimensions={0} | all-to-all | bytes 131072 | tf_op jit(solution)/shard_map/all_to_all | solution.py:472
  114.4 1.2 shard_map.175
  115.6 17.0 %all_to_all.47 = bf16[16,128,256]{2,1,0:T(8,128)(2,1)S(1)} all-to-all(bf16[16,128,256]{2,1,0:T(8,128)(2,1)S(1)} %shard_map.175), channel_id=1, replica_groups=mesh['pipe'=32,'tp'=16] {'tp'}, dimensions={0} | all-to-all | bytes 2097152 | tf_op jit(solution)/shard_map/all_to_all | solution.py:397
  132.6 0.1 convert_reduce_fusion
  132.7 6.1 %collective-permute-start.1 = (bf16[128,256]{1,0:T(8,128)(2,1)S(1)}, bf16[128,256]{1,0:T(8,128)(2,1)S(1)}, u32[]{:S(2)}, u32[]{:S(2)}) collective-permute-start(bf16[128,256]{1,0:T(8,128)(2,1)S(1)} %add_convert_fusion), channel_id=1, source_target_pairs={{16,0},{32,16},{48,32},{64,48},{80,64},{96,80},{112,96},{128,112},... | collective-permute-start | bytes 196616 | tf_op jit(solution)/shard_map/ppermute | solution.py:346
  138.9 0.7 maximum_bitcast_fusion
  139.5 2.4 %collective-permute-done.1.received_ref = bf16[128,256]{1,0:T(8,128)(2,1)S(1)} collective-permute-done((bf16[128,256]{1,0:T(8,128)(2,1)S(1)}, bf16[128,256]{1,0:T(8,128)(2,1)S(1)}, u32[]{:S(2)}, u32[]{:S(2)}) %collective-permute-start.1) | collective-permute-done | bytes 65568 | tf_op jit(solution)/shard_map/ppermute | solution.py:346
  141.9 0.6 shard_map.176
  (10 shorter events, 0.0 us)
Async XLA Ops:
  14.8 25.5 %copy-start = (bf16[1,4096,256]{2,1,0:T(8,128)(2,1)S(1)}, bf16[1,4096,256]{2,1,0:T(8,128)(2,1)}, u32[]{:S(2)}) copy-start(bf16[1,4096,256]{2,1,0:T(8,128)(2,1)} %param.19) | copy-start | bytes 6291460
  14.9 25.5 %copy-start.3 = (bf16[1,4096]{1,0:T(2,128)(2,1)S(1)}, bf16[1,4096]{1,0:T(2,128)(2,1)}, u32[]{:S(2)}) copy-start(bf16[1,4096]{1,0:T(2,128)(2,1)} %gain_ref.7) | copy-start | bytes 24580
  14.9 25.5 %copy-start.4 = (bf16[1,4096,32]{1,2,0:T(8,128)(2,1)S(1)}, bf16[1,4096,32]{1,2,0:T(8,128)(2,1)}, u32[]{:S(2)}) copy-start(bf16[1,4096,32]{1,2,0:T(8,128)(2,1)} %param.20) | copy-start | bytes 786436
  14.9 25.5 %copy-start.5 = (bf16[1,4096,32]{1,2,0:T(8,128)(2,1)S(1)}, bf16[1,4096,32]{1,2,0:T(8,128)(2,1)}, u32[]{:S(2)}) copy-start(bf16[1,4096,32]{1,2,0:T(8,128)(2,1)} %param.21) | copy-start | bytes 786436
  14.9 25.5 %copy-start.6 = (bf16[3,128,128]{2,1,0:T(8,128)(2,1)S(1)}, bf16[3,128,128]{2,1,0:T(8,128)(2,1)}, u32[]{:S(2)}) copy-start(bf16[3,128,128]{2,1,0:T(8,128)(2,1)} %constant.28.clone.stabt_ref) | copy-start | bytes 294916
  14.9 25.5 %copy-start.7 = (bf16[3,128,128]{2,1,0:T(8,128)(2,1)S(1)}, bf16[3,128,128]{2,1,0:T(8,128)(2,1)}, u32[]{:S(2)}) copy-start(bf16[3,128,128]{2,1,0:T(8,128)(2,1)} %constant.27.clone.ctabt_ref) | copy-start | bytes 294916
  14.9 25.5 %copy-start.8 = (bf16[3,128,128]{2,1,0:T(8,128)(2,1)S(1)}, bf16[3,128,128]{2,1,0:T(8,128)(2,1)}, u32[]{:S(2)}) copy-start(bf16[3,128,128]{2,1,0:T(8,128)(2,1)} %constant.26.clone.stab_ref) | copy-start | bytes 294916
  14.9 25.5 %copy-start.9 = (bf16[3,128,128]{2,1,0:T(8,128)(2,1)S(1)}, bf16[3,128,128]{2,1,0:T(8,128)(2,1)}, u32[]{:S(2)}) copy-start(bf16[3,128,128]{2,1,0:T(8,128)(2,1)} %constant.25.clone.ctab_ref) | copy-start | bytes 294916
  14.9 25.5 %copy-start.10 = (s32[1,2,4]{2,1,0:T(2,128)S(1)}, s32[1,2,4]{2,1,0:T(2,128)}, u32[]{:S(2)}) copy-start(s32[1,2,4]{2,1,0:T(2,128)} %seg_ref.7) | copy-start | bytes 100
  40.4 8.7 %copy-start.1 = (bf16[1,256,4096]{2,1,0:T(8,128)(2,1)S(1)}, bf16[1,256,4096]{2,1,0:T(8,128)(2,1)}, u32[]{:S(2)}) copy-start(bf16[1,256,4096]{2,1,0:T(8,128)(2,1)} %param.22) | copy-start | bytes 6291460
  58.8 14.7 %copy-start.14 = (bf16[1,128,256]{2,1,0:T(8,128)(2,1)S(1)}, bf16[1,128,256]{2,1,0:T(8,128)(2,1)}, u32[]{:S(2)}) copy-start(bf16[1,128,256]{2,1,0:T(8,128)(2,1)} %param.17) | copy-start | bytes 196612
  73.5 12.7 %copy-start.2 = (bf16[2,128,256]{2,1,0:T(8,128)(2,1)S(1)}, bf16[2,128,256]{2,1,0:T(8,128)(2,1)}, u32[]{:S(2)}) copy-start(bf16[2,128,256]{2,1,0:T(8,128)(2,1)} %score_ref.3) | copy-start | bytes 393220
  73.5 12.6 %copy-start.11 = (f32[512]{0:T(512)S(1)}, f32[512]{0:T(512)}, u32[]{:S(2)}) copy-start(f32[512]{0:T(512)} %param.25) | copy-start | bytes 6148
  73.5 12.6 %copy-start.12 = (s32[512]{0:T(512)S(1)}, s32[512]{0:T(512)}, u32[]{:S(2)}) copy-start(s32[512]{0:T(512)} %param.26) | copy-start | bytes 6148
  73.5 12.6 %copy-start.13 = (s32[2,128]{1,0:T(2,128)S(1)}, s32[2,128]{1,0:T(2,128)}, u32[]{:S(2)}) copy-start(s32[2,128]{1,0:T(2,128)} %sample_ref.3) | copy-start | bytes 3076
  73.6 12.6 %collective-permute-start = (bf16[128,256]{1,0:T(8,128)(2,1)S(1)}, bf16[128,256]{1,0:T(8,128)(2,1)S(1)}, u32[]{:S(2)}, u32[]{:S(2)}) collective-permute-start(bf16[128,256]{1,0:T(8,128)(2,1)S(1)} %add_convert_fusion.1), channel_id=1, source_target_pairs={{16,0},{32,16},{48,32},{64,48},{80,64},{96,80},{112,96},{128,112},... | collective-permute-start | bytes 196616 | tf_op jit(solution)/shard_map/ppermute | solution.py:346
  132.7 9.2 %collective-permute-start.1 = (bf16[128,256]{1,0:T(8,128)(2,1)S(1)}, bf16[128,256]{1,0:T(8,128)(2,1)S(1)}, u32[]{:S(2)}, u32[]{:S(2)}) collective-permute-start(bf16[128,256]{1,0:T(8,128)(2,1)S(1)} %add_convert_fusion), channel_id=1, source_target_pairs={{16,0},{32,16},{48,32},{64,48},{80,64},{96,80},{112,96},{128,112},... | collective-permute-start | bytes 196616 | tf_op jit(solution)/shard_map/ppermute | solution.py:346

commit v7 on v6

--- a/solution.py
+++ b/solution.py
@@ -87,7 +87,13 @@
     return jnp.where(odd_ref[0] > 0, across, block)
 
 
-def relay_body(got_ref, out_ref):
+def relay_body(
+    first_ref, got_ref, score_ref, rewards_ref, group_ref, sample_ref, out_ref, head_ref
+):
+    @pl.when(first_ref[0] > 0)
+    def _():
+        head_rows(score_ref, rewards_ref, group_ref, sample_ref, head_ref)
+
     for i in range(out_ref.shape[0]):
         out_ref[i] = got_ref[...]
 
@@ -170,40 +176,24 @@
             kv_ref[i, tick] = both
 
 
-def next_gradient(tick, last_ref, received_ref, score_ref, rewards_ref, group_ref, sample_ref, grad_ref):
-    grad_ref[...] = received_ref[...]
-
-    @pl.when(last_ref[0] > 0)
-    def _():
-        rewards = rewards_ref[...]
-        samples = rewards.shape[1]
-        prompt = lax.broadcasted_iota(jnp.int32, (GROUPS, samples), 0)
-        member = prompt == group_ref[...]
-        totals = jnp.sum(jnp.where(member, rewards, 0.0), axis=1, keepdims=True)
-        own_total = jnp.sum(jnp.where(member, totals, 0.0), axis=0, keepdims=True)
-        advantage = rewards - (own_total - rewards) / (GROUP_SIZE - 1)
-        sample = lax.broadcasted_iota(jnp.int32, (ROWS, samples), 1)
-        row, column = iotas()
+def head_rows(score_ref, rewards_ref, group_ref, sample_ref, head_ref):
+    rewards = rewards_ref[...]
+    samples = rewards.shape[1]
+    prompt = lax.broadcasted_iota(jnp.int32, (GROUPS, samples), 0)
+    member = prompt == group_ref[...]
+    totals = jnp.sum(jnp.where(member, rewards, 0.0), axis=1, keepdims=True)
+    own_total = jnp.sum(jnp.where(member, totals, 0.0), axis=0, keepdims=True)
+    advantage = rewards - (own_total - rewards) / (GROUP_SIZE - 1)
+    sample = lax.broadcasted_iota(jnp.int32, (ROWS, samples), 1)
+    row, column = iotas()
+    for tick in range(TICKS):
         own = jnp.where(row == column, sample_ref[tick : tick + 1, :].astype(F32), 0.0)
         chosen = sample.astype(F32) == jnp.sum(own, axis=1, keepdims=True)
         row_adv = jnp.sum(jnp.where(chosen, advantage, 0.0), axis=1, keepdims=True)
-        grad_ref[...] = (-row_adv * score_ref[tick].astype(F32)).astype(BF16)
-
-
-def turn_body(
-    tick,
-    last_ref,
-    received_ref,
-    score_ref,
-    rewards_ref,
-    group_ref,
-    sample_ref,
-    grad_ref,
-    out_ref,
-):
-    next_gradient(
-        tick, last_ref, received_ref, score_ref, rewards_ref, group_ref, sample_ref, grad_ref
-    )
+        head_ref[tick] = (-row_adv * score_ref[tick].astype(F32)).astype(BF16)
+
+
+def turn_body(grad_ref, out_ref):
     for i in range(out_ref.shape[0]):
         out_ref[i] = grad_ref[...]
 
@@ -340,10 +330,9 @@
         out_ref[j] = (scaled - xj * along).astype(BF16)
 
 
-def shifted(value, axis, steps):
+def ring_down(value, axis):
     count = lax.axis_size(axis)
-    first, last = (max(0, -steps), min(count, count - steps))
-    return lax.ppermute(value, axis, [(source, source + steps) for source in range(first, last)])
+    return lax.ppermute(value, axis, [(source, (source - 1) % count) for source in range(count)])
 
 
 def thirds(table):
@@ -381,7 +370,7 @@
 ):
     tp_index = lax.axis_index("tp")
     tp_count = lax.axis_size("tp")
-    last_section = lax.axis_index("pipe") == lax.axis_size("pipe") - 1
+    first_section = lax.axis_index("pipe") == 0
     share = tp_count // KV
     groups = [list(range(g * share, (g + 1) * share)) for g in range(KV)]
     wq, wk, wv, wo = w_query[0], w_key[0].T, w_value[0].T, w_out[0]
@@ -396,9 +385,11 @@
     def exchange(rows):
         return lax.all_to_all(rows, "tp", 0, 0)
 
-    last_flag = last_section.astype(jnp.int32)[None]
+    first_flag = first_section.astype(jnp.int32)[None]
     odd = (lax.axis_index("pipe") & 1).astype(jnp.int32)[None]
-    saved, place, odd, last_flag = lax.optimization_barrier((saved, place, odd, last_flag))
+    saved, place, odd, first_flag, first_section = lax.optimization_barrier(
+        (saved, place, odd, first_flag, first_section)
+    )
     def stage(blocks, along):
         lines = []
         for section in range(lax.axis_size("pipe")):
@@ -417,16 +408,23 @@
         "v",
         (jnp.concatenate([saved[0].reshape(TICKS * ROWS, width), incoming[0]], axis=0),),
     )
-    (relay,) = kernel_call(
+    relay, heads = kernel_call(
         relay_body,
-        (jax.ShapeDtypeStruct((share, share, rows_in, width), BF16),),
-        "v",
-        (stage(spread, 0),),
+        (
+            jax.ShapeDtypeStruct((share, share, rows_in, width), BF16),
+            jax.ShapeDtypeStruct(score_grad.shape, BF16),
+        ),
+        "s" + "v" * 5,
+        (
+            first_flag,
+            stage(spread, 0),
+            score_grad,
+            rewards[None],
+            sample_group[None],
+            head_sample,
+        ),
     )
     first = stage(relay, 1).reshape(tp_count, rows_in, width)
-
-    def chooser(received):
-        return (last_flag, received, score_grad, rewards[None], sample_group[None], head_sample)
 
     grad = incoming[0]
     query, kv, inverse, cos, sin, cos_t, sin_t, wkv = kernel_call(
@@ -452,12 +450,8 @@
         if tick == 0:
             got, got_at = first, TICKS * ROWS
         else:
-            grad, packed = kernel_call(
-                functools.partial(turn_body, tick - 1),
-                (jax.ShapeDtypeStruct(grad.shape, BF16),) + blocks_of(ROWS),
-                "s" + "v" * 5,
-                chooser(received),
-            )
+            grad = received
+            (packed,) = kernel_call(turn_body, blocks_of(ROWS), "v", (grad,))
             got, got_at = exchange(packed), 0
         dquery, dkv, along = kernel_call(
             functools.partial(attention_body, tick, got_at),
@@ -481,7 +475,7 @@
             blocks, inverse = lax.optimization_barrier((blocks, inverse))
         total = jnp.sum(blocks.astype(F32), axis=0)
         result = (grad.astype(F32) + total).astype(BF16)
-        received = shifted(result, "pipe", -1)
+        received = ring_down(jnp.where(first_section, heads[tick], result), "pipe")
         if tick == 0:
             later = kernel_call(
                 functools.partial(query_body, 1),
@@ -495,13 +489,7 @@
             received, result, later = lax.optimization_barrier((received, result, later))
             query, *ready = later
         outputs.append(result)
-    (carried,) = kernel_call(
-        functools.partial(next_gradient, TICKS - 1),
-        (jax.ShapeDtypeStruct(grad.shape, BF16),),
-        "s" + "v" * 5,
-        chooser(received),
-    )
-    return (jnp.stack(outputs, axis=0)[None], carried[None])
+    return (jnp.stack(outputs, axis=0)[None], received[None])
 
 
 def solution(mesh):

time: 144 us -> 140 us (0.972)
  blocking collectives: 110 us -> 107 us
  starting transfers between devices: 17.2 us -> 15.4 us
  waiting for transfers between devices: 3.06 us -> 4.67 us
    all_to_all x3, blocking collectives: 51.1 us -> 47.3 us  [exchange(): return lax.all_to_all(rows, 'tp', 0, 0)]
    ppermute x2, starting transfers between devices: 17.2 us -> 15.4 us  [ring_down(): lax.ppermute(value, axis, [(source, (source - 1) % count) for source in r...]
    ppermute x2, waiting for transfers between devices: 3.06 us -> 4.67 us  [ring_down(): lax.ppermute(value, axis, [(source, (source - 1) % count) for source in r...]
    pallas_call x10 -> x9, Pallas kernels: 8.93 us -> 8.26 us  [kernel_call(): pl.pallas_call(body, out_shape=outs, in_specs=[kinds[kind] for kind in sp...]
where the time goes in v7:
time: 140 us; the launch traced here: 139 us
  blocking collectives  107 us (76%)
  starting transfers between devices  15.4 us (11%)
  Pallas kernels  8.26 us (6%)
  waiting for transfers between devices  4.67 us (3%)
  other arithmetic  2.03 us (1%)
    all_to_all x3, blocking collectives, exchange(): return lax.all_to_all(rows, 'tp', 0, 0)  47.3 us
    all_to_all x2, blocking collectives, stage(): return lax.all_to_all(blocks, ('pipe', 'tp'), 0, 0, axis_index_groups=lines)  38.5 us
    ppermute x2, starting transfers between devices, ring_down(): lax.ppermute(value, axis, [(source, (source - 1) % count) for source in r...  15.4 us
    all_to_all x2, blocking collectives, per_device(): dkv = lax.all_to_all(dkv, 'tp', 0, 0, axis_index_groups=groups)  13.7 us
    pallas_call x9, Pallas kernels, kernel_call(): pl.pallas_call(body, out_shape=outs, in_specs=[kinds[kind] for kind in sp...  8.26 us
    all_to_all x1, blocking collectives, per_device(): kv = lax.all_to_all(kv, 'tp', 0, 0, axis_index_groups=groups)  7.21 us
    ppermute x2, waiting for transfers between devices, ring_down(): lax.ppermute(value, axis, [(source, (source - 1) % count) for source in r...  4.67 us
  transfers between devices with their start and end apart: 2, of which 2 were waited for; matrix products, arithmetic and copies ran while one was open for 0% of the time, Pallas kernels for 1%

profile of v7, /device:TPU:1, one launch (start us, length us, event | category | flops | bytes accessed | tf_op | source)
XLA Modules:
  0.0 138.7 jit_solution(12001274525208403032)
XLA Ops:
  0.6 0.0 copy-start.13
  0.6 0.0 copy-start.12
  0.7 0.0 copy-start.11
  0.7 0.0 copy-start.5
  0.7 1.0 pad_maximum_fusion.rows_ref
  1.7 0.1 shard_map.167
  1.7 13.0 %all_to_all.40.got_ref = bf16[4,384,256]{2,1,0:T(8,128)(2,1)S(1)} all-to-all(bf16[4,384,256]{2,1,0:T(8,128)(2,1)S(1)} %shard_map.167), channel_id=1, replica_groups={{0,1,2,3},{4,5,6,7},{8,9,10,11},{12,13,14,15},{16,20,24,28},{17,21,25,2..., dimensions={0} | all-to-all | bytes 1572864 | tf_op jit(solution)/shard_map/all_to_all | solution.py:402
  14.7 0.0 copy-done.13
  14.7 0.0 copy-done.12
  14.7 0.0 copy-done.11
  14.7 0.0 copy-done.5
  14.8 0.2 shard_map.168
  15.0 0.0 copy-start
  15.0 0.0 copy-start.2
  15.0 0.0 copy-start.3
  15.0 0.0 copy-start.4
  15.0 0.0 copy-start.6
  15.0 0.0 copy-start.7
  15.0 0.0 copy-start.8
  15.1 0.0 copy-start.9
  15.1 0.0 copy-start.10
  15.1 25.5 %all_to_all.41 = bf16[4,4,384,256]{3,2,1,0:T(8,128)(2,1)S(1)} all-to-all(bf16[4,4,384,256]{3,2,1,0:T(8,128)(2,1)S(1)} %get-tuple-element.36), channel_id=1, replica_groups={{0,4,8,12},{1,5,9,13},{2,6,10,14},{3,7,11,15},{16,17,18,19},{20,21,22,2..., dimensions={0} | all-to-all | bytes 6291456 | tf_op jit(solution)/shard_map/all_to_all | solution.py:402
  40.6 0.0 copy-done
  40.6 0.0 copy-done.2
  40.6 0.0 copy-done.3
  40.7 0.0 copy-start.1
  40.7 1.5 %shard_map.169 = (bf16[128,256]{1,0:T(8,128)(2,1)S(1)}, bf16[4,2,64,128]{3,2,1,0:T(8,128)(2,1)S(1)}, f32[2,128,1]{2,1,0:T(8,128)S(1)}, f32[2,128,128]{2,1,0:T(8,...) custom-call(s32[1]{0:T(128)} %bitcast.place_ref, ...), custom_call_target="tpu_custom_call" | custom-call | tf_op jit(solution)/shard_map/pallas_call | solution.py:53
  42.1 7.2 %all_to_all.42.kv_ref = bf16[4,2,64,128]{3,2,1,0:T(8,128)(2,1)S(1)} all-to-all(bf16[4,2,64,128]{3,2,1,0:T(8,128)(2,1)S(1)} %get-tuple-element.39), channel_id=1, replica_groups={{0,1,2,3},{4,5,6,7},{8,9,10,11},{12,13,14,15},{16,17,18,19},{20,21,22,2..., dimensions={0} | all-to-all | bytes 262144 | tf_op jit(solution)/shard_map/all_to_all | solution.py:445
  49.4 1.6 %shard_map.170 = (bf16[128,256]{1,0:T(8,128)(2,1)S(1)}, bf16[4,64,128]{2,1,0:T(8,128)(2,1)S(1)}, f32[128,1]{1,0:T(8,128)S(1)}) custom-call(s32[1]{0:T(128)} %bitcast.1.odd_ref, s32[1,2,4]{2,1,0:T(2,128)S(1)} %copy-done.10, bf16[16,384,256]{2,1,0:T(8,128)(2,1)S(1)} %bitcast.29, bf16[256,4096]{1,0:T(8,128)(2,1)S(1)} %bitcast.37, ...), custom_call_target="tpu_custom_call" | custom-call | tf_op jit(solution)/shard_map/pallas_call | solution.py:53
  50.9 6.8 %all_to_all.43.dkv_ref = bf16[4,64,128]{2,1,0:T(8,128)(2,1)S(1)} all-to-all(bf16[4,64,128]{2,1,0:T(8,128)(2,1)S(1)} %get-tuple-element.43), channel_id=1, replica_groups={{0,1,2,3},{4,5,6,7},{8,9,10,11},{12,13,14,15},{16,17,18,19},{20,21,22,2..., dimensions={0} | all-to-all | bytes 131072 | tf_op jit(solution)/shard_map/all_to_all | solution.py:466
  57.8 1.2 shard_map.171
  59.0 0.0 copy-start.14
  59.0 14.6 %all_to_all.44 = bf16[16,128,256]{2,1,0:T(8,128)(2,1)S(1)} all-to-all(bf16[16,128,256]{2,1,0:T(8,128)(2,1)S(1)} %shard_map.171), channel_id=1, replica_groups=mesh['pipe'=32,'tp'=16] {'tp'}, dimensions={0} | all-to-all | bytes 2097152 | tf_op jit(solution)/shard_map/all_to_all | solution.py:386
  73.6 0.1 convert_reduce_fusion.1
  73.8 9.1 %collective-permute-start = (bf16[128,256]{1,0:T(8,128)(2,1)S(1)}, bf16[128,256]{1,0:T(8,128)(2,1)S(1)}, u32[]{:S(2)}, u32[]{:S(2)}) collective-permute-start(bf16[128,256]{1,0:T(8,128)(2,1)S(1)} %get-tuple-element.60), channel_id=1, source_target_pairs={{0,496},{16,0},{32,16},{48,32},{64,48},{80,64},{96,80},{112,96},{1... | collective-permute-start | bytes 196616 | tf_op jit(solution)/shard_map/ppermute | solution.py:335
  82.9 0.8 shard_map.172
  83.7 0.5 collective-permute-done.grad_ref
  84.2 0.1 shard_map.173
  84.3 17.6 %all_to_all.45.got_ref = bf16[16,128,256]{2,1,0:T(8,128)(2,1)S(1)} all-to-all(bf16[16,128,256]{2,1,0:T(8,128)(2,1)S(1)} %shard_map.173), channel_id=1, replica_groups=mesh['pipe'=32,'tp'=16] {'tp'}, dimensions={0} | all-to-all | bytes 2097152 | tf_op jit(solution)/shard_map/all_to_all | solution.py:386
  101.9 1.6 %shard_map.174 = (bf16[128,256]{1,0:T(8,128)(2,1)S(1)}, bf16[4,64,128]{2,1,0:T(8,128)(2,1)S(1)}, f32[128,1]{1,0:T(8,128)S(1)}) custom-call(s32[1]{0:T(128)} %bitcast.1.odd_ref, s32[1,2,4]{2,1,0:T(2,128)S(1)} %copy-done.10, bf16[16,128,256]{2,1,0:T(8,128)(2,1)S(1)} %all_to_all.45.got_ref, bf16[256,4096]{1,0:T(8,128)(2,1)S(1)} %bitcast.38, ...), custom_call_target="tpu_custom_call" | custom-call | tf_op jit(solution)/shard_map/pallas_call | solution.py:53
  103.6 6.8 %all_to_all.46.dkv_ref = bf16[4,64,128]{2,1,0:T(8,128)(2,1)S(1)} all-to-all(bf16[4,64,128]{2,1,0:T(8,128)(2,1)S(1)} %get-tuple-element.58), channel_id=1, replica_groups={{0,1,2,3},{4,5,6,7},{8,9,10,11},{12,13,14,15},{16,17,18,19},{20,21,22,2..., dimensions={0} | all-to-all | bytes 131072 | tf_op jit(solution)/shard_map/all_to_all | solution.py:466
  110.4 1.2 shard_map.175
  111.6 15.1 %all_to_all.47 = bf16[16,128,256]{2,1,0:T(8,128)(2,1)S(1)} all-to-all(bf16[16,128,256]{2,1,0:T(8,128)(2,1)S(1)} %shard_map.175), channel_id=1, replica_groups=mesh['pipe'=32,'tp'=16] {'tp'}, dimensions={0} | all-to-all | bytes 2097152 | tf_op jit(solution)/shard_map/all_to_all | solution.py:386
  126.7 0.1 convert_reduce_fusion
  126.9 6.3 %collective-permute-start.1 = (bf16[128,256]{1,0:T(8,128)(2,1)S(1)}, bf16[128,256]{1,0:T(8,128)(2,1)S(1)}, u32[]{:S(2)}, u32[]{:S(2)}) collective-permute-start(bf16[128,256]{1,0:T(8,128)(2,1)S(1)} %bitcast_select_fusion), channel_id=1, source_target_pairs={{0,496},{16,0},{32,16},{48,32},{64,48},{80,64},{96,80},{112,96},{1... | collective-permute-start | bytes 196616 | tf_op jit(solution)/shard_map/ppermute | solution.py:335
  133.2 0.7 maximum_bitcast_fusion
  133.9 4.2 %collective-permute-done.1 = bf16[128,256]{1,0:T(8,128)(2,1)S(1)} collective-permute-done((bf16[128,256]{1,0:T(8,128)(2,1)S(1)}, bf16[128,256]{1,0:T(8,128)(2,1)S(1)}, u32[]{:S(2)}, u32[]{:S(2)}) %collective-permute-start.1) | collective-permute-done | bytes 65568 | tf_op jit(solution)/shard_map/ppermute | solution.py:335
  138.1 0.6 copy.19
  (11 shorter events, 0.1 us)
Async XLA Ops:
  0.6 14.1 %copy-start.13 = (s32[2,128]{1,0:T(2,128)S(1)}, s32[2,128]{1,0:T(2,128)}, u32[]{:S(2)}) copy-start(s32[2,128]{1,0:T(2,128)} %sample_ref.1) | copy-start | bytes 3076
  0.6 14.1 %copy-start.12 = (s32[512]{0:T(512)S(1)}, s32[512]{0:T(512)}, u32[]{:S(2)}) copy-start(s32[512]{0:T(512)} %param.26) | copy-start | bytes 6148
  0.7 14.1 %copy-start.11 = (f32[512]{0:T(512)S(1)}, f32[512]{0:T(512)}, u32[]{:S(2)}) copy-start(f32[512]{0:T(512)} %param.25) | copy-start | bytes 6148
  0.7 14.1 %copy-start.5 = (bf16[2,128,256]{2,1,0:T(8,128)(2,1)S(1)}, bf16[2,128,256]{2,1,0:T(8,128)(2,1)}, u32[]{:S(2)}) copy-start(bf16[2,128,256]{2,1,0:T(8,128)(2,1)} %score_ref.1) | copy-start | bytes 393220
  15.0 25.6 %copy-start = (bf16[1,4096,256]{2,1,0:T(8,128)(2,1)S(1)}, bf16[1,4096,256]{2,1,0:T(8,128)(2,1)}, u32[]{:S(2)}) copy-start(bf16[1,4096,256]{2,1,0:T(8,128)(2,1)} %param.19) | copy-start | bytes 6291460
  15.0 25.6 %copy-start.2 = (bf16[1,4096]{1,0:T(2,128)(2,1)S(1)}, bf16[1,4096]{1,0:T(2,128)(2,1)}, u32[]{:S(2)}) copy-start(bf16[1,4096]{1,0:T(2,128)(2,1)} %gain_ref.7) | copy-start | bytes 24580
  15.0 25.6 %copy-start.3 = (bf16[1,4096,32]{1,2,0:T(8,128)(2,1)S(1)}, bf16[1,4096,32]{1,2,0:T(8,128)(2,1)}, u32[]{:S(2)}) copy-start(bf16[1,4096,32]{1,2,0:T(8,128)(2,1)} %param.20) | copy-start | bytes 786436
  15.0 25.6 %copy-start.4 = (bf16[1,4096,32]{1,2,0:T(8,128)(2,1)S(1)}, bf16[1,4096,32]{1,2,0:T(8,128)(2,1)}, u32[]{:S(2)}) copy-start(bf16[1,4096,32]{1,2,0:T(8,128)(2,1)} %param.21) | copy-start | bytes 786436
  15.0 25.6 %copy-start.6 = (bf16[3,128,128]{2,1,0:T(8,128)(2,1)S(1)}, bf16[3,128,128]{2,1,0:T(8,128)(2,1)}, u32[]{:S(2)}) copy-start(bf16[3,128,128]{2,1,0:T(8,128)(2,1)} %constant.28.clone.stabt_ref) | copy-start | bytes 294916
  15.0 25.6 %copy-start.7 = (bf16[3,128,128]{2,1,0:T(8,128)(2,1)S(1)}, bf16[3,128,128]{2,1,0:T(8,128)(2,1)}, u32[]{:S(2)}) copy-start(bf16[3,128,128]{2,1,0:T(8,128)(2,1)} %constant.27.clone.ctabt_ref) | copy-start | bytes 294916
  15.0 25.6 %copy-start.8 = (bf16[3,128,128]{2,1,0:T(8,128)(2,1)S(1)}, bf16[3,128,128]{2,1,0:T(8,128)(2,1)}, u32[]{:S(2)}) copy-start(bf16[3,128,128]{2,1,0:T(8,128)(2,1)} %constant.26.clone.stab_ref) | copy-start | bytes 294916
  15.1 25.6 %copy-start.9 = (bf16[3,128,128]{2,1,0:T(8,128)(2,1)S(1)}, bf16[3,128,128]{2,1,0:T(8,128)(2,1)}, u32[]{:S(2)}) copy-start(bf16[3,128,128]{2,1,0:T(8,128)(2,1)} %constant.25.clone.ctab_ref) | copy-start | bytes 294916
  15.1 25.6 %copy-start.10 = (s32[1,2,4]{2,1,0:T(2,128)S(1)}, s32[1,2,4]{2,1,0:T(2,128)}, u32[]{:S(2)}) copy-start(s32[1,2,4]{2,1,0:T(2,128)} %seg_ref.7) | copy-start | bytes 100
  40.7 8.7 %copy-start.1 = (bf16[1,256,4096]{2,1,0:T(8,128)(2,1)S(1)}, bf16[1,256,4096]{2,1,0:T(8,128)(2,1)}, u32[]{:S(2)}) copy-start(bf16[1,256,4096]{2,1,0:T(8,128)(2,1)} %param.22) | copy-start | bytes 6291460
  59.0 14.7 %copy-start.14 = (bf16[1,128,256]{2,1,0:T(8,128)(2,1)S(1)}, bf16[1,128,256]{2,1,0:T(8,128)(2,1)}, u32[]{:S(2)}) copy-start(bf16[1,128,256]{2,1,0:T(8,128)(2,1)} %param.17) | copy-start | bytes 196612
  73.8 10.4 %collective-permute-start = (bf16[128,256]{1,0:T(8,128)(2,1)S(1)}, bf16[128,256]{1,0:T(8,128)(2,1)S(1)}, u32[]{:S(2)}, u32[]{:S(2)}) collective-permute-start(bf16[128,256]{1,0:T(8,128)(2,1)S(1)} %get-tuple-element.60), channel_id=1, source_target_pairs={{0,496},{16,0},{32,16},{48,32},{64,48},{80,64},{96,80},{112,96},{1... | collective-permute-start | bytes 196616 | tf_op jit(solution)/shard_map/ppermute | solution.py:335
  126.9 11.2 %collective-permute-start.1 = (bf16[128,256]{1,0:T(8,128)(2,1)S(1)}, bf16[128,256]{1,0:T(8,128)(2,1)S(1)}, u32[]{:S(2)}, u32[]{:S(2)}) collective-permute-start(bf16[128,256]{1,0:T(8,128)(2,1)S(1)} %bitcast_select_fusion), channel_id=1, source_target_pairs={{0,496},{16,0},{32,16},{48,32},{64,48},{80,64},{96,80},{112,96},{1... | collective-permute-start | bytes 196616 | tf_op jit(solution)/shard_map/ppermute | solution.py:335

commit v8 on v7

--- a/solution.py
+++ b/solution.py
@@ -101,6 +101,12 @@
 def spread_body(rows_ref, out_ref):
     for i in range(out_ref.shape[0]):
         out_ref[i] = rows_ref[...]
+
+
+def row_tables(match, ctab_ref, stab_ref):
+    cos = sum(nn(match, ctab_ref[i]) for i in range(3))
+    sin = sum(nn(match, stab_ref[i]) for i in range(3))
+    return cos, sin
 
 
 def rotate_heads(query, cos, sin, q_ref):
@@ -159,15 +165,14 @@
         here = slice(tick * ROWS, (tick + 1) * ROWS)
         inv_ref[tick] = inverse[here]
         match = position_match(seg_ref, tick)
-        cos = sum(nn(match, ctab_ref[i]) for i in range(3))
-        sin = sum(nn(match, stab_ref[i]) for i in range(3))
         cos_t = sum(nt(ctabt_ref[i, own, :], match) for i in range(3))
         sin_t = sum(nt(stabt_ref[i, own, :], match) for i in range(3))
-        cos_ref[tick] = cos
-        sin_ref[tick] = sin
         cost_ref[tick] = cos_t
         sint_ref[tick] = sin_t
         if tick == 0:
+            cos, sin = row_tables(match, ctab_ref, stab_ref)
+            cos_ref[...] = cos
+            sin_ref[...] = sin
             rotate_heads(query, cos, sin, q_ref)
         keys = kvt[:half, here]
         keys = keys * cos_t + pair_swap(keys, 0) * sin_t
@@ -207,7 +212,7 @@
     for h in range(q_ref.shape[1] // HD):
         query = q_ref[:, h * HD : (h + 1) * HD]
         weights = jnp.where(allowed, jnp.exp(nn(query, keys) * SCALE), 0.0)
-        out.append(weights / jnp.sum(weights, axis=1, keepdims=True))
+        out.append(weights * (1.0 / jnp.sum(weights, axis=1, keepdims=True)))
     return out
 
 
@@ -220,10 +225,12 @@
     x_ref,
     kv_ref,
     inv_ref,
+    ctab_ref,
+    stab_ref,
+    q_ref,
+    soft_ref,
     cos_ref,
     sin_ref,
-    q_ref,
-    soft_ref,
 ):
     blocks, _, width = x_ref.shape
     shares, half = kv_ref.shape[0], kv_ref.shape[2] // 2
@@ -234,7 +241,10 @@
         xj = x_ref[located(odd_ref, j, shares), here].astype(F32)
         gained = (xj * gain_ref[:, part].astype(F32)).astype(BF16)
         query = query + nn(gained, wq_ref[part, :])
-    rotate_heads(query * inv_ref[tick], cos_ref[tick], sin_ref[tick], q_ref)
+    cos, sin = row_tables(position_match(seg_ref, tick), ctab_ref, stab_ref)
+    cos_ref[...] = cos
+    sin_ref[...] = sin
+    rotate_heads(query * inv_ref[tick], cos, sin, q_ref)
     keys = jnp.concatenate([kv_ref[i, tick, :half] for i in range(shares)], axis=0)
     for h, softmax in enumerate(softmaxes(tick, seg_ref, q_ref, keys)):
         soft_ref[h] = softmax
@@ -258,8 +268,8 @@
     shares, half = dkv_ref.shape[0], dkv_ref.shape[1] // 2
     keys = jnp.concatenate([kv_ref[i, tick, :half] for i in range(shares)], axis=0)
     values = jnp.concatenate([kv_ref[i, tick, half:] for i in range(shares)], axis=0)
-    cos = cos_ref[tick]
-    sin = sin_ref[tick]
+    cos = cos_ref[...]
+    sin = sin_ref[...]
     if ready:
         soft = [ready[0][h] for h in range(ready[0].shape[0])]
     else:
@@ -287,7 +297,9 @@
         own = own + dquery * query.astype(F32)
         dq_ref[:, cols] = (dquery * cos - pair_swap(dquery, 1) * sin).astype(BF16)
     shared = dkeys * keys.astype(F32) + dvalues * values.astype(F32)
-    t_ref[...] = jnp.sum(own + shared.T, axis=1, keepdims=True)
+    shared = jnp.sum(shared, axis=0, keepdims=True)
+    row, column = iotas()
+    t_ref[...] = jnp.sum(own + jnp.where(row == column, shared, 0.0), axis=1, keepdims=True)
     for i in range(shares):
         part = slice(i * half, (i + 1) * half)
         dkv_ref[i, :half] = dkeys[part].astype(BF16)
@@ -433,8 +445,8 @@
             jax.ShapeDtypeStruct((ROWS, wq.shape[1]), BF16),
             jax.ShapeDtypeStruct((share, TICKS, 2 * kv_share, ROWS), BF16),
             jax.ShapeDtypeStruct((TICKS, ROWS, 1), F32),
-            jax.ShapeDtypeStruct((TICKS, ROWS, HD), F32),
-            jax.ShapeDtypeStruct((TICKS, ROWS, HD), F32),
+            jax.ShapeDtypeStruct((ROWS, HD), F32),
+            jax.ShapeDtypeStruct((ROWS, HD), F32),
             jax.ShapeDtypeStruct((TICKS, kv_share, ROWS), F32),
             jax.ShapeDtypeStruct((TICKS, kv_share, ROWS), F32),
             jax.ShapeDtypeStruct((2 * kv_share, wk.shape[1]), BF16),
@@ -482,12 +494,14 @@
                 (
                     jax.ShapeDtypeStruct(query.shape, BF16),
                     jax.ShapeDtypeStruct((query.shape[1] // HD, ROWS, ROWS), F32),
+                    jax.ShapeDtypeStruct((ROWS, HD), F32),
+                    jax.ShapeDtypeStruct((ROWS, HD), F32),
                 ),
                 "s" + "v" * 8,
-                (odd, seg_lengths, wq, gain, first, kv, inverse, cos, sin),
+                (odd, seg_lengths, wq, gain, first, kv, inverse, tables[0], tables[1]),
             )
             received, result, later = lax.optimization_barrier((received, result, later))
-            query, *ready = later
+            query, *ready, cos, sin = later
         outputs.append(result)
     return (jnp.stack(outputs, axis=0)[None], received[None])
 

time: 140 us -> 140 us (level)
  no operation moved by 1% of the time
where the time goes in v8:
time: 140 us; the launch traced here: 139 us
  blocking collectives  107 us (76%)
  starting transfers between devices  15.4 us (11%)
  Pallas kernels  8.16 us (6%)
  waiting for transfers between devices  4.51 us (3%)
  other arithmetic  2.04 us (1%)
    all_to_all x3, blocking collectives, exchange(): return lax.all_to_all(rows, 'tp', 0, 0)  47.5 us
    all_to_all x2, blocking collectives, stage(): return lax.all_to_all(blocks, ('pipe', 'tp'), 0, 0, axis_index_groups=lines)  38.5 us
    ppermute x2, starting transfers between devices, ring_down(): lax.ppermute(value, axis, [(source, (source - 1) % count) for source in r...  15.4 us
    all_to_all x2, blocking collectives, per_device(): dkv = lax.all_to_all(dkv, 'tp', 0, 0, axis_index_groups=groups)  13.7 us
    pallas_call x9, Pallas kernels, kernel_call(): pl.pallas_call(body, out_shape=outs, in_specs=[kinds[kind] for kind in sp...  8.16 us
    all_to_all x1, blocking collectives, per_device(): kv = lax.all_to_all(kv, 'tp', 0, 0, axis_index_groups=groups)  7.21 us
    ppermute x2, waiting for transfers between devices, ring_down(): lax.ppermute(value, axis, [(source, (source - 1) % count) for source in r...  4.51 us
  transfers between devices with their start and end apart: 2, of which 2 were waited for; matrix products, arithmetic and copies ran while one was open for 0% of the time, Pallas kernels for 1%

profile of v8, /device:TPU:1, one launch (start us, length us, event | category | flops | bytes accessed | tf_op | source)
XLA Modules:
  0.0 138.5 jit_solution(14652235003397039554)
XLA Ops:
  0.6 0.0 copy-start.13
  0.6 0.0 copy-start.12
  0.7 0.0 copy-start.11
  0.7 0.0 copy-start.7
  0.7 1.0 pad_maximum_fusion.rows_ref
  1.7 0.1 shard_map.167
  1.7 13.0 %all_to_all.40.got_ref = bf16[4,384,256]{2,1,0:T(8,128)(2,1)S(1)} all-to-all(bf16[4,384,256]{2,1,0:T(8,128)(2,1)S(1)} %shard_map.167), channel_id=1, replica_groups={{0,1,2,3},{4,5,6,7},{8,9,10,11},{12,13,14,15},{16,20,24,28},{17,21,25,2..., dimensions={0} | all-to-all | bytes 1572864 | tf_op jit(solution)/shard_map/all_to_all | solution.py:414
  14.7 0.0 copy-done.13
  14.7 0.0 copy-done.12
  14.7 0.0 copy-done.11
  14.7 0.0 copy-done.7
  14.8 0.2 shard_map.168
  15.0 0.0 copy-start
  15.0 0.0 copy-start.2
  15.0 0.0 copy-start.3
  15.0 0.0 copy-start.4
  15.0 0.0 copy-start.5
  15.0 0.0 copy-start.6
  15.0 0.0 copy-start.8
  15.1 0.0 copy-start.9
  15.1 0.0 copy-start.10
  15.1 25.5 %all_to_all.41 = bf16[4,4,384,256]{3,2,1,0:T(8,128)(2,1)S(1)} all-to-all(bf16[4,4,384,256]{3,2,1,0:T(8,128)(2,1)S(1)} %get-tuple-element.40), channel_id=1, replica_groups={{0,4,8,12},{1,5,9,13},{2,6,10,14},{3,7,11,15},{16,17,18,19},{20,21,22,2..., dimensions={0} | all-to-all | bytes 6291456 | tf_op jit(solution)/shard_map/all_to_all | solution.py:414
  40.6 0.0 copy-done.2
  40.7 0.0 copy-start.1
  40.7 1.4 %shard_map.169 = (bf16[128,256]{1,0:T(8,128)(2,1)S(1)}, bf16[4,2,64,128]{3,2,1,0:T(8,128)(2,1)S(1)}, f32[2,128,1]{2,1,0:T(8,128)S(1)}, f32[128,128]{1,0:T(8,128)...) custom-call(s32[1]{0:T(128)} %bitcast.place_ref, ...), custom_call_target="tpu_custom_call" | custom-call | tf_op jit(solution)/shard_map/pallas_call | solution.py:53
  42.1 7.2 %all_to_all.42.kv_ref = bf16[4,2,64,128]{3,2,1,0:T(8,128)(2,1)S(1)} all-to-all(bf16[4,2,64,128]{3,2,1,0:T(8,128)(2,1)S(1)} %get-tuple-element.43), channel_id=1, replica_groups={{0,1,2,3},{4,5,6,7},{8,9,10,11},{12,13,14,15},{16,17,18,19},{20,21,22,2..., dimensions={0} | all-to-all | bytes 262144 | tf_op jit(solution)/shard_map/all_to_all | solution.py:457
  49.3 0.0 copy-done.1
  49.3 1.5 %shard_map.170 = (bf16[128,256]{1,0:T(8,128)(2,1)S(1)}, bf16[4,64,128]{2,1,0:T(8,128)(2,1)S(1)}, f32[128,1]{1,0:T(8,128)S(1)}) custom-call(s32[1]{0:T(128)} %bitcast.1.odd_ref, s32[1,2,4]{2,1,0:T(2,128)S(1)} %copy-done.10, bf16[16,384,256]{2,1,0:T(8,128)(2,1)S(1)} %bitcast.29, bf16[256,4096]{1,0:T(8,128)(2,1)S(1)} %bitcast.37, ...), custom_call_target="tpu_custom_call" | custom-call | tf_op jit(solution)/shard_map/pallas_call | solution.py:53
  50.8 6.8 %all_to_all.43.dkv_ref = bf16[4,64,128]{2,1,0:T(8,128)(2,1)S(1)} all-to-all(bf16[4,64,128]{2,1,0:T(8,128)(2,1)S(1)} %get-tuple-element.47), channel_id=1, replica_groups={{0,1,2,3},{4,5,6,7},{8,9,10,11},{12,13,14,15},{16,17,18,19},{20,21,22,2..., dimensions={0} | all-to-all | bytes 131072 | tf_op jit(solution)/shard_map/all_to_all | solution.py:478
  57.7 1.2 shard_map.171
  58.9 0.0 copy-start.14
  58.9 14.6 %all_to_all.44 = bf16[16,128,256]{2,1,0:T(8,128)(2,1)S(1)} all-to-all(bf16[16,128,256]{2,1,0:T(8,128)(2,1)S(1)} %shard_map.171), channel_id=1, replica_groups=mesh['pipe'=32,'tp'=16] {'tp'}, dimensions={0} | all-to-all | bytes 2097152 | tf_op jit(solution)/shard_map/all_to_all | solution.py:398
  73.5 0.1 convert_reduce_fusion.1
  73.7 0.0 copy-done.14
  73.7 9.1 %collective-permute-start = (bf16[128,256]{1,0:T(8,128)(2,1)S(1)}, bf16[128,256]{1,0:T(8,128)(2,1)S(1)}, u32[]{:S(2)}, u32[]{:S(2)}) collective-permute-start(bf16[128,256]{1,0:T(8,128)(2,1)S(1)} %get-tuple-element.68), channel_id=1, source_target_pairs={{0,496},{16,0},{32,16},{48,32},{64,48},{80,64},{96,80},{112,96},{1... | collective-permute-start | bytes 196616 | tf_op jit(solution)/shard_map/ppermute | solution.py:347
  82.8 0.9 shard_map.172
  83.7 0.5 collective-permute-done.grad_ref
  84.1 0.1 shard_map.173
  84.2 17.6 %all_to_all.45.got_ref = bf16[16,128,256]{2,1,0:T(8,128)(2,1)S(1)} all-to-all(bf16[16,128,256]{2,1,0:T(8,128)(2,1)S(1)} %shard_map.173), channel_id=1, replica_groups=mesh['pipe'=32,'tp'=16] {'tp'}, dimensions={0} | all-to-all | bytes 2097152 | tf_op jit(solution)/shard_map/all_to_all | solution.py:398
  101.8 1.6 %shard_map.174 = (bf16[128,256]{1,0:T(8,128)(2,1)S(1)}, bf16[4,64,128]{2,1,0:T(8,128)(2,1)S(1)}, f32[128,1]{1,0:T(8,128)S(1)}) custom-call(s32[1]{0:T(128)} %bitcast.1.odd_ref, s32[1,2,4]{2,1,0:T(2,128)S(1)} %copy-done.10, bf16[16,128,256]{2,1,0:T(8,128)(2,1)S(1)} %all_to_all.45.got_ref, bf16[256,4096]{1,0:T(8,128)(2,1)S(1)} %bitcast.38, ...), custom_call_target="tpu_custom_call" | custom-call | tf_op jit(solution)/shard_map/pallas_call | solution.py:53
  103.4 6.8 %all_to_all.46.dkv_ref = bf16[4,64,128]{2,1,0:T(8,128)(2,1)S(1)} all-to-all(bf16[4,64,128]{2,1,0:T(8,128)(2,1)S(1)} %get-tuple-element.66), channel_id=1, replica_groups={{0,1,2,3},{4,5,6,7},{8,9,10,11},{12,13,14,15},{16,17,18,19},{20,21,22,2..., dimensions={0} | all-to-all | bytes 131072 | tf_op jit(solution)/shard_map/all_to_all | solution.py:478
  110.2 1.2 shard_map.175
  111.5 15.3 %all_to_all.47 = bf16[16,128,256]{2,1,0:T(8,128)(2,1)S(1)} all-to-all(bf16[16,128,256]{2,1,0:T(8,128)(2,1)S(1)} %shard_map.175), channel_id=1, replica_groups=mesh['pipe'=32,'tp'=16] {'tp'}, dimensions={0} | all-to-all | bytes 2097152 | tf_op jit(solution)/shard_map/all_to_all | solution.py:398
  126.7 0.1 convert_reduce_fusion
  126.9 6.3 %collective-permute-start.1 = (bf16[128,256]{1,0:T(8,128)(2,1)S(1)}, bf16[128,256]{1,0:T(8,128)(2,1)S(1)}, u32[]{:S(2)}, u32[]{:S(2)}) collective-permute-start(bf16[128,256]{1,0:T(8,128)(2,1)S(1)} %bitcast_select_fusion), channel_id=1, source_target_pairs={{0,496},{16,0},{32,16},{48,32},{64,48},{80,64},{96,80},{112,96},{1... | collective-permute-start | bytes 196616 | tf_op jit(solution)/shard_map/ppermute | solution.py:347
  133.2 0.7 maximum_bitcast_fusion
  133.9 4.1 %collective-permute-done.1 = bf16[128,256]{1,0:T(8,128)(2,1)S(1)} collective-permute-done((bf16[128,256]{1,0:T(8,128)(2,1)S(1)}, bf16[128,256]{1,0:T(8,128)(2,1)S(1)}, u32[]{:S(2)}, u32[]{:S(2)}) %collective-permute-start.1) | collective-permute-done | bytes 65568 | tf_op jit(solution)/shard_map/ppermute | solution.py:347
  137.9 0.6 copy.19
  (11 shorter events, 0.1 us)
Async XLA Ops:
  0.6 14.1 %copy-start.13 = (s32[2,128]{1,0:T(2,128)S(1)}, s32[2,128]{1,0:T(2,128)}, u32[]{:S(2)}) copy-start(s32[2,128]{1,0:T(2,128)} %sample_ref.1) | copy-start | bytes 3076
  0.6 14.1 %copy-start.12 = (s32[512]{0:T(512)S(1)}, s32[512]{0:T(512)}, u32[]{:S(2)}) copy-start(s32[512]{0:T(512)} %param.26) | copy-start | bytes 6148
  0.7 14.1 %copy-start.11 = (f32[512]{0:T(512)S(1)}, f32[512]{0:T(512)}, u32[]{:S(2)}) copy-start(f32[512]{0:T(512)} %param.25) | copy-start | bytes 6148
  0.7 14.1 %copy-start.7 = (bf16[2,128,256]{2,1,0:T(8,128)(2,1)S(1)}, bf16[2,128,256]{2,1,0:T(8,128)(2,1)}, u32[]{:S(2)}) copy-start(bf16[2,128,256]{2,1,0:T(8,128)(2,1)} %score_ref.1) | copy-start | bytes 393220
  15.0 25.6 %copy-start = (bf16[1,4096,256]{2,1,0:T(8,128)(2,1)S(1)}, bf16[1,4096,256]{2,1,0:T(8,128)(2,1)}, u32[]{:S(2)}) copy-start(bf16[1,4096,256]{2,1,0:T(8,128)(2,1)} %param.19) | copy-start | bytes 6291460
  15.0 25.6 %copy-start.2 = (bf16[3,128,128]{2,1,0:T(8,128)(2,1)S(1)}, bf16[3,128,128]{2,1,0:T(8,128)(2,1)}, u32[]{:S(2)}) copy-start(bf16[3,128,128]{2,1,0:T(8,128)(2,1)} %constant.26.clone.stab_ref) | copy-start | bytes 294916
  15.0 25.6 %copy-start.3 = (bf16[3,128,128]{2,1,0:T(8,128)(2,1)S(1)}, bf16[3,128,128]{2,1,0:T(8,128)(2,1)}, u32[]{:S(2)}) copy-start(bf16[3,128,128]{2,1,0:T(8,128)(2,1)} %constant.25.clone.ctab_ref) | copy-start | bytes 294916
  15.0 25.6 %copy-start.4 = (bf16[1,4096]{1,0:T(2,128)(2,1)S(1)}, bf16[1,4096]{1,0:T(2,128)(2,1)}, u32[]{:S(2)}) copy-start(bf16[1,4096]{1,0:T(2,128)(2,1)} %gain_ref.7) | copy-start | bytes 24580
  15.0 25.6 %copy-start.5 = (bf16[1,4096,32]{1,2,0:T(8,128)(2,1)S(1)}, bf16[1,4096,32]{1,2,0:T(8,128)(2,1)}, u32[]{:S(2)}) copy-start(bf16[1,4096,32]{1,2,0:T(8,128)(2,1)} %param.20) | copy-start | bytes 786436
  15.0 25.6 %copy-start.6 = (bf16[1,4096,32]{1,2,0:T(8,128)(2,1)S(1)}, bf16[1,4096,32]{1,2,0:T(8,128)(2,1)}, u32[]{:S(2)}) copy-start(bf16[1,4096,32]{1,2,0:T(8,128)(2,1)} %param.21) | copy-start | bytes 786436
  15.0 25.6 %copy-start.8 = (bf16[3,128,128]{2,1,0:T(8,128)(2,1)S(1)}, bf16[3,128,128]{2,1,0:T(8,128)(2,1)}, u32[]{:S(2)}) copy-start(bf16[3,128,128]{2,1,0:T(8,128)(2,1)} %constant.28.clone.stabt_ref) | copy-start | bytes 294916
  15.1 25.6 %copy-start.9 = (bf16[3,128,128]{2,1,0:T(8,128)(2,1)S(1)}, bf16[3,128,128]{2,1,0:T(8,128)(2,1)}, u32[]{:S(2)}) copy-start(bf16[3,128,128]{2,1,0:T(8,128)(2,1)} %constant.27.clone.ctabt_ref) | copy-start | bytes 294916
  15.1 25.6 %copy-start.10 = (s32[1,2,4]{2,1,0:T(2,128)S(1)}, s32[1,2,4]{2,1,0:T(2,128)}, u32[]{:S(2)}) copy-start(s32[1,2,4]{2,1,0:T(2,128)} %seg_ref.7) | copy-start | bytes 100
  40.7 8.7 %copy-start.1 = (bf16[1,256,4096]{2,1,0:T(8,128)(2,1)S(1)}, bf16[1,256,4096]{2,1,0:T(8,128)(2,1)}, u32[]{:S(2)}) copy-start(bf16[1,256,4096]{2,1,0:T(8,128)(2,1)} %param.22) | copy-start | bytes 6291460
  58.9 14.7 %copy-start.14 = (bf16[1,128,256]{2,1,0:T(8,128)(2,1)S(1)}, bf16[1,128,256]{2,1,0:T(8,128)(2,1)}, u32[]{:S(2)}) copy-start(bf16[1,128,256]{2,1,0:T(8,128)(2,1)} %param.17) | copy-start | bytes 196612
  73.7 10.4 %collective-permute-start = (bf16[128,256]{1,0:T(8,128)(2,1)S(1)}, bf16[128,256]{1,0:T(8,128)(2,1)S(1)}, u32[]{:S(2)}, u32[]{:S(2)}) collective-permute-start(bf16[128,256]{1,0:T(8,128)(2,1)S(1)} %get-tuple-element.68), channel_id=1, source_target_pairs={{0,496},{16,0},{32,16},{48,32},{64,48},{80,64},{96,80},{112,96},{1... | collective-permute-start | bytes 196616 | tf_op jit(solution)/shard_map/ppermute | solution.py:347
  126.9 11.0 %collective-permute-start.1 = (bf16[128,256]{1,0:T(8,128)(2,1)S(1)}, bf16[128,256]{1,0:T(8,128)(2,1)S(1)}, u32[]{:S(2)}, u32[]{:S(2)}) collective-permute-start(bf16[128,256]{1,0:T(8,128)(2,1)S(1)} %bitcast_select_fusion), channel_id=1, source_target_pairs={{0,496},{16,0},{32,16},{48,32},{64,48},{80,64},{96,80},{112,96},{1... | collective-permute-start | bytes 196616 | tf_op jit(solution)/shard_map/ppermute | solution.py:347

commit v9 on v8

--- a/solution.py
+++ b/solution.py
@@ -398,7 +398,7 @@
         return lax.all_to_all(rows, "tp", 0, 0)
 
     first_flag = first_section.astype(jnp.int32)[None]
-    odd = (lax.axis_index("pipe") & 1).astype(jnp.int32)[None]
+    odd = (1 - (lax.axis_index("pipe") & 1)).astype(jnp.int32)[None]
     saved, place, odd, first_flag, first_section = lax.optimization_barrier(
         (saved, place, odd, first_flag, first_section)
     )
@@ -407,7 +407,7 @@
         for section in range(lax.axis_size("pipe")):
             for line in range(share):
                 chosen = [
-                    line * share + i if (section + along) % 2 == 0 else i * share + line
+                    line * share + i if (section + along) % 2 == 1 else i * share + line
                     for i in range(share)
                 ]
                 lines.append([section * tp_count + member for member in chosen])

time: 140 us -> 140 us (level)
  no operation moved by 1% of the time
where the time goes in v9:
time: 140 us; the launch traced here: 139 us
  blocking collectives  108 us (77%)
  starting transfers between devices  14.5 us (10%)
  Pallas kernels  8.16 us (6%)
  waiting for transfers between devices  4.33 us (3%)
  other arithmetic  2.03 us (1%)
    all_to_all x3, blocking collectives, exchange(): return lax.all_to_all(rows, 'tp', 0, 0)  48.5 us
    all_to_all x2, blocking collectives, stage(): return lax.all_to_all(blocks, ('pipe', 'tp'), 0, 0, axis_index_groups=lines)  38.5 us
    ppermute x2, starting transfers between devices, ring_down(): lax.ppermute(value, axis, [(source, (source - 1) % count) for source in r...  14.5 us
    all_to_all x2, blocking collectives, per_device(): dkv = lax.all_to_all(dkv, 'tp', 0, 0, axis_index_groups=groups)  13.7 us
    pallas_call x9, Pallas kernels, kernel_call(): pl.pallas_call(body, out_shape=outs, in_specs=[kinds[kind] for kind in sp...  8.16 us
    all_to_all x1, blocking collectives, per_device(): kv = lax.all_to_all(kv, 'tp', 0, 0, axis_index_groups=groups)  7.21 us
    ppermute x2, waiting for transfers between devices, ring_down(): lax.ppermute(value, axis, [(source, (source - 1) % count) for source in r...  4.33 us
  transfers between devices with their start and end apart: 2, of which 2 were waited for; matrix products, arithmetic and copies ran while one was open for 0% of the time, Pallas kernels for 1%

profile of v9, /device:TPU:1, one launch (start us, length us, event | category | flops | bytes accessed | tf_op | source)
XLA Modules:
  0.0 138.5 jit_solution(9883038181247064719)
XLA Ops:
  0.6 0.0 copy-start.13
  0.6 0.0 copy-start.12
  0.7 0.0 copy-start.11
  0.7 0.0 copy-start.7
  0.7 1.0 pad_maximum_fusion.rows_ref
  1.7 0.1 shard_map.167
  1.7 13.2 %all_to_all.40.got_ref = bf16[4,384,256]{2,1,0:T(8,128)(2,1)S(1)} all-to-all(bf16[4,384,256]{2,1,0:T(8,128)(2,1)S(1)} %shard_map.167), channel_id=1, replica_groups={{0,4,8,12},{1,5,9,13},{2,6,10,14},{3,7,11,15},{16,17,18,19},{20,21,22,2..., dimensions={0} | all-to-all | bytes 1572864 | tf_op jit(solution)/shard_map/all_to_all | solution.py:414
  14.9 0.0 copy-done.13
  14.9 0.0 copy-done.12
  14.9 0.0 copy-done.11
  14.9 0.0 copy-done.7
  14.9 0.2 shard_map.168
  15.1 0.0 copy-start
  15.2 0.0 copy-start.2
  15.2 0.0 copy-start.3
  15.2 0.0 copy-start.4
  15.2 0.0 copy-start.5
  15.2 0.0 copy-start.6
  15.2 0.0 copy-start.8
  15.2 0.0 copy-start.9
  15.2 0.0 copy-start.10
  15.3 25.3 %all_to_all.41 = bf16[4,4,384,256]{3,2,1,0:T(8,128)(2,1)S(1)} all-to-all(bf16[4,4,384,256]{3,2,1,0:T(8,128)(2,1)S(1)} %get-tuple-element.40), channel_id=1, replica_groups={{0,1,2,3},{4,5,6,7},{8,9,10,11},{12,13,14,15},{16,20,24,28},{17,21,25,2..., dimensions={0} | all-to-all | bytes 6291456 | tf_op jit(solution)/shard_map/all_to_all | solution.py:414
  40.6 0.0 copy-done
  40.6 0.0 copy-done.2
  40.7 0.0 copy-start.1
  40.7 1.4 %shard_map.169 = (bf16[128,256]{1,0:T(8,128)(2,1)S(1)}, bf16[4,2,64,128]{3,2,1,0:T(8,128)(2,1)S(1)}, f32[2,128,1]{2,1,0:T(8,128)S(1)}, f32[128,128]{1,0:T(8,128)...) custom-call(s32[1]{0:T(128)} %bitcast.place_ref, ...), custom_call_target="tpu_custom_call" | custom-call | tf_op jit(solution)/shard_map/pallas_call | solution.py:53
  42.1 7.2 %all_to_all.42.kv_ref = bf16[4,2,64,128]{3,2,1,0:T(8,128)(2,1)S(1)} all-to-all(bf16[4,2,64,128]{3,2,1,0:T(8,128)(2,1)S(1)} %get-tuple-element.43), channel_id=1, replica_groups={{0,1,2,3},{4,5,6,7},{8,9,10,11},{12,13,14,15},{16,17,18,19},{20,21,22,2..., dimensions={0} | all-to-all | bytes 262144 | tf_op jit(solution)/shard_map/all_to_all | solution.py:457
  49.3 0.0 copy-done.1
  49.3 1.5 %shard_map.170 = (bf16[128,256]{1,0:T(8,128)(2,1)S(1)}, bf16[4,64,128]{2,1,0:T(8,128)(2,1)S(1)}, f32[128,1]{1,0:T(8,128)S(1)}) custom-call(s32[1]{0:T(128)} %bitcast.1.odd_ref, s32[1,2,4]{2,1,0:T(2,128)S(1)} %copy-done.10, bf16[16,384,256]{2,1,0:T(8,128)(2,1)S(1)} %bitcast.29, bf16[256,4096]{1,0:T(8,128)(2,1)S(1)} %bitcast.37, ...), custom_call_target="tpu_custom_call" | custom-call | tf_op jit(solution)/shard_map/pallas_call | solution.py:53
  50.8 6.8 %all_to_all.43.dkv_ref = bf16[4,64,128]{2,1,0:T(8,128)(2,1)S(1)} all-to-all(bf16[4,64,128]{2,1,0:T(8,128)(2,1)S(1)} %get-tuple-element.47), channel_id=1, replica_groups={{0,1,2,3},{4,5,6,7},{8,9,10,11},{12,13,14,15},{16,17,18,19},{20,21,22,2..., dimensions={0} | all-to-all | bytes 131072 | tf_op jit(solution)/shard_map/all_to_all | solution.py:478
  57.7 1.2 shard_map.171
  58.9 0.0 copy-start.14
  58.9 14.5 %all_to_all.44 = bf16[16,128,256]{2,1,0:T(8,128)(2,1)S(1)} all-to-all(bf16[16,128,256]{2,1,0:T(8,128)(2,1)S(1)} %shard_map.171), channel_id=1, replica_groups=mesh['pipe'=32,'tp'=16] {'tp'}, dimensions={0} | all-to-all | bytes 2097152 | tf_op jit(solution)/shard_map/all_to_all | solution.py:398
  73.5 0.1 convert_reduce_fusion.1
  73.7 9.1 %collective-permute-start = (bf16[128,256]{1,0:T(8,128)(2,1)S(1)}, bf16[128,256]{1,0:T(8,128)(2,1)S(1)}, u32[]{:S(2)}, u32[]{:S(2)}) collective-permute-start(bf16[128,256]{1,0:T(8,128)(2,1)S(1)} %get-tuple-element.68), channel_id=1, source_target_pairs={{0,496},{16,0},{32,16},{48,32},{64,48},{80,64},{96,80},{112,96},{1... | collective-permute-start | bytes 196616 | tf_op jit(solution)/shard_map/ppermute | solution.py:347
  82.8 0.9 shard_map.172
  83.7 0.5 collective-permute-done.grad_ref
  84.1 0.1 shard_map.173
  84.2 17.6 %all_to_all.45.got_ref = bf16[16,128,256]{2,1,0:T(8,128)(2,1)S(1)} all-to-all(bf16[16,128,256]{2,1,0:T(8,128)(2,1)S(1)} %shard_map.173), channel_id=1, replica_groups=mesh['pipe'=32,'tp'=16] {'tp'}, dimensions={0} | all-to-all | bytes 2097152 | tf_op jit(solution)/shard_map/all_to_all | solution.py:398
  101.8 1.6 %shard_map.174 = (bf16[128,256]{1,0:T(8,128)(2,1)S(1)}, bf16[4,64,128]{2,1,0:T(8,128)(2,1)S(1)}, f32[128,1]{1,0:T(8,128)S(1)}) custom-call(s32[1]{0:T(128)} %bitcast.1.odd_ref, s32[1,2,4]{2,1,0:T(2,128)S(1)} %copy-done.10, bf16[16,128,256]{2,1,0:T(8,128)(2,1)S(1)} %all_to_all.45.got_ref, bf16[256,4096]{1,0:T(8,128)(2,1)S(1)} %bitcast.38, ...), custom_call_target="tpu_custom_call" | custom-call | tf_op jit(solution)/shard_map/pallas_call | solution.py:53
  103.3 6.8 %all_to_all.46.dkv_ref = bf16[4,64,128]{2,1,0:T(8,128)(2,1)S(1)} all-to-all(bf16[4,64,128]{2,1,0:T(8,128)(2,1)S(1)} %get-tuple-element.66), channel_id=1, replica_groups={{0,1,2,3},{4,5,6,7},{8,9,10,11},{12,13,14,15},{16,17,18,19},{20,21,22,2..., dimensions={0} | all-to-all | bytes 131072 | tf_op jit(solution)/shard_map/all_to_all | solution.py:478
  110.2 1.2 shard_map.175
  111.4 16.4 %all_to_all.47 = bf16[16,128,256]{2,1,0:T(8,128)(2,1)S(1)} all-to-all(bf16[16,128,256]{2,1,0:T(8,128)(2,1)S(1)} %shard_map.175), channel_id=1, replica_groups=mesh['pipe'=32,'tp'=16] {'tp'}, dimensions={0} | all-to-all | bytes 2097152 | tf_op jit(solution)/shard_map/all_to_all | solution.py:398
  127.8 0.1 convert_reduce_fusion
  128.0 5.4 %collective-permute-start.1 = (bf16[128,256]{1,0:T(8,128)(2,1)S(1)}, bf16[128,256]{1,0:T(8,128)(2,1)S(1)}, u32[]{:S(2)}, u32[]{:S(2)}) collective-permute-start(bf16[128,256]{1,0:T(8,128)(2,1)S(1)} %bitcast_select_fusion), channel_id=1, source_target_pairs={{0,496},{16,0},{32,16},{48,32},{64,48},{80,64},{96,80},{112,96},{1... | collective-permute-start | bytes 196616 | tf_op jit(solution)/shard_map/ppermute | solution.py:347
  133.4 0.7 maximum_bitcast_fusion
  134.0 3.9 %collective-permute-done.1 = bf16[128,256]{1,0:T(8,128)(2,1)S(1)} collective-permute-done((bf16[128,256]{1,0:T(8,128)(2,1)S(1)}, bf16[128,256]{1,0:T(8,128)(2,1)S(1)}, u32[]{:S(2)}, u32[]{:S(2)}) %collective-permute-start.1) | collective-permute-done | bytes 65568 | tf_op jit(solution)/shard_map/ppermute | solution.py:347
  137.9 0.6 copy.19
  (11 shorter events, 0.1 us)
Async XLA Ops:
  0.6 14.3 %copy-start.13 = (s32[2,128]{1,0:T(2,128)S(1)}, s32[2,128]{1,0:T(2,128)}, u32[]{:S(2)}) copy-start(s32[2,128]{1,0:T(2,128)} %sample_ref.1) | copy-start | bytes 3076
  0.6 14.3 %copy-start.12 = (s32[512]{0:T(512)S(1)}, s32[512]{0:T(512)}, u32[]{:S(2)}) copy-start(s32[512]{0:T(512)} %param.26) | copy-start | bytes 6148
  0.7 14.3 %copy-start.11 = (f32[512]{0:T(512)S(1)}, f32[512]{0:T(512)}, u32[]{:S(2)}) copy-start(f32[512]{0:T(512)} %param.25) | copy-start | bytes 6148
  0.7 14.3 %copy-start.7 = (bf16[2,128,256]{2,1,0:T(8,128)(2,1)S(1)}, bf16[2,128,256]{2,1,0:T(8,128)(2,1)}, u32[]{:S(2)}) copy-start(bf16[2,128,256]{2,1,0:T(8,128)(2,1)} %score_ref.1) | copy-start | bytes 393220
  15.1 25.5 %copy-start = (bf16[1,4096,256]{2,1,0:T(8,128)(2,1)S(1)}, bf16[1,4096,256]{2,1,0:T(8,128)(2,1)}, u32[]{:S(2)}) copy-start(bf16[1,4096,256]{2,1,0:T(8,128)(2,1)} %param.19) | copy-start | bytes 6291460
  15.2 25.5 %copy-start.2 = (bf16[3,128,128]{2,1,0:T(8,128)(2,1)S(1)}, bf16[3,128,128]{2,1,0:T(8,128)(2,1)}, u32[]{:S(2)}) copy-start(bf16[3,128,128]{2,1,0:T(8,128)(2,1)} %constant.26.clone.stab_ref) | copy-start | bytes 294916
  15.2 25.4 %copy-start.3 = (bf16[3,128,128]{2,1,0:T(8,128)(2,1)S(1)}, bf16[3,128,128]{2,1,0:T(8,128)(2,1)}, u32[]{:S(2)}) copy-start(bf16[3,128,128]{2,1,0:T(8,128)(2,1)} %constant.25.clone.ctab_ref) | copy-start | bytes 294916
  15.2 25.4 %copy-start.4 = (bf16[1,4096]{1,0:T(2,128)(2,1)S(1)}, bf16[1,4096]{1,0:T(2,128)(2,1)}, u32[]{:S(2)}) copy-start(bf16[1,4096]{1,0:T(2,128)(2,1)} %gain_ref.7) | copy-start | bytes 24580
  15.2 25.4 %copy-start.5 = (bf16[1,4096,32]{1,2,0:T(8,128)(2,1)S(1)}, bf16[1,4096,32]{1,2,0:T(8,128)(2,1)}, u32[]{:S(2)}) copy-start(bf16[1,4096,32]{1,2,0:T(8,128)(2,1)} %param.20) | copy-start | bytes 786436
  15.2 25.4 %copy-start.6 = (bf16[1,4096,32]{1,2,0:T(8,128)(2,1)S(1)}, bf16[1,4096,32]{1,2,0:T(8,128)(2,1)}, u32[]{:S(2)}) copy-start(bf16[1,4096,32]{1,2,0:T(8,128)(2,1)} %param.21) | copy-start | bytes 786436
  15.2 25.4 %copy-start.8 = (bf16[3,128,128]{2,1,0:T(8,128)(2,1)S(1)}, bf16[3,128,128]{2,1,0:T(8,128)(2,1)}, u32[]{:S(2)}) copy-start(bf16[3,128,128]{2,1,0:T(8,128)(2,1)} %constant.28.clone.stabt_ref) | copy-start | bytes 294916
  15.2 25.4 %copy-start.9 = (bf16[3,128,128]{2,1,0:T(8,128)(2,1)S(1)}, bf16[3,128,128]{2,1,0:T(8,128)(2,1)}, u32[]{:S(2)}) copy-start(bf16[3,128,128]{2,1,0:T(8,128)(2,1)} %constant.27.clone.ctabt_ref) | copy-start | bytes 294916
  15.2 25.4 %copy-start.10 = (s32[1,2,4]{2,1,0:T(2,128)S(1)}, s32[1,2,4]{2,1,0:T(2,128)}, u32[]{:S(2)}) copy-start(s32[1,2,4]{2,1,0:T(2,128)} %seg_ref.7) | copy-start | bytes 100
  40.7 8.7 %copy-start.1 = (bf16[1,256,4096]{2,1,0:T(8,128)(2,1)S(1)}, bf16[1,256,4096]{2,1,0:T(8,128)(2,1)}, u32[]{:S(2)}) copy-start(bf16[1,256,4096]{2,1,0:T(8,128)(2,1)} %param.22) | copy-start | bytes 6291460
  58.9 14.7 %copy-start.14 = (bf16[1,128,256]{2,1,0:T(8,128)(2,1)S(1)}, bf16[1,128,256]{2,1,0:T(8,128)(2,1)}, u32[]{:S(2)}) copy-start(bf16[1,128,256]{2,1,0:T(8,128)(2,1)} %param.17) | copy-start | bytes 196612
  73.7 10.5 %collective-permute-start = (bf16[128,256]{1,0:T(8,128)(2,1)S(1)}, bf16[128,256]{1,0:T(8,128)(2,1)S(1)}, u32[]{:S(2)}, u32[]{:S(2)}) collective-permute-start(bf16[128,256]{1,0:T(8,128)(2,1)S(1)} %get-tuple-element.68), channel_id=1, source_target_pairs={{0,496},{16,0},{32,16},{48,32},{64,48},{80,64},{96,80},{112,96},{1... | collective-permute-start | bytes 196616 | tf_op jit(solution)/shard_map/ppermute | solution.py:347
  128.0 9.9 %collective-permute-start.1 = (bf16[128,256]{1,0:T(8,128)(2,1)S(1)}, bf16[128,256]{1,0:T(8,128)(2,1)S(1)}, u32[]{:S(2)}, u32[]{:S(2)}) collective-permute-start(bf16[128,256]{1,0:T(8,128)(2,1)S(1)} %bitcast_select_fusion), channel_id=1, source_target_pairs={{0,496},{16,0},{32,16},{48,32},{64,48},{80,64},{96,80},{112,96},{1... | collective-permute-start | bytes 196616 | tf_op jit(solution)/shard_map/ppermute | solution.py:347
